TPU v7x, 768 devices: a whole 4x8x12 slice. The times are simulated.
768 devices in a mesh: row: 32 (over x, z_lo, core), col: 24 (over z_hi, y).
Axes of the slice: x: 4, y: 8, z: 12 (z_hi: 3, z_lo: 4; z = z_hi * 4 + z_lo), core: 2. Of those that a mesh axis runs over, the one named last changes fastest.
Arguments:
- x_blocks: float32 [1536, 4, 128, 128], P(('row', 'col')), may hold values from -2.5 to 2.5
- x_cols: int32 [1536, 4], replicated, may hold values from 0 to 1535, as said below
- mask_cols: int32 [1536, 6], replicated, may hold values from 0 to 1535, as said below
- mask_count: int32 [1536], replicated, may hold values from 4 to 6
Outputs:
- square: float32 [1536, 6, 128, 128], P(('row', 'col'))
- x_cubed: float32 [1536, 6, 128, 128], P(('row', 'col'))
Inputs may be any that keep to these rules, and one draw needn't show every extreme that they name: `x_cols`: slot 0 of block row i is i itself; slots 1, 2 and 3 are the cell positions one step away from i, periodically, along the first, second and third dimension of the cell respectively, each in a direction of its own. `mask_cols`: the 6 product columns of block row i are distinct cell positions at offsets from i among (0,0,0), (1,0,0), (-1,0,0), (2,0,0), (0,1,0), (0,-1,0), (0,2,0), (0,0,1), periodically, in any order; slots past mask_count also hold such columns.
All inputs are finite; a program needn't handle non-finite values.
Results may differ from a plain program's by a relative error of at most 0.0003.
Values sent between devices are 32-bit elements; how exact they have to be, the bound alone decides.
No kernel may reach another device: no remote copies, remote signals or barrier semaphores. Data moves between devices by JAX's collectives and lax.ppermute only.
A program may use at most 32 MiB of HBM per device.

v0:
```python
import jax
import jax.numpy as jnp
from jax import lax
from jax.sharding import PartitionSpec as P


def with_halo(cells, sides, width):
    for axis, dim in sides:
        count = lax.axis_size(axis)
        head = lax.slice_in_dim(cells, 0, width, axis=dim)
        tail = lax.slice_in_dim(cells, cells.shape[dim] - width, cells.shape[dim], axis=dim)
        cells = jnp.concatenate(
            [
                lax.ppermute(tail, axis, [(i, (i + 1) % count) for i in range(count)]),
                cells,
                lax.ppermute(head, axis, [((i + 1) % count, i) for i in range(count)]),
            ],
            axis=dim,
        )
    return cells


def passed_along(value, axis, steps):
    count = lax.axis_size(axis)
    pairs = [(source, (source + steps) % count) for source in range(count)]
    return lax.ppermute(value, axis, pairs)


def pick_product(a_vals, pool_row, block_pool, b_cols, out_cols, live_mask):
    pool_rows = b_cols.shape[0]
    pool_slots = b_cols.shape[1]
    row_columns = jnp.take(b_cols, pool_row, axis=0)
    matches = row_columns[:, None, :, :] == out_cols[:, :, None, None]
    present = jnp.any(matches, axis=-1)
    slot_index = jnp.sum(jnp.where(matches, jnp.arange(pool_slots, dtype=jnp.int32), 0), axis=-1)
    flat_index = jnp.where(
        present, pool_row[:, None, :] * pool_slots + slot_index, pool_rows * pool_slots
    )
    picked = jnp.take(block_pool, flat_index, axis=0)
    products = jnp.einsum(
        "rsij,rmsjk->rmik",
        a_vals,
        picked,
        precision=lax.Precision.HIGHEST,
        preferred_element_type=jnp.float32,
    )
    return products * live_mask[:, :, None, None].astype(jnp.float32)


def add_empty(values):
    block_size = values.shape[-1]
    flat_blocks = values.reshape(values.shape[0] * values.shape[1], block_size, block_size)
    return jnp.concatenate(
        [flat_blocks, jnp.zeros((1, block_size, block_size), values.dtype)], axis=0
    )


def per_device(x_blocks, x_cols, mask_cols, mask_count):
    rows_dev = x_blocks.shape[0]
    mask_slots = mask_cols.shape[1]
    row_count = lax.axis_size("row")
    col_count = lax.axis_size("col")
    row_pos = lax.axis_index("row")
    col_pos = lax.axis_index("col")
    local_rows = jnp.arange(rows_dev, dtype=jnp.int32)

    def rows_at(row_dev, col_dev):
        return (row_dev * col_count + col_dev) * rows_dev + local_rows

    own_ids = rows_at(row_pos, col_pos)
    left_ids = rows_at(row_pos, jnp.mod(col_pos - 1, col_count))[rows_dev - 1 :]
    right_ids = rows_at(row_pos, jnp.mod(col_pos + 1, col_count))[:1]
    layer_rows = [jnp.mod(row_pos - shift_by, row_count) for shift_by in (4, -4)]
    group_base = row_pos - jnp.mod(row_pos, 4)
    group_place = jnp.mod(row_pos, 4)
    group_rows = [
        group_base + jnp.mod(group_place - 1, 4),
        group_base + jnp.mod(group_place + 1, 4),
    ]
    pool_ids = jnp.concatenate(
        [left_ids, own_ids, right_ids]
        + [rows_at(one_row, col_pos) for one_row in layer_rows + group_rows],
        axis=0,
    )

    def neighbours(values):
        pieces = [with_halo(values, (("col", 0),), 1)]
        for shift_by in (4, -4):
            pieces.append(passed_along(values, "row", shift_by))
        moved = {}
        for shift_by in (1, -3, -1, 3):
            moved[shift_by] = passed_along(values, "row", shift_by)
        pieces.append(jnp.where(group_place == 0, moved[-3], moved[1]))
        pieces.append(jnp.where(group_place == 3, moved[3], moved[-1]))
        return jnp.concatenate(pieces, axis=0)

    own_xcol = jnp.take(x_cols, own_ids, axis=0)
    own_mcol = jnp.take(mask_cols, own_ids, axis=0)
    own_live = (
        jnp.arange(mask_slots, dtype=jnp.int32)[None, :] < jnp.take(mask_count, own_ids)[:, None]
    )
    pool_order = jnp.arange(pool_ids.shape[0], dtype=jnp.int32)
    found = own_xcol[:, :, None] == pool_ids[None, None, :]
    pool_row = jnp.max(jnp.where(found, pool_order, -1), axis=-1)
    pool_xcol = jnp.take(x_cols, pool_ids, axis=0)
    pool_mcol = jnp.take(mask_cols, pool_ids, axis=0)
    square = pick_product(
        x_blocks, pool_row, add_empty(neighbours(x_blocks)), pool_xcol, own_mcol, own_live
    )
    x_cubed = pick_product(
        x_blocks, pool_row, add_empty(neighbours(square)), pool_mcol, own_mcol, own_live
    )
    return (square, x_cubed)


def solution(mesh):
    in_specs = (P(("row", "col"), None, None, None), P(), P(), P())
    out_specs = (P(("row", "col"), None, None, None), P(("row", "col"), None, None, None))
    return jax.shard_map(
        per_device, mesh=mesh, in_specs=in_specs, out_specs=out_specs, check_vma=False
    )
```

profile of v0, /device:TPU:1, one launch (start us, length us, event | category | flops | bytes accessed | tf_op | source)
XLA Modules:
  0.0 336.4 jit_solution(8595999583687494911)
XLA Ops:
  0.7 6.8 %collective-permute-start.2 = (f32[2,4,128,128]{3,2,1,0:T(8,128)}, f32[2,4,128,128]{3,2,1,0:T(8,128)}, u32[]{:S(2)}, u32[]{:S(2)}) collective-permute-start(f32[2,4,128,128]{3,2,1,0:T(8,128)} %param.4), channel_id=1, source_target_pairs={{0,96},{24,120},{48,144},{72,168},{96,192},{120,216},{144,240},{16... | collective-permute-start | bytes 1572872 | tf_op jit(solution)/shard_map/ppermute | solution.py:26
  7.4 4.1 %collective-permute-start.3 = (f32[2,4,128,128]{3,2,1,0:T(8,128)}, f32[2,4,128,128]{3,2,1,0:T(8,128)S(1)}, u32[]{:S(2)}, u32[]{:S(2)}) collective-permute-start(f32[2,4,128,128]{3,2,1,0:T(8,128)} %param.4), channel_id=1, source_target_pairs={{0,672},{24,696},{48,720},{72,744},{96,0},{120,24},{144,48},{168,7... | collective-permute-start | bytes 1572872 | tf_op jit(solution)/shard_map/ppermute | solution.py:26
  11.6 7.2 %collective-permute-start.4 = (f32[2,4,128,128]{3,2,1,0:T(8,128)}, f32[2,4,128,128]{3,2,1,0:T(8,128)S(1)}, u32[]{:S(2)}, u32[]{:S(2)}) collective-permute-start(f32[2,4,128,128]{3,2,1,0:T(8,128)} %param.4), channel_id=1, source_target_pairs={{0,696},{24,720},{48,744},{72,0},{96,24},{120,48},{144,72},{168,96... | collective-permute-start | bytes 1572872 | tf_op jit(solution)/shard_map/ppermute | solution.py:26
  18.8 1.9 fusion.42
  20.6 3.2 collective-permute-start
  23.8 13.2 %collective-permute-start.1 = (f32[1,4,128,128]{3,2,1,0:T(8,128)}, f32[1,4,128,128]{3,2,1,0:T(8,128)S(1)}, u32[]{:S(2)}, u32[]{:S(2)}) collective-permute-start(f32[1,4,128,128]{3,2,1,0:T(8,128)} %get-tuple-element.10), channel_id=1, source_target_pairs={{1,0},{2,1},{3,2},{4,3},{5,4},{6,5},{7,6},{8,7},{9,8},{10,9},{11,1... | collective-permute-start | bytes 786440 | tf_op jit(solution)/shard_map/ppermute | solution.py:16
  47.6 24.3 %collective-permute-done = f32[1,4,128,128]{3,2,1,0:T(8,128)} collective-permute-done((f32[1,4,128,128]{3,2,1,0:T(8,128)}, f32[1,4,128,128]{3,2,1,0:T(8,128)}, u32[]{:S(2)}, u32[]{:S(2)}) %collective-permute-start) | collective-permute-done | bytes 262176 | tf_op jit(solution)/shard_map/ppermute | solution.py:14
  71.9 41.3 %collective-permute-start.5 = (f32[2,4,128,128]{3,2,1,0:T(8,128)S(1)}, f32[2,4,128,128]{3,2,1,0:T(8,128)S(1)}, u32[]{:S(2)}, u32[]{:S(2)}) collective-permute-start(f32[2,4,128,128]{3,2,1,0:T(8,128)S(1)} %copy-done.2), channel_id=1, source_target_pairs={{0,24},{24,48},{48,72},{72,96},{96,120},{120,144},{144,168},{168,1... | collective-permute-start | bytes 1572872 | tf_op jit(solution)/shard_map/ppermute | solution.py:26
  114.3 1.9 collective-permute-start.6
  116.2 1.9 collective-permute-start.7
  119.4 13.3 %collective-permute-done.6 = f32[2,4,128,128]{3,2,1,0:T(8,128)S(1)} collective-permute-done((f32[2,4,128,128]{3,2,1,0:T(8,128)S(1)}, f32[2,4,128,128]{3,2,1,0:T(8,128)S(1)}, u32[]{:S(2)}, u32[]{:S(2)}) %collective-permute-start.6) | collective-permute-done | bytes 524320 | tf_op jit(solution)/shard_map/ppermute | solution.py:26
  133.1 2.4 gather_fusion.4
  135.5 2.4 copy.39
  137.9 3.9 %fusion.23 = f32[2,6,128,128]{2,3,1,0:T(8,128)S(1)} fusion(f32[2,6,4,128,128]{3,4,2,1,0:T(8,128)S(1)} %bitcast.73, pred[2,6,4]{2,1,0:T(8,128)(4,1)S(1)} %copy.37, f32[2,4,128,128]{3,2,1,0:T(8,128)} %param.4, f32[2,6]{1,0:T(2,128)S(1)} %compare_convert_fusion), kind=kOutput, calls=%fused_computation.22 | convolution fusion | flops 1208942592 | bytes 4456544 | tf_op jit(solution)/shard_map/rsij,rmsjk->rmik/dot_general | solution.py:40
  143.6 1.9 collective-permute-start.8
  146.0 6.5 %collective-permute-start.10 = (f32[2,6,128,128]{2,3,1,0:T(8,128)}, f32[2,6,128,128]{2,3,1,0:T(8,128)S(1)}, u32[]{:S(2)}, u32[]{:S(2)}) collective-permute-start(f32[2,6,128,128]{2,3,1,0:T(8,128)} %copy-done.1), channel_id=1, source_target_pairs={{0,96},{24,120},{48,144},{72,168},{96,192},{120,216},{144,240},{16... | collective-permute-start | bytes 2359304 | tf_op jit(solution)/shard_map/ppermute | solution.py:26
  153.6 1.3 compare_select_fusion.2
  155.0 3.1 collective-permute-start.11
  158.1 4.4 %collective-permute-start.12 = (f32[2,6,128,128]{2,3,1,0:T(8,128)}, f32[2,6,128,128]{2,3,1,0:T(8,128)S(1)}, u32[]{:S(2)}, u32[]{:S(2)}) collective-permute-start(f32[2,6,128,128]{2,3,1,0:T(8,128)} %copy-done.1), channel_id=1, source_target_pairs={{0,696},{24,720},{48,744},{72,0},{96,24},{120,48},{144,72},{168,96... | collective-permute-start | bytes 2359304 | tf_op jit(solution)/shard_map/ppermute | solution.py:26
  162.5 1.9 collective-permute-start.13
  164.4 15.5 %collective-permute-done.8 = f32[1,6,128,128]{2,3,1,0:T(8,128)S(1)} collective-permute-done((f32[1,6,128,128]{2,3,1,0:T(8,128)}, f32[1,6,128,128]{2,3,1,0:T(8,128)S(1)}, u32[]{:S(2)}, u32[]{:S(2)}) %collective-permute-start.8) | collective-permute-done | bytes 393248 | tf_op jit(solution)/shard_map/ppermute | solution.py:14
  179.9 1.9 collective-permute-start.9
  183.1 1.4 copy.43
  186.5 2.3 copy.47
  189.6 114.4 %collective-permute-start.14 = (f32[2,6,128,128]{2,3,1,0:T(8,128)}, f32[2,6,128,128]{2,3,1,0:T(8,128)S(1)}, u32[]{:S(2)}, u32[]{:S(2)}) collective-permute-start(f32[2,6,128,128]{2,3,1,0:T(8,128)} %copy-done.1), channel_id=1, source_target_pairs={{0,72},{24,96},{48,120},{72,144},{96,168},{120,192},{144,216},{168... | collective-permute-start | bytes 2359304 | tf_op jit(solution)/shard_map/ppermute | solution.py:26
  304.0 1.9 collective-permute-start.15
  308.4 4.9 %collective-permute-done.14 = f32[2,6,128,128]{2,3,1,0:T(8,128)S(1)} collective-permute-done((f32[2,6,128,128]{2,3,1,0:T(8,128)}, f32[2,6,128,128]{2,3,1,0:T(8,128)S(1)}, u32[]{:S(2)}, u32[]{:S(2)}) %collective-permute-start.14) | collective-permute-done | bytes 786464 | tf_op jit(solution)/shard_map/ppermute | solution.py:26
  313.3 10.0 %collective-permute-done.15 = f32[2,6,128,128]{2,3,1,0:T(8,128)S(1)} collective-permute-done((f32[2,6,128,128]{2,3,1,0:T(8,128)}, f32[2,6,128,128]{2,3,1,0:T(8,128)S(1)}, u32[]{:S(2)}, u32[]{:S(2)}) %collective-permute-start.15) | collective-permute-done | bytes 786464 | tf_op jit(solution)/shard_map/ppermute | solution.py:26
  323.4 2.7 concatenate.64
  326.1 3.1 gather_fusion.8
  329.3 4.8 %fusion.17 = f32[2,6,128,128]{2,3,1,0:T(8,128)} fusion(f32[2,6,4,128,128]{3,4,2,1,0:T(8,128)S(1)} %bitcast.72, pred[2,6,4]{2,1,0:T(8,128)(4,1)S(1)} %copy-done.4, f32[2,4,128,128]{3,2,1,0:T(8,128)} %param.4, f32[2,6]{1,0:T(2,128)S(1)} %copy-done.6), kind=kOutput, calls=%fused_computation.20 | convolution fusion | flops 1208942592 | bytes 4456544 | tf_op jit(solution)/shard_map/rsij,rmsjk->rmik/dot_general | solution.py:40
  334.1 2.3 copy.48
  (98 shorter events, 22.9 us)
Async XLA Ops:
  0.6 37.2 %copy-start = (s32[1536]{0:T(1024)S(1)}, s32[1536]{0:T(1024)}, u32[]{:S(2)}) copy-start(s32[1536]{0:T(1024)} %param.7) | copy-start | bytes 18436
  0.6 71.3 %copy-start.2 = (f32[2,4,128,128]{3,2,1,0:T(8,128)S(1)}, f32[2,4,128,128]{3,2,1,0:T(8,128)}, u32[]{:S(2)}) copy-start(f32[2,4,128,128]{3,2,1,0:T(8,128)} %param.4) | copy-start | bytes 1572868
  0.7 115.5 %collective-permute-start.2 = (f32[2,4,128,128]{3,2,1,0:T(8,128)}, f32[2,4,128,128]{3,2,1,0:T(8,128)}, u32[]{:S(2)}, u32[]{:S(2)}) collective-permute-start(f32[2,4,128,128]{3,2,1,0:T(8,128)} %param.4), channel_id=1, source_target_pairs={{0,96},{24,120},{48,144},{72,168},{96,192},{120,216},{144,240},{16... | collective-permute-start | bytes 1572872 | tf_op jit(solution)/shard_map/ppermute | solution.py:26
  7.4 111.8 %collective-permute-start.3 = (f32[2,4,128,128]{3,2,1,0:T(8,128)}, f32[2,4,128,128]{3,2,1,0:T(8,128)S(1)}, u32[]{:S(2)}, u32[]{:S(2)}) collective-permute-start(f32[2,4,128,128]{3,2,1,0:T(8,128)} %param.4), channel_id=1, source_target_pairs={{0,672},{24,696},{48,720},{72,744},{96,0},{120,24},{144,48},{168,7... | collective-permute-start | bytes 1572872 | tf_op jit(solution)/shard_map/ppermute | solution.py:26
  11.6 107.7 %collective-permute-start.4 = (f32[2,4,128,128]{3,2,1,0:T(8,128)}, f32[2,4,128,128]{3,2,1,0:T(8,128)S(1)}, u32[]{:S(2)}, u32[]{:S(2)}) collective-permute-start(f32[2,4,128,128]{3,2,1,0:T(8,128)} %param.4), channel_id=1, source_target_pairs={{0,696},{24,720},{48,744},{72,0},{96,24},{120,48},{144,72},{168,96... | collective-permute-start | bytes 1572872 | tf_op jit(solution)/shard_map/ppermute | solution.py:26
  20.6 51.3 %collective-permute-start = (f32[1,4,128,128]{3,2,1,0:T(8,128)}, f32[1,4,128,128]{3,2,1,0:T(8,128)}, u32[]{:S(2)}, u32[]{:S(2)}) collective-permute-start(f32[1,4,128,128]{3,2,1,0:T(8,128)} %get-tuple-element.11), channel_id=1, source_target_pairs={{0,1},{1,2},{2,3},{3,4},{4,5},{5,6},{6,7},{7,8},{8,9},{9,10},{10,1... | collective-permute-start | bytes 786440 | tf_op jit(solution)/shard_map/ppermute | solution.py:14
  23.8 90.4 %collective-permute-start.1 = (f32[1,4,128,128]{3,2,1,0:T(8,128)}, f32[1,4,128,128]{3,2,1,0:T(8,128)S(1)}, u32[]{:S(2)}, u32[]{:S(2)}) collective-permute-start(f32[1,4,128,128]{3,2,1,0:T(8,128)} %get-tuple-element.10), channel_id=1, source_target_pairs={{1,0},{2,1},{3,2},{4,3},{5,4},{6,5},{7,6},{8,7},{9,8},{10,9},{11,1... | collective-permute-start | bytes 786440 | tf_op jit(solution)/shard_map/ppermute | solution.py:16
  45.3 100.3 %copy-start.3 = (s32[2,6]{1,0:T(2,128)}, s32[2,6]{1,0:T(2,128)S(1)}, u32[]{:S(2)}) copy-start(s32[2,6]{1,0:T(2,128)S(1)} %broadcast_select_fusion.4) | copy-start | bytes 148
  47.4 90.4 %copy-start.5 = (f32[2,6]{1,0:T(2,128)}, f32[2,6]{1,0:T(2,128)S(1)}, u32[]{:S(2)}) copy-start(f32[2,6]{1,0:T(2,128)S(1)} %compare_convert_fusion) | copy-start | bytes 148
  71.9 47.4 %collective-permute-start.5 = (f32[2,4,128,128]{3,2,1,0:T(8,128)S(1)}, f32[2,4,128,128]{3,2,1,0:T(8,128)S(1)}, u32[]{:S(2)}, u32[]{:S(2)}) collective-permute-start(f32[2,4,128,128]{3,2,1,0:T(8,128)S(1)} %copy-done.2), channel_id=1, source_target_pairs={{0,24},{24,48},{48,72},{72,96},{96,120},{120,144},{144,168},{168,1... | collective-permute-start | bytes 1572872 | tf_op jit(solution)/shard_map/ppermute | solution.py:26
  114.3 18.4 %collective-permute-start.6 = (f32[2,4,128,128]{3,2,1,0:T(8,128)S(1)}, f32[2,4,128,128]{3,2,1,0:T(8,128)S(1)}, u32[]{:S(2)}, u32[]{:S(2)}) collective-permute-start(f32[2,4,128,128]{3,2,1,0:T(8,128)S(1)} %copy-done.2), channel_id=1, source_target_pairs={{0,72},{24,96},{48,120},{72,144},{96,168},{120,192},{144,216},{168... | collective-permute-start | bytes 1572872 | tf_op jit(solution)/shard_map/ppermute | solution.py:26
  116.2 16.5 %collective-permute-start.7 = (f32[2,4,128,128]{3,2,1,0:T(8,128)S(1)}, f32[2,4,128,128]{3,2,1,0:T(8,128)S(1)}, u32[]{:S(2)}, u32[]{:S(2)}) collective-permute-start(f32[2,4,128,128]{3,2,1,0:T(8,128)S(1)} %copy-done.2), channel_id=1, source_target_pairs={{0,744},{24,0},{48,24},{72,48},{96,72},{120,96},{144,120},{168,144... | collective-permute-start | bytes 1572872 | tf_op jit(solution)/shard_map/ppermute | solution.py:26
  141.8 0.9 copy-start.1
  143.6 36.3 %collective-permute-start.8 = (f32[1,6,128,128]{2,3,1,0:T(8,128)}, f32[1,6,128,128]{2,3,1,0:T(8,128)S(1)}, u32[]{:S(2)}, u32[]{:S(2)}) collective-permute-start(f32[1,6,128,128]{2,3,1,0:T(8,128)} %get-tuple-element.9), channel_id=1, source_target_pairs={{0,1},{1,2},{2,3},{3,4},{4,5},{5,6},{6,7},{7,8},{8,9},{9,10},{10,1... | collective-permute-start | bytes 1179656 | tf_op jit(solution)/shard_map/ppermute | solution.py:14
  146.0 158.0 %collective-permute-start.10 = (f32[2,6,128,128]{2,3,1,0:T(8,128)}, f32[2,6,128,128]{2,3,1,0:T(8,128)S(1)}, u32[]{:S(2)}, u32[]{:S(2)}) collective-permute-start(f32[2,6,128,128]{2,3,1,0:T(8,128)} %copy-done.1), channel_id=1, source_target_pairs={{0,96},{24,120},{48,144},{72,168},{96,192},{120,216},{144,240},{16... | collective-permute-start | bytes 2359304 | tf_op jit(solution)/shard_map/ppermute | solution.py:26
  155.0 153.3 %collective-permute-start.11 = (f32[2,6,128,128]{2,3,1,0:T(8,128)}, f32[2,6,128,128]{2,3,1,0:T(8,128)S(1)}, u32[]{:S(2)}, u32[]{:S(2)}) collective-permute-start(f32[2,6,128,128]{2,3,1,0:T(8,128)} %copy-done.1), channel_id=1, source_target_pairs={{0,672},{24,696},{48,720},{72,744},{96,0},{120,24},{144,48},{168,7... | collective-permute-start | bytes 2359304 | tf_op jit(solution)/shard_map/ppermute | solution.py:26
  158.1 150.2 %collective-permute-start.12 = (f32[2,6,128,128]{2,3,1,0:T(8,128)}, f32[2,6,128,128]{2,3,1,0:T(8,128)S(1)}, u32[]{:S(2)}, u32[]{:S(2)}) collective-permute-start(f32[2,6,128,128]{2,3,1,0:T(8,128)} %copy-done.1), channel_id=1, source_target_pairs={{0,696},{24,720},{48,744},{72,0},{96,24},{120,48},{144,72},{168,96... | collective-permute-start | bytes 2359304 | tf_op jit(solution)/shard_map/ppermute | solution.py:26
  162.5 145.9 %collective-permute-start.13 = (f32[2,6,128,128]{2,3,1,0:T(8,128)}, f32[2,6,128,128]{2,3,1,0:T(8,128)S(1)}, u32[]{:S(2)}, u32[]{:S(2)}) collective-permute-start(f32[2,6,128,128]{2,3,1,0:T(8,128)} %copy-done.1), channel_id=1, source_target_pairs={{0,24},{24,48},{48,72},{72,96},{96,120},{120,144},{144,168},{168,1... | collective-permute-start | bytes 2359304 | tf_op jit(solution)/shard_map/ppermute | solution.py:26
  179.9 9.7 %collective-permute-start.9 = (f32[1,6,128,128]{2,3,1,0:T(8,128)}, f32[1,6,128,128]{2,3,1,0:T(8,128)}, u32[]{:S(2)}, u32[]{:S(2)}) collective-permute-start(f32[1,6,128,128]{2,3,1,0:T(8,128)} %get-tuple-element.8), channel_id=1, source_target_pairs={{1,0},{2,1},{3,2},{4,3},{5,4},{6,5},{7,6},{8,7},{9,8},{10,9},{11,1... | collective-permute-start | bytes 1179656 | tf_op jit(solution)/shard_map/ppermute | solution.py:16
  189.6 123.7 %collective-permute-start.14 = (f32[2,6,128,128]{2,3,1,0:T(8,128)}, f32[2,6,128,128]{2,3,1,0:T(8,128)S(1)}, u32[]{:S(2)}, u32[]{:S(2)}) collective-permute-start(f32[2,6,128,128]{2,3,1,0:T(8,128)} %copy-done.1), channel_id=1, source_target_pairs={{0,72},{24,96},{48,120},{72,144},{96,168},{120,192},{144,216},{168... | collective-permute-start | bytes 2359304 | tf_op jit(solution)/shard_map/ppermute | solution.py:26
  304.0 19.3 %collective-permute-start.15 = (f32[2,6,128,128]{2,3,1,0:T(8,128)}, f32[2,6,128,128]{2,3,1,0:T(8,128)S(1)}, u32[]{:S(2)}, u32[]{:S(2)}) collective-permute-start(f32[2,6,128,128]{2,3,1,0:T(8,128)} %copy-done.1), channel_id=1, source_target_pairs={{0,744},{24,0},{48,24},{72,48},{96,72},{120,96},{144,120},{168,144... | collective-permute-start | bytes 2359304 | tf_op jit(solution)/shard_map/ppermute | solution.py:26
  326.1 3.1 copy-start.4
  326.1 3.1 copy-start.6
where the time goes:
time: 338 us; the launch traced here: 336 us
  starting transfers between devices  216 us (64%)
  waiting for transfers between devices  68.8 us (20%)
  local copies, waits for them, and re-layouts  35.2 us (10%)
  matrix products  8.78 us (3%)
  other arithmetic  6.65 us (2%)
    ppermute x12, starting transfers between devices, passed_along(): return lax.ppermute(value, axis, pairs)  195 us
    ppermute x2, waiting for transfers between devices, with_halo(): lax.ppermute(tail, axis, [(i, (i + 1) % count) for i in range(count)])  39.8 us
    ppermute x12, waiting for transfers between devices, passed_along(): return lax.ppermute(value, axis, pairs)  28.2 us
    ppermute x2, starting transfers between devices, with_halo(): lax.ppermute(head, axis, [((i + 1) % count, i) for i in range(count)])  15.1 us
    unnamed x28, local copies, waits for them, and re-layouts  12.1 us
    dot_general x2, matrix products, pick_product(): jnp.einsum('rsij,rmsjk->rmik', a_vals, picked, precision=lax.Precision.HI...  8.78 us
    gather x3, local copies, waits for them, and re-layouts, pick_product(): picked = jnp.take(block_pool, flat_index, axis=0)  7.89 us
  transfers between devices with their start and end apart: 16, of which 6 were waited for; matrix products, arithmetic and copies ran while one was open for 8% of the time, Pallas kernels for 0%

commit v1 on v0

v1 whole, which is shorter than its diff:
```python
import jax
import jax.numpy as jnp
from jax import lax
from jax.experimental import pallas as pl
from jax.experimental.pallas import tpu as pltpu
from jax.sharding import PartitionSpec as P

GX, GY, GZ = 48, 4, 8
BS = 128
SLOTS = 6

ZERO, UP1, DOWN1, TWO1, UP2, DOWN2, TWO2, UP3 = range(8)
OFFSETS = ((0, 0, 0), (1, 0, 0), (-1, 0, 0), (2, 0, 0), (0, 1, 0), (0, -1, 0), (0, 2, 0), (0, 0, 1))

POS1, POS2, POS3, NPOS1, NPOS2, NPOS3, FPOS2, NEAR2 = range(8)
SLOT_OF = 8
HAS1_ZERO, HAS1_STEP, HAS2_ZERO, HAS2_STEP, HAS2_TWO, HAS3_ZERO, HAS3_STEP = range(16, 23)
META = 24


def wrap(value, size):
    value = jnp.where(value >= size, value - size, value)
    return jnp.where(value < 0, value + size, value)


def structure_kernel(place_ref, xcol_ref, mcol_ref, count_ref, out_ref):
    row, col = place_ref[0], place_ref[1]
    second, third = lax.rem(row, GY), lax.div(row, GY)

    def column(a, b, c):
        return wrap(a, GX) + GX * (wrap(b, GY) + GY * wrap(c, GZ))

    def holds(place, target):
        found = jnp.int32(0)
        count = count_ref[place]
        for m in range(SLOTS):
            hit = jnp.logical_and(count > m, mcol_ref[m, place] == target)
            found = found + hit.astype(jnp.int32)
        return found

    for r in range(2):
        first = 2 * col + r
        me = column(first, second, third)
        pos1 = xcol_ref[1, me] == column(first + 1, second, third)
        pos2 = xcol_ref[2, me] == column(first, second + 1, third)
        pos3 = xcol_ref[3, me] == column(first, second, third + 1)
        s1, s2, s3 = (jnp.where(p, 1, -1) for p in (pos1, pos2, pos3))
        f1, f2, f3 = wrap(first + s1, GX), wrap(second + s2, GY), wrap(third + s3, GZ)
        c1, c2, c3 = column(f1, second, third), column(first, f2, third), column(first, second, f3)
        far2 = column(first, f2 + s2, third)
        npos1 = xcol_ref[1, c1] == column(f1 + 1, second, third)
        npos2 = xcol_ref[2, c2] == column(first, f2 + 1, third)
        npos3 = xcol_ref[3, c3] == column(first, second, f3 + 1)
        fpos2 = xcol_ref[2, far2] == column(first, f2 + s2 + 1 - jnp.where(f2 + s2 >= GY, GY, 0), third)
        even = lax.rem(second, 2) == 0
        for place, flag in (
            (POS1, pos1),
            (POS2, pos2),
            (POS3, pos3),
            (NPOS1, npos1),
            (NPOS2, npos2),
            (NPOS3, npos3),
            (FPOS2, fpos2),
            (NEAR2, pos2 == even),
        ):
            out_ref[r, place] = flag.astype(jnp.int32)
        count = count_ref[me]
        for k, (a, b, c) in enumerate(OFFSETS):
            target = column(first + a, second + b, third + c)
            slot = jnp.int32(-1)
            for m in range(SLOTS):
                hit = jnp.logical_and(count > m, mcol_ref[m, me] == target)
                slot = jnp.where(hit, m, slot)
            out_ref[r, SLOT_OF + k] = slot
        n1, n2 = jnp.where(npos1, 1, -1), jnp.where(npos2, 1, -1)
        out_ref[r, HAS1_ZERO] = holds(c1, c1)
        out_ref[r, HAS1_STEP] = holds(c1, column(f1 + n1, second, third))
        out_ref[r, HAS2_ZERO] = holds(c2, c2)
        out_ref[r, HAS2_STEP] = holds(c2, column(first, f2 + n2, third))
        out_ref[r, HAS2_TWO] = holds(c2, column(first, f2 + 2, third))
        out_ref[r, HAS3_ZERO] = holds(c3, c3)
        out_ref[r, HAS3_STEP] = holds(c3, column(first, second, f3 + 1))
        out_ref[r, META - 1] = jnp.int32(0)


def halves(value):
    high = value.astype(jnp.bfloat16)
    low = (value - high.astype(jnp.float32)).astype(jnp.bfloat16)
    return high, low


def left(value):
    high, low = halves(value)
    return jnp.concatenate([high, low, high], axis=1)


def right(value):
    high, low = halves(value)
    return jnp.concatenate([high, high, low], axis=0)


def product(lefts, rights):
    a = lefts[0] if len(lefts) == 1 else jnp.concatenate(lefts, axis=1)
    b = rights[0] if len(rights) == 1 else jnp.concatenate(rights, axis=0)
    return jnp.dot(a, b, preferred_element_type=jnp.float32)


def row_view(meta, r):
    flag = lambda k: meta[r, k] != 0
    slot = lambda k: meta[r, SLOT_OF + k]
    return flag, slot


def first_neighbour(r, pos1, x, from_left, from_right):
    ups = (x[1, 0], x[1, 1]) if r == 0 else (from_right[0], from_right[1])
    downs = (from_left[0], from_left[1]) if r == 0 else (x[0, 0], x[0, 1])
    return jnp.where(pos1, ups[0], downs[0]), jnp.where(pos1, ups[1], downs[1])


def square_kernel(
    meta, x, from_left, from_right, near, across, above, below, square, middle, middle0, middle1
):
    square[...] = jnp.zeros_like(square)
    for r in range(2):
        flag, slot = row_view(meta, r)
        pos1, pos2, pos3 = flag(POS1), flag(POS2), flag(POS3)
        mutual = [flag(POS1 + k) != flag(NPOS1 + k) for k in range(3)]
        d, a1, a2, a3 = (x[r, s] for s in range(4))
        d1, b1 = first_neighbour(r, pos1, x, from_left, from_right)
        near2 = flag(NEAR2)
        d2 = jnp.where(near2, near[0, r], across[0, r])
        b2 = jnp.where(near2, near[1, r], across[1, r])
        d3 = above[0, r]
        b3 = jnp.where(pos3, above[1, r], below[r])
        ld, l1, l2, l3 = left(d), left(a1), left(a2), left(a3)
        zero = jnp.zeros_like(d)

        centre = product(
            [ld, l1, l2, l3],
            [right(d)] + [right(jnp.where(m, b, zero)) for m, b in zip(mutual, (b1, b2, b3))],
        )
        middle[r] = centre
        (middle0 if r == 0 else middle1)[0] = centre

        @pl.when(slot(ZERO) >= 0)
        def _():
            square[r, slot(ZERO)] = centre

        step1 = jnp.where(pos1, slot(UP1), slot(DOWN1))
        step2 = jnp.where(pos2, slot(UP2), slot(DOWN2))

        @pl.when(step1 >= 0)
        def _():
            square[r, step1] = product([ld, l1], [right(a1), right(d1)])

        @pl.when(jnp.logical_and(slot(TWO1) >= 0, jnp.logical_and(pos1, flag(NPOS1))))
        def _():
            square[r, slot(TWO1)] = product([l1], [right(b1)])

        @pl.when(step2 >= 0)
        def _():
            square[r, step2] = product([ld, l2], [right(a2), right(d2)])

        @pl.when(jnp.logical_and(slot(TWO2) >= 0, pos2 == flag(NPOS2)))
        def _():
            square[r, slot(TWO2)] = product([l2], [right(b2)])

        @pl.when(jnp.logical_and(slot(UP3) >= 0, pos3))
        def _():
            square[r, slot(UP3)] = product([ld, l3], [right(a3), right(d3)])


def cube_kernel(
    meta,
    x,
    square,
    from_left,
    from_right,
    right_next,
    near,
    across,
    opposite,
    above,
    below,
    below_d,
    mid_left,
    mid_right,
    mid_local,
    mid_near,
    mid_across,
    mid_above,
    cube,
):
    for r in range(2):
        flag, slot = row_view(meta, r)
        pos1, pos2, pos3 = flag(POS1), flag(POS2), flag(POS3)
        npos1, npos2 = flag(NPOS1), flag(NPOS2)
        d, a1, a2, a3 = (x[r, s] for s in range(4))
        ld = left(d)
        for m in range(SLOTS):
            cube[r, m] = product([ld], [right(square[r, m])])

        step1 = jnp.where(pos1, slot(UP1), slot(DOWN1))
        mutual1 = pos1 != npos1
        other1 = jnp.where(mutual1, slot(ZERO), jnp.where(pos1, slot(TWO1), -1))
        d1, b1 = first_neighbour(r, pos1, x, from_left, from_right)

        @pl.when(jnp.logical_and(step1 >= 0, flag(HAS1_ZERO)))
        def _():
            up = mid_local[1] if r == 0 else mid_right[0]
            down = mid_left[0] if r == 0 else mid_local[0]
            cube[r, step1] += product([left(a1)], [right(jnp.where(pos1, up, down))])

        @pl.when(jnp.logical_and(other1 >= 0, flag(HAS1_STEP)))
        def _():
            beyond = jnp.where(mutual1, d, from_right[0] if r == 0 else right_next[0])
            step = product([left(d1), left(b1)], [right(b1), right(beyond)])
            cube[r, other1] += product([left(a1)], [right(step)])

        near2 = flag(NEAR2)
        step2 = jnp.where(pos2, slot(UP2), slot(DOWN2))
        back2 = jnp.where(pos2, slot(DOWN2), slot(UP2))
        mutual2 = pos2 != npos2
        other2 = jnp.where(mutual2, slot(ZERO), slot(TWO2))
        d2 = jnp.where(near2, near[0, r], across[0, r])
        b2 = jnp.where(near2, near[1, r], across[1, r])

        @pl.when(jnp.logical_and(step2 >= 0, flag(HAS2_ZERO)))
        def _():
            middle = jnp.where(near2, mid_near[r], mid_across[r])
            cube[r, step2] += product([left(a2)], [right(middle)])

        @pl.when(jnp.logical_and(other2 >= 0, flag(HAS2_STEP)))
        def _():
            beyond = jnp.where(mutual2, d, opposite[0, r])
            step = product([left(d2), left(b2)], [right(b2), right(beyond)])
            cube[r, other2] += product([left(a2)], [right(step)])

        onward2 = jnp.logical_and(jnp.logical_not(mutual2), npos2 == flag(FPOS2))

        @pl.when(jnp.logical_and(onward2, jnp.logical_and(back2 >= 0, flag(HAS2_TWO))))
        def _():
            two = product([left(b2)], [right(opposite[1, r])])
            cube[r, back2] += product([left(a2)], [right(two)])

        @pl.when(jnp.logical_and(pos3, jnp.logical_and(slot(UP3) >= 0, flag(HAS3_ZERO))))
        def _():
            cube[r, slot(UP3)] += product([left(a3)], [right(mid_above[r])])

        back3 = jnp.logical_and(jnp.logical_not(pos3), flag(NPOS3))

        @pl.when(jnp.logical_and(back3, jnp.logical_and(slot(ZERO) >= 0, flag(HAS3_STEP))))
        def _():
            b3 = below[r]
            step = product([left(below_d[r]), left(b3)], [right(b3), right(d)])
            cube[r, slot(ZERO)] += product([left(a3)], [right(step)])


def call(kernel, out_shapes, *operands, smem=0, smem_out=False, flops=0):
    spaces = [pltpu.SMEM] * smem + [pltpu.VMEM] * (len(operands) - smem)
    out_space = pltpu.SMEM if smem_out else pltpu.VMEM
    return pl.pallas_call(
        kernel,
        out_shape=out_shapes,
        in_specs=[pl.BlockSpec(memory_space=s) for s in spaces],
        out_specs=jax.tree.map(lambda _: pl.BlockSpec(memory_space=out_space), out_shapes),
        compiler_params=pltpu.CompilerParams(vmem_limit_bytes=32 * 2**20),
        cost_estimate=pl.CostEstimate(flops=flops, bytes_accessed=2**21, transcendentals=0),
    )(*operands)


def per_device(x, x_cols, mask_cols, mask_count):
    row_count, col_count = lax.axis_size("row"), lax.axis_size("col")
    row, col = lax.axis_index("row"), lax.axis_index("col")

    def along(value, axis, target, count):
        return lax.ppermute(value, axis, [(i, target(i) % count) for i in range(count)])

    def to_col(value, step):
        return along(value, "col", lambda i: i + step, col_count)

    def to_row(value, step):
        return along(value, "row", lambda i: i + step, row_count)

    def flip_row(value, bits):
        return along(value, "row", lambda i: i ^ bits, row_count)

    block = lambda *lead: jax.ShapeDtypeStruct(lead + (BS, BS), jnp.float32)

    pair2 = jnp.stack([x[:, 0], x[:, 2]])
    pair3 = jnp.stack([x[:, 0], x[:, 3]])
    above = to_row(pair3, -GY)
    below = to_row(x[:, 3], GY)
    opposite = flip_row(pair2, 2)
    near = flip_row(pair2, 1)
    from_left = to_col(x[1, 0:2], 1)
    from_right = to_col(x[0, 0:2], -1)
    across = flip_row(opposite, 1)
    below_d = to_row(x[:, 0], GY)
    right_next = to_col(x[1, 0:1], -1)

    place = jnp.stack([row, col]).astype(jnp.int32)
    meta = call(
        structure_kernel,
        jax.ShapeDtypeStruct((2, META), jnp.int32),
        place,
        x_cols.T,
        mask_cols.T,
        mask_count,
        smem=4,
        smem_out=True,
    )
    square, middle, middle0, middle1 = call(
        square_kernel,
        [block(2, SLOTS), block(2), block(1), block(1)],
        meta,
        x,
        from_left,
        from_right,
        near,
        across,
        above,
        below,
        smem=1,
        flops=60 * 2 * BS**3,
    )
    mid_above = to_row(middle, -GY)
    mid_left = to_col(middle1, 1)
    mid_right = to_col(middle0, -1)
    mid_across = flip_row(middle, 3)
    mid_near = flip_row(middle, 1)
    cube = call(
        cube_kernel,
        block(2, SLOTS),
        meta,
        x,
        square,
        from_left,
        from_right,
        right_next,
        near,
        across,
        opposite,
        above,
        below,
        below_d,
        mid_left,
        mid_right,
        middle,
        mid_near,
        mid_across,
        mid_above,
        smem=1,
        flops=80 * 2 * BS**3,
    )
    return square, cube


def solution(mesh):
    in_specs = (P(("row", "col"), None, None, None), P(), P(), P())
    out_specs = (P(("row", "col"), None, None, None), P(("row", "col"), None, None, None))
    return jax.shard_map(
        per_device, mesh=mesh, in_specs=in_specs, out_specs=out_specs, check_vma=False
    )
```

time: 338 us -> 102 us (0.30)
  starting transfers between devices: 216 us -> 78.8 us
  waiting for transfers between devices: 68.8 us -> 9.17 us
  local copies, waits for them, and re-layouts: 35.2 us -> 2.26 us
  Pallas kernels: 0 us -> 9.25 us
  matrix products: 8.78 us -> 0 us
  other arithmetic: 6.65 us -> 0.11 us
    ppermute x16 -> x14, starting transfers between devices: 216 us -> 78.8 us  [along(): lax.ppermute(value, axis, [(i, target(i) % count) for i in range(count)])]
    ppermute x16 -> x14, waiting for transfers between devices: 68.8 us -> 9.17 us  [along(): lax.ppermute(value, axis, [(i, target(i) % count) for i in range(count)])]
    gather x11 -> x0, local copies, waits for them, and re-layouts: 12 us -> none  [the longest x3 7.89 us: pick_product(): picked = jnp.take(block_pool, flat_index, axis=0)]
    unnamed x28 -> x10, local copies, waits for them, and re-layouts: 12.1 us -> 1.15 us
    pallas_call x0 -> x3, Pallas kernels: none -> 9.25 us  [call(): pl.pallas_call(kernel, out_shape=out_shapes, in_specs=[pl.BlockSpec(memor...]
    dot_general x2 -> x0, matrix products: 8.78 us -> none  [pick_product(): jnp.einsum('rsij,rmsjk->rmik', a_vals, picked, precision=lax.Precision.HI...]
    concatenate x4 -> x0, local copies, waits for them, and re-layouts: 4.36 us -> none  [the longest x2 3.07 us: add_empty(): jnp.concatenate([flat_blocks, jnp.zeros((1, block_size, block_size), valu...]
  transfers between devices with their start and end apart: 16 -> 14, of which waited for: 6 -> 3; matrix products, arithmetic and copies ran while one was open for 8% -> 0% of each run, Pallas kernels for 0% -> 6%
where the time goes in v1:
time: 102 us; the launch traced here: 101 us
  starting transfers between devices  78.8 us (77%)
  Pallas kernels  9.25 us (9%)
  waiting for transfers between devices  9.17 us (9%)
  local copies, waits for them, and re-layouts  2.26 us (2%)
    ppermute x14, starting transfers between devices, along(): lax.ppermute(value, axis, [(i, target(i) % count) for i in range(count)])  78.8 us
    pallas_call x3, Pallas kernels, call(): pl.pallas_call(kernel, out_shape=out_shapes, in_specs=[pl.BlockSpec(memor...  9.25 us
    ppermute x14, waiting for transfers between devices, along(): lax.ppermute(value, axis, [(i, target(i) % count) for i in range(count)])  9.17 us
  transfers between devices with their start and end apart: 14, of which 3 were waited for; matrix products, arithmetic and copies ran while one was open for 0% of the time, Pallas kernels for 6%

profile of v1, /device:TPU:1, one launch (start us, length us, event | category | flops | bytes accessed | tf_op | source)
XLA Modules:
  0.0 100.5 jit_solution(16184315209327328101)
XLA Ops:
  0.6 1.1 %slice_bitcast_fusion.6 = (f32[2,128,128]{2,1,0:T(8,128)S(1)}, f32[1,2,128,128]{3,2,1,0:T(8,128)S(1)}, f32[1,2,128,128]{3,2,1,0:T(8,128)S(1)}, f32[1,2,128,128]{3,2,1,0:T(8,128)S(1)}, f32[2,128,128]{2,1,0:T(8,128)S(1)}) fusion(f32[2,4,128,128]{3,2,1,0:T(8,128)} %x.3), kind=kLoop, calls=%fused_computation.8 | loop fusion | bytes 1048576 | tf_op jit(solution)/shard_map/squeeze | solution.py:299
  1.7 0.0 copy-start
  1.8 5.0 %collective-permute-start.3 = (f32[2,2,128,128]{3,2,1,0:T(8,128)S(1)}, f32[2,2,128,128]{3,2,1,0:T(8,128)S(1)}, u32[]{:S(2)}, u32[]{:S(2)}) collective-permute-start(f32[2,2,128,128]{3,2,1,0:T(8,128)S(1)} %get-tuple-element.18), channel_id=1, source_target_pairs={{0,48},{24,72},{48,0},{72,24},{96,144},{120,168},{144,96},{168,120... | collective-permute-start | bytes 786440 | tf_op jit(solution)/shard_map/ppermute | solution.py:277
  6.8 16.3 %collective-permute-start.1 = (f32[2,128,128]{2,1,0:T(8,128)S(1)}, f32[2,128,128]{2,1,0:T(8,128)S(1)}, u32[]{:S(2)}, u32[]{:S(2)}) collective-permute-start(f32[2,128,128]{2,1,0:T(8,128)S(1)} %get-tuple-element.15), channel_id=1, source_target_pairs={{0,23},{1,0},{2,1},{3,2},{4,3},{5,4},{6,5},{7,6},{8,7},{9,8},{10,9... | collective-permute-start | bytes 393224 | tf_op jit(solution)/shard_map/ppermute | solution.py:277
  23.1 3.1 %collective-permute-start.2 = (f32[2,2,128,128]{3,2,1,0:T(8,128)S(1)}, f32[2,2,128,128]{3,2,1,0:T(8,128)S(1)}, u32[]{:S(2)}, u32[]{:S(2)}) collective-permute-start(f32[2,2,128,128]{3,2,1,0:T(8,128)S(1)} %get-tuple-element.18), channel_id=1, source_target_pairs={{0,24},{24,0},{48,72},{72,48},{96,120},{120,96},{144,168},{168,144... | collective-permute-start | bytes 786440 | tf_op jit(solution)/shard_map/ppermute | solution.py:277
  26.2 1.9 %collective-permute-start = (f32[2,128,128]{2,1,0:T(8,128)S(1)}, f32[2,128,128]{2,1,0:T(8,128)S(1)}, u32[]{:S(2)}, u32[]{:S(2)}) collective-permute-start(f32[2,128,128]{2,1,0:T(8,128)S(1)} %get-tuple-element.16), channel_id=1, source_target_pairs={{0,1},{1,2},{2,3},{3,4},{4,5},{5,6},{6,7},{7,8},{8,9},{9,10},{10,1... | collective-permute-start | bytes 393224 | tf_op jit(solution)/shard_map/ppermute | solution.py:277
  28.1 4.0 %collective-permute-start.6 = (f32[2,128,128]{2,1,0:T(8,128)S(1)}, f32[2,128,128]{2,1,0:T(8,128)S(1)}, u32[]{:S(2)}, u32[]{:S(2)}) collective-permute-start(f32[2,128,128]{2,1,0:T(8,128)S(1)} %get-tuple-element.14), channel_id=1, source_target_pairs={{0,96},{24,120},{48,144},{72,168},{96,192},{120,216},{144,240},{16... | collective-permute-start | bytes 393224 | tf_op jit(solution)/shard_map/ppermute | solution.py:277
  32.2 2.6 %collective-permute-done.1.from_right = f32[2,128,128]{2,1,0:T(8,128)S(1)} collective-permute-done((f32[2,128,128]{2,1,0:T(8,128)S(1)}, f32[2,128,128]{2,1,0:T(8,128)S(1)}, u32[]{:S(2)}, u32[]{:S(2)}) %collective-permute-start.1) | collective-permute-done | bytes 131104 | tf_op jit(solution)/shard_map/ppermute | solution.py:277
  34.7 5.5 %collective-permute-start.5 = (f32[2,2,128,128]{3,2,1,0:T(8,128)S(1)}, f32[2,2,128,128]{3,2,1,0:T(8,128)S(1)}, u32[]{:S(2)}, u32[]{:S(2)}) collective-permute-start(f32[2,2,128,128]{3,2,1,0:T(8,128)S(1)} %get-tuple-element.17), channel_id=1, source_target_pairs={{0,672},{24,696},{48,720},{72,744},{96,0},{120,24},{144,48},{168,7... | collective-permute-start | bytes 786440 | tf_op jit(solution)/shard_map/ppermute | solution.py:277
  40.2 2.9 %collective-permute-start.4 = (f32[2,2,128,128]{3,2,1,0:T(8,128)S(1)}, f32[2,2,128,128]{3,2,1,0:T(8,128)S(1)}, u32[]{:S(2)}, u32[]{:S(2)}) collective-permute-start(f32[2,2,128,128]{3,2,1,0:T(8,128)S(1)} %collective-permute-done.3.opposite), channel_id=1, source_target_pairs={{0,24},{24,0},{48,72},{72,48},{96,120},{120,96},{144,168},{168,144... | collective-permute-start | bytes 786440 | tf_op jit(solution)/shard_map/ppermute | solution.py:277
  43.1 0.0 copy-start.3
  43.1 0.0 copy-start.4
  43.1 2.8 %collective-permute-done.from_left = f32[2,128,128]{2,1,0:T(8,128)S(1)} collective-permute-done((f32[2,128,128]{2,1,0:T(8,128)S(1)}, f32[2,128,128]{2,1,0:T(8,128)S(1)}, u32[]{:S(2)}, u32[]{:S(2)}) %collective-permute-start) | collective-permute-done | bytes 131104 | tf_op jit(solution)/shard_map/ppermute | solution.py:277
  45.9 1.9 %collective-permute-start.8 = (f32[2,128,128]{2,1,0:T(8,128)S(1)}, f32[2,128,128]{2,1,0:T(8,128)S(1)}, u32[]{:S(2)}, u32[]{:S(2)}) collective-permute-start(f32[2,128,128]{2,1,0:T(8,128)S(1)} %get-tuple-element.10), channel_id=1, source_target_pairs={{0,96},{24,120},{48,144},{72,168},{96,192},{120,216},{144,240},{16... | collective-permute-start | bytes 393224 | tf_op jit(solution)/shard_map/ppermute | solution.py:277
  47.9 0.1 pad_add_fusion.place_ref
  47.9 2.9 %shard_map.59.meta = s32[2,24]{1,0:T(2,128)S(1)} custom-call(s32[2]{0:T(128)S(1)} %pad_add_fusion.place_ref, s32[4,1536]{1,0:T(4,128)S(1)} %bitcast.29, s32[6,1536]{1,0:T(8,128)S(1)} %bitcast.28, s32[1536]{0:T(1024)S(1)} %copy-done.4), custom_call_target="tpu_custom_call" | custom-call | bytes 2097152 | tf_op jit(solution)/shard_map/pallas_call | solution.py:262
  50.9 7.4 %collective-permute-start.7 = (f32[1,128,128]{2,1,0:T(8,128)S(1)}, f32[1,128,128]{2,1,0:T(8,128)S(1)}, u32[]{:S(2)}, u32[]{:S(2)}) collective-permute-start(f32[1,128,128]{2,1,0:T(8,128)S(1)} %slice_bitcast_fusion.7), channel_id=1, source_target_pairs={{0,23},{1,0},{2,1},{3,2},{4,3},{5,4},{6,5},{7,6},{8,7},{9,8},{10,9... | collective-permute-start | bytes 196616 | tf_op jit(solution)/shard_map/ppermute | solution.py:277
  58.3 0.0 collective-permute-done.5.above
  58.3 2.8 %shard_map.60 = (f32[2,6,128,128]{3,2,1,0:T(8,128)}, f32[2,128,128]{2,1,0:T(8,128)S(1)}, f32[1,128,128]{2,1,0:T(8,128)S(1)}, f32[1,128,128]{2,1,0:T(8,128)S(1)}) custom-call(s32[2,24]{1,0:T(2,128)S(1)} %shard_map.59.meta, f32[2,4,128,128]{3,2,1,0:T(8,128)S(1)} %copy-done, f32[2,128,128]{2,1,0:T(8,128)S(1)} %collective-permute-done.from_left, ...), custom_call_target="tpu_custom_call" | custom-call | flops 251658240 | bytes 2097152 | tf_op jit(solution)/shard_map/pallas_call | solution.py:262
  61.1 6.3 %collective-permute-start.13 = (f32[2,128,128]{2,1,0:T(8,128)S(1)}, f32[2,128,128]{2,1,0:T(8,128)S(1)}, u32[]{:S(2)}, u32[]{:S(2)}) collective-permute-start(f32[2,128,128]{2,1,0:T(8,128)S(1)} %get-tuple-element.9.mid_local), channel_id=1, source_target_pairs={{0,672},{24,696},{48,720},{72,744},{96,0},{120,24},{144,48},{168,7... | collective-permute-start | bytes 393224 | tf_op jit(solution)/shard_map/ppermute | solution.py:277
  67.5 11.4 %collective-permute-start.12 = (f32[2,128,128]{2,1,0:T(8,128)S(1)}, f32[2,128,128]{2,1,0:T(8,128)S(1)}, u32[]{:S(2)}, u32[]{:S(2)}) collective-permute-start(f32[2,128,128]{2,1,0:T(8,128)S(1)} %get-tuple-element.9.mid_local), channel_id=1, source_target_pairs={{0,72},{24,48},{48,24},{72,0},{96,168},{120,144},{144,120},{168,96... | collective-permute-start | bytes 393224 | tf_op jit(solution)/shard_map/ppermute | solution.py:277
  78.9 1.9 %collective-permute-start.11 = (f32[2,128,128]{2,1,0:T(8,128)S(1)}, f32[2,128,128]{2,1,0:T(8,128)S(1)}, u32[]{:S(2)}, u32[]{:S(2)}) collective-permute-start(f32[2,128,128]{2,1,0:T(8,128)S(1)} %get-tuple-element.9.mid_local), channel_id=1, source_target_pairs={{0,24},{24,0},{48,72},{72,48},{96,120},{120,96},{144,168},{168,144... | collective-permute-start | bytes 393224 | tf_op jit(solution)/shard_map/ppermute | solution.py:277
  80.8 0.0 collective-permute-done.7.right_next
  80.8 3.6 %collective-permute-start.9 = (f32[1,128,128]{2,1,0:T(8,128)S(1)}, f32[1,128,128]{2,1,0:T(8,128)S(1)}, u32[]{:S(2)}, u32[]{:S(2)}) collective-permute-start(f32[1,128,128]{2,1,0:T(8,128)S(1)} %get-tuple-element.7), channel_id=1, source_target_pairs={{0,1},{1,2},{2,3},{3,4},{4,5},{5,6},{6,7},{7,8},{8,9},{9,10},{10,1... | collective-permute-start | bytes 196616 | tf_op jit(solution)/shard_map/ppermute | solution.py:277
  84.4 0.0 collective-permute-done.8.below_d
  84.4 7.7 %collective-permute-start.10 = (f32[1,128,128]{2,1,0:T(8,128)S(1)}, f32[1,128,128]{2,1,0:T(8,128)S(1)}, u32[]{:S(2)}, u32[]{:S(2)}) collective-permute-start(f32[1,128,128]{2,1,0:T(8,128)S(1)} %get-tuple-element.8), channel_id=1, source_target_pairs={{0,23},{1,0},{2,1},{3,2},{4,3},{5,4},{6,5},{7,6},{8,7},{9,8},{10,9... | collective-permute-start | bytes 196616 | tf_op jit(solution)/shard_map/ppermute | solution.py:277
  92.1 3.8 %collective-permute-done.10.mid_right = f32[1,128,128]{2,1,0:T(8,128)S(1)} collective-permute-done((f32[1,128,128]{2,1,0:T(8,128)S(1)}, f32[1,128,128]{2,1,0:T(8,128)S(1)}, u32[]{:S(2)}, u32[]{:S(2)}) %collective-permute-start.10) | collective-permute-done | bytes 65568 | tf_op jit(solution)/shard_map/ppermute | solution.py:277
  95.9 0.0 collective-permute-done.13.mid_above
  95.9 0.0 collective-permute-done.12.mid_across
  95.9 0.0 copy-start.1
  95.9 1.1 %copy-done.1 = f32[2,6,128,128]{3,2,1,0:T(8,128)S(1)} copy-done((f32[2,6,128,128]{3,2,1,0:T(8,128)S(1)}, f32[2,6,128,128]{3,2,1,0:T(8,128)}, u32[]{:S(2)}) %copy-start.1) | copy-done | bytes 786456
  97.0 3.5 %shard_map.61 = f32[2,6,128,128]{3,2,1,0:T(8,128)} custom-call(s32[2,24]{1,0:T(2,128)S(1)} %shard_map.59.meta, f32[2,4,128,128]{3,2,1,0:T(8,128)S(1)} %copy-done, f32[2,6,128,128]{3,2,1,0:T(8,128)S(1)} %copy-done.1, f32[2,128,128]{2,1,0:T(8,128)S(1)} %collective-permute-done.from_left, f32[2,128,128]{2,1,0:T(8,128)S(1)} %collective-permute-done.1.from_right, ...), custom_call_target="tpu_custom_call" | custom-call | flops 335544320 | bytes 2097152 | tf_op jit(solution)/shard_map/pallas_call | solution.py:262
  (14 shorter events, 0.1 us)
Async XLA Ops:
  1.7 5.0 %copy-start = (f32[2,4,128,128]{3,2,1,0:T(8,128)S(1)}, f32[2,4,128,128]{3,2,1,0:T(8,128)}, u32[]{:S(2)}) copy-start(f32[2,4,128,128]{3,2,1,0:T(8,128)} %x.3) | copy-start | bytes 1572868
  1.8 38.4 %collective-permute-start.3 = (f32[2,2,128,128]{3,2,1,0:T(8,128)S(1)}, f32[2,2,128,128]{3,2,1,0:T(8,128)S(1)}, u32[]{:S(2)}, u32[]{:S(2)}) collective-permute-start(f32[2,2,128,128]{3,2,1,0:T(8,128)S(1)} %get-tuple-element.18), channel_id=1, source_target_pairs={{0,48},{24,72},{48,0},{72,24},{96,144},{120,168},{144,96},{168,120... | collective-permute-start | bytes 786440 | tf_op jit(solution)/shard_map/ppermute | solution.py:277
  6.8 27.9 %collective-permute-start.1 = (f32[2,128,128]{2,1,0:T(8,128)S(1)}, f32[2,128,128]{2,1,0:T(8,128)S(1)}, u32[]{:S(2)}, u32[]{:S(2)}) collective-permute-start(f32[2,128,128]{2,1,0:T(8,128)S(1)} %get-tuple-element.15), channel_id=1, source_target_pairs={{0,23},{1,0},{2,1},{3,2},{4,3},{5,4},{6,5},{7,6},{8,7},{9,8},{10,9... | collective-permute-start | bytes 393224 | tf_op jit(solution)/shard_map/ppermute | solution.py:277
  23.1 35.3 %collective-permute-start.2 = (f32[2,2,128,128]{3,2,1,0:T(8,128)S(1)}, f32[2,2,128,128]{3,2,1,0:T(8,128)S(1)}, u32[]{:S(2)}, u32[]{:S(2)}) collective-permute-start(f32[2,2,128,128]{3,2,1,0:T(8,128)S(1)} %get-tuple-element.18), channel_id=1, source_target_pairs={{0,24},{24,0},{48,72},{72,48},{96,120},{120,96},{144,168},{168,144... | collective-permute-start | bytes 786440 | tf_op jit(solution)/shard_map/ppermute | solution.py:277
  26.2 19.7 %collective-permute-start = (f32[2,128,128]{2,1,0:T(8,128)S(1)}, f32[2,128,128]{2,1,0:T(8,128)S(1)}, u32[]{:S(2)}, u32[]{:S(2)}) collective-permute-start(f32[2,128,128]{2,1,0:T(8,128)S(1)} %get-tuple-element.16), channel_id=1, source_target_pairs={{0,1},{1,2},{2,3},{3,4},{4,5},{5,6},{6,7},{7,8},{8,9},{9,10},{10,1... | collective-permute-start | bytes 393224 | tf_op jit(solution)/shard_map/ppermute | solution.py:277
  28.1 22.8 %collective-permute-start.6 = (f32[2,128,128]{2,1,0:T(8,128)S(1)}, f32[2,128,128]{2,1,0:T(8,128)S(1)}, u32[]{:S(2)}, u32[]{:S(2)}) collective-permute-start(f32[2,128,128]{2,1,0:T(8,128)S(1)} %get-tuple-element.14), channel_id=1, source_target_pairs={{0,96},{24,120},{48,144},{72,168},{96,192},{120,216},{144,240},{16... | collective-permute-start | bytes 393224 | tf_op jit(solution)/shard_map/ppermute | solution.py:277
  34.7 13.2 %copy-start.2 = (s32[1536,6]{0,1:T(8,128)S(1)}, s32[1536,6]{0,1:T(8,128)}, u32[]{:S(2)}) copy-start(s32[1536,6]{0,1:T(8,128)} %param.6) | copy-start | bytes 110596
  34.7 23.6 %collective-permute-start.5 = (f32[2,2,128,128]{3,2,1,0:T(8,128)S(1)}, f32[2,2,128,128]{3,2,1,0:T(8,128)S(1)}, u32[]{:S(2)}, u32[]{:S(2)}) collective-permute-start(f32[2,2,128,128]{3,2,1,0:T(8,128)S(1)} %get-tuple-element.17), channel_id=1, source_target_pairs={{0,672},{24,696},{48,720},{72,744},{96,0},{120,24},{144,48},{168,7... | collective-permute-start | bytes 786440 | tf_op jit(solution)/shard_map/ppermute | solution.py:277
  40.2 18.1 %collective-permute-start.4 = (f32[2,2,128,128]{3,2,1,0:T(8,128)S(1)}, f32[2,2,128,128]{3,2,1,0:T(8,128)S(1)}, u32[]{:S(2)}, u32[]{:S(2)}) collective-permute-start(f32[2,2,128,128]{3,2,1,0:T(8,128)S(1)} %collective-permute-done.3.opposite), channel_id=1, source_target_pairs={{0,24},{24,0},{48,72},{72,48},{96,120},{120,96},{144,168},{168,144... | collective-permute-start | bytes 786440 | tf_op jit(solution)/shard_map/ppermute | solution.py:277
  43.1 4.9 %copy-start.3 = (s32[1536,4]{0,1:T(4,128)S(1)}, s32[1536,4]{0,1:T(4,128)}, u32[]{:S(2)}) copy-start(s32[1536,4]{0,1:T(4,128)} %param.5) | copy-start | bytes 73732
  43.1 4.8 %copy-start.4 = (s32[1536]{0:T(1024)S(1)}, s32[1536]{0:T(1024)}, u32[]{:S(2)}) copy-start(s32[1536]{0:T(1024)} %count_ref.1) | copy-start | bytes 18436
  45.9 38.4 %collective-permute-start.8 = (f32[2,128,128]{2,1,0:T(8,128)S(1)}, f32[2,128,128]{2,1,0:T(8,128)S(1)}, u32[]{:S(2)}, u32[]{:S(2)}) collective-permute-start(f32[2,128,128]{2,1,0:T(8,128)S(1)} %get-tuple-element.10), channel_id=1, source_target_pairs={{0,96},{24,120},{48,144},{72,168},{96,192},{120,216},{144,240},{16... | collective-permute-start | bytes 393224 | tf_op jit(solution)/shard_map/ppermute | solution.py:277
  50.9 29.9 %collective-permute-start.7 = (f32[1,128,128]{2,1,0:T(8,128)S(1)}, f32[1,128,128]{2,1,0:T(8,128)S(1)}, u32[]{:S(2)}, u32[]{:S(2)}) collective-permute-start(f32[1,128,128]{2,1,0:T(8,128)S(1)} %slice_bitcast_fusion.7), channel_id=1, source_target_pairs={{0,23},{1,0},{2,1},{3,2},{4,3},{5,4},{6,5},{7,6},{8,7},{9,8},{10,9... | collective-permute-start | bytes 196616 | tf_op jit(solution)/shard_map/ppermute | solution.py:277
  61.1 34.7 %collective-permute-start.13 = (f32[2,128,128]{2,1,0:T(8,128)S(1)}, f32[2,128,128]{2,1,0:T(8,128)S(1)}, u32[]{:S(2)}, u32[]{:S(2)}) collective-permute-start(f32[2,128,128]{2,1,0:T(8,128)S(1)} %get-tuple-element.9.mid_local), channel_id=1, source_target_pairs={{0,672},{24,696},{48,720},{72,744},{96,0},{120,24},{144,48},{168,7... | collective-permute-start | bytes 393224 | tf_op jit(solution)/shard_map/ppermute | solution.py:277
  67.5 28.4 %collective-permute-start.12 = (f32[2,128,128]{2,1,0:T(8,128)S(1)}, f32[2,128,128]{2,1,0:T(8,128)S(1)}, u32[]{:S(2)}, u32[]{:S(2)}) collective-permute-start(f32[2,128,128]{2,1,0:T(8,128)S(1)} %get-tuple-element.9.mid_local), channel_id=1, source_target_pairs={{0,72},{24,48},{48,24},{72,0},{96,168},{120,144},{144,120},{168,96... | collective-permute-start | bytes 393224 | tf_op jit(solution)/shard_map/ppermute | solution.py:277
  78.9 17.0 %collective-permute-start.11 = (f32[2,128,128]{2,1,0:T(8,128)S(1)}, f32[2,128,128]{2,1,0:T(8,128)S(1)}, u32[]{:S(2)}, u32[]{:S(2)}) collective-permute-start(f32[2,128,128]{2,1,0:T(8,128)S(1)} %get-tuple-element.9.mid_local), channel_id=1, source_target_pairs={{0,24},{24,0},{48,72},{72,48},{96,120},{120,96},{144,168},{168,144... | collective-permute-start | bytes 393224 | tf_op jit(solution)/shard_map/ppermute | solution.py:277
  80.8 11.3 %collective-permute-start.9 = (f32[1,128,128]{2,1,0:T(8,128)S(1)}, f32[1,128,128]{2,1,0:T(8,128)S(1)}, u32[]{:S(2)}, u32[]{:S(2)}) collective-permute-start(f32[1,128,128]{2,1,0:T(8,128)S(1)} %get-tuple-element.7), channel_id=1, source_target_pairs={{0,1},{1,2},{2,3},{3,4},{4,5},{5,6},{6,7},{7,8},{8,9},{9,10},{10,1... | collective-permute-start | bytes 196616 | tf_op jit(solution)/shard_map/ppermute | solution.py:277
  84.4 11.5 %collective-permute-start.10 = (f32[1,128,128]{2,1,0:T(8,128)S(1)}, f32[1,128,128]{2,1,0:T(8,128)S(1)}, u32[]{:S(2)}, u32[]{:S(2)}) collective-permute-start(f32[1,128,128]{2,1,0:T(8,128)S(1)} %get-tuple-element.8), channel_id=1, source_target_pairs={{0,23},{1,0},{2,1},{3,2},{4,3},{5,4},{6,5},{7,6},{8,7},{9,8},{10,9... | collective-permute-start | bytes 196616 | tf_op jit(solution)/shard_map/ppermute | solution.py:277
  95.9 1.1 %copy-start.1 = (f32[2,6,128,128]{3,2,1,0:T(8,128)S(1)}, f32[2,6,128,128]{3,2,1,0:T(8,128)}, u32[]{:S(2)}) copy-start(f32[2,6,128,128]{3,2,1,0:T(8,128)} %get-tuple-element.4.square) | copy-start | bytes 2359300

commit v2 on v1

--- a/solution.py
+++ b/solution.py
@@ -14,7 +14,7 @@
 
 POS1, POS2, POS3, NPOS1, NPOS2, NPOS3, FPOS2, NEAR2 = range(8)
 SLOT_OF = 8
-HAS1_ZERO, HAS1_STEP, HAS2_ZERO, HAS2_STEP, HAS2_TWO, HAS3_ZERO, HAS3_STEP = range(16, 23)
+HAS1_ZERO, HAS1_STEP, HAS2_ZERO, HAS2_STEP, HAS2_TWO, HAS3_ZERO, HAS3_STEP, RELAY_OWN = range(16, 24)
 META = 24
 
 
@@ -80,7 +80,10 @@
         out_ref[r, HAS2_TWO] = holds(c2, column(first, f2 + 2, third))
         out_ref[r, HAS3_ZERO] = holds(c3, c3)
         out_ref[r, HAS3_STEP] = holds(c3, column(first, second, f3 + 1))
-        out_ref[r, META - 1] = jnp.int32(0)
+        odd = lax.rem(third, 2)
+        partner = third + 1 - 2 * odd
+        wants_up = xcol_ref[3, column(first, second, partner)] == column(first, second, partner + 1)
+        out_ref[r, RELAY_OWN] = (wants_up == (odd == 1)).astype(jnp.int32)
 
 
 def halves(value):
@@ -117,34 +120,44 @@
     return jnp.where(pos1, ups[0], downs[0]), jnp.where(pos1, ups[1], downs[1])
 
 
+def second_neighbour(r, near2, near, across):
+    return jnp.where(near2, near[0, r], across[0, r]), jnp.where(near2, near[1, r], across[1, r])
+
+
+def middle_kernel(meta, x, from_left, from_right, near, across, third, middle, middle0, middle1):
+    for r in range(2):
+        flag, _ = row_view(meta, r)
+        d, a1, a2, a3 = (x[r, s] for s in range(4))
+        _, b1 = first_neighbour(r, flag(POS1), x, from_left, from_right)
+        _, b2 = second_neighbour(r, flag(NEAR2), near, across)
+        b3 = third[1, r]
+        zero = jnp.zeros_like(d)
+        mutual = [flag(POS1 + k) != flag(NPOS1 + k) for k in range(3)]
+        centre = product(
+            [left(d), left(a1), left(a2), left(a3)],
+            [right(d)] + [right(jnp.where(m, b, zero)) for m, b in zip(mutual, (b1, b2, b3))],
+        )
+        middle[r] = centre
+        (middle0 if r == 0 else middle1)[0] = centre
+
+
 def square_kernel(
-    meta, x, from_left, from_right, near, across, above, below, square, middle, middle0, middle1
+    meta, x, middle, from_left, from_right, near, across, opposite, third, square, cube
 ):
     square[...] = jnp.zeros_like(square)
     for r in range(2):
         flag, slot = row_view(meta, r)
         pos1, pos2, pos3 = flag(POS1), flag(POS2), flag(POS3)
-        mutual = [flag(POS1 + k) != flag(NPOS1 + k) for k in range(3)]
+        npos1, npos2, npos3 = flag(NPOS1), flag(NPOS2), flag(NPOS3)
         d, a1, a2, a3 = (x[r, s] for s in range(4))
         d1, b1 = first_neighbour(r, pos1, x, from_left, from_right)
-        near2 = flag(NEAR2)
-        d2 = jnp.where(near2, near[0, r], across[0, r])
-        b2 = jnp.where(near2, near[1, r], across[1, r])
-        d3 = above[0, r]
-        b3 = jnp.where(pos3, above[1, r], below[r])
+        d2, b2 = second_neighbour(r, flag(NEAR2), near, across)
+        d3, b3 = third[0, r], third[1, r]
         ld, l1, l2, l3 = left(d), left(a1), left(a2), left(a3)
-        zero = jnp.zeros_like(d)
-
-        centre = product(
-            [ld, l1, l2, l3],
-            [right(d)] + [right(jnp.where(m, b, zero)) for m, b in zip(mutual, (b1, b2, b3))],
-        )
-        middle[r] = centre
-        (middle0 if r == 0 else middle1)[0] = centre
 
         @pl.when(slot(ZERO) >= 0)
         def _():
-            square[r, slot(ZERO)] = centre
+            square[r, slot(ZERO)] = middle[r]
 
         step1 = jnp.where(pos1, slot(UP1), slot(DOWN1))
         step2 = jnp.where(pos2, slot(UP2), slot(DOWN2))
@@ -153,7 +166,7 @@
         def _():
             square[r, step1] = product([ld, l1], [right(a1), right(d1)])
 
-        @pl.when(jnp.logical_and(slot(TWO1) >= 0, jnp.logical_and(pos1, flag(NPOS1))))
+        @pl.when(jnp.logical_and(slot(TWO1) >= 0, jnp.logical_and(pos1, npos1)))
         def _():
             square[r, slot(TWO1)] = product([l1], [right(b1)])
 
@@ -161,7 +174,7 @@
         def _():
             square[r, step2] = product([ld, l2], [right(a2), right(d2)])
 
-        @pl.when(jnp.logical_and(slot(TWO2) >= 0, pos2 == flag(NPOS2)))
+        @pl.when(jnp.logical_and(slot(TWO2) >= 0, pos2 == npos2))
         def _():
             square[r, slot(TWO2)] = product([l2], [right(b2)])
 
@@ -169,91 +182,65 @@
         def _():
             square[r, slot(UP3)] = product([ld, l3], [right(a3), right(d3)])
 
-
-def cube_kernel(
-    meta,
-    x,
-    square,
-    from_left,
-    from_right,
-    right_next,
-    near,
-    across,
-    opposite,
-    above,
-    below,
-    below_d,
-    mid_left,
-    mid_right,
-    mid_local,
-    mid_near,
-    mid_across,
-    mid_above,
-    cube,
-):
+        for m in range(SLOTS):
+            cube[r, m] = product([ld], [right(square[r, m])])
+
+        mutual1 = pos1 != npos1
+        other1 = jnp.where(mutual1, slot(ZERO), jnp.where(pos1, slot(TWO1), -1))
+
+        @pl.when(jnp.logical_and(other1 >= 0, flag(HAS1_STEP)))
+        def _():
+            beyond = jnp.where(mutual1, d, from_right[2 * r])
+            step = product([left(d1), left(b1)], [right(b1), right(beyond)])
+            cube[r, other1] += product([l1], [right(step)])
+
+        mutual2 = pos2 != npos2
+        other2 = jnp.where(mutual2, slot(ZERO), slot(TWO2))
+        back2 = jnp.where(pos2, slot(DOWN2), slot(UP2))
+
+        @pl.when(jnp.logical_and(other2 >= 0, flag(HAS2_STEP)))
+        def _():
+            beyond = jnp.where(mutual2, d, opposite[0, r])
+            step = product([left(d2), left(b2)], [right(b2), right(beyond)])
+            cube[r, other2] += product([l2], [right(step)])
+
+        onward2 = jnp.logical_and(jnp.logical_not(mutual2), npos2 == flag(FPOS2))
+
+        @pl.when(jnp.logical_and(onward2, jnp.logical_and(back2 >= 0, flag(HAS2_TWO))))
+        def _():
+            two = product([left(b2)], [right(opposite[1, r])])
+            cube[r, back2] += product([l2], [right(two)])
+
+        back3 = jnp.logical_and(jnp.logical_not(pos3), npos3)
+
+        @pl.when(jnp.logical_and(back3, jnp.logical_and(slot(ZERO) >= 0, flag(HAS3_STEP))))
+        def _():
+            step = product([left(d3), left(b3)], [right(b3), right(d)])
+            cube[r, slot(ZERO)] += product([l3], [right(step)])
+
+
+def cube_kernel(meta, x, part, middle, mid_left, mid_right, mid_near, mid_across, mid_above, cube):
+    cube[...] = part[...]
     for r in range(2):
         flag, slot = row_view(meta, r)
         pos1, pos2, pos3 = flag(POS1), flag(POS2), flag(POS3)
-        npos1, npos2 = flag(NPOS1), flag(NPOS2)
-        d, a1, a2, a3 = (x[r, s] for s in range(4))
-        ld = left(d)
-        for m in range(SLOTS):
-            cube[r, m] = product([ld], [right(square[r, m])])
-
         step1 = jnp.where(pos1, slot(UP1), slot(DOWN1))
-        mutual1 = pos1 != npos1
-        other1 = jnp.where(mutual1, slot(ZERO), jnp.where(pos1, slot(TWO1), -1))
-        d1, b1 = first_neighbour(r, pos1, x, from_left, from_right)
+        step2 = jnp.where(pos2, slot(UP2), slot(DOWN2))
 
         @pl.when(jnp.logical_and(step1 >= 0, flag(HAS1_ZERO)))
         def _():
-            up = mid_local[1] if r == 0 else mid_right[0]
-            down = mid_left[0] if r == 0 else mid_local[0]
-            cube[r, step1] += product([left(a1)], [right(jnp.where(pos1, up, down))])
-
-        @pl.when(jnp.logical_and(other1 >= 0, flag(HAS1_STEP)))
-        def _():
-            beyond = jnp.where(mutual1, d, from_right[0] if r == 0 else right_next[0])
-            step = product([left(d1), left(b1)], [right(b1), right(beyond)])
-            cube[r, other1] += product([left(a1)], [right(step)])
-
-        near2 = flag(NEAR2)
-        step2 = jnp.where(pos2, slot(UP2), slot(DOWN2))
-        back2 = jnp.where(pos2, slot(DOWN2), slot(UP2))
-        mutual2 = pos2 != npos2
-        other2 = jnp.where(mutual2, slot(ZERO), slot(TWO2))
-        d2 = jnp.where(near2, near[0, r], across[0, r])
-        b2 = jnp.where(near2, near[1, r], across[1, r])
+            up = middle[1] if r == 0 else mid_right[0]
+            down = mid_left[0] if r == 0 else middle[0]
+            cube[r, step1] += product([left(x[r, 1])], [right(jnp.where(pos1, up, down))])
 
         @pl.when(jnp.logical_and(step2 >= 0, flag(HAS2_ZERO)))
         def _():
-            middle = jnp.where(near2, mid_near[r], mid_across[r])
-            cube[r, step2] += product([left(a2)], [right(middle)])
-
-        @pl.when(jnp.logical_and(other2 >= 0, flag(HAS2_STEP)))
-        def _():
-            beyond = jnp.where(mutual2, d, opposite[0, r])
-            step = product([left(d2), left(b2)], [right(b2), right(beyond)])
-            cube[r, other2] += product([left(a2)], [right(step)])
-
-        onward2 = jnp.logical_and(jnp.logical_not(mutual2), npos2 == flag(FPOS2))
-
-        @pl.when(jnp.logical_and(onward2, jnp.logical_and(back2 >= 0, flag(HAS2_TWO))))
-        def _():
-            two = product([left(b2)], [right(opposite[1, r])])
-            cube[r, back2] += product([left(a2)], [right(two)])
+            beside = jnp.where(flag(NEAR2), mid_near[r], mid_across[r])
+            cube[r, step2] += product([left(x[r, 2])], [right(beside)])
 
         @pl.when(jnp.logical_and(pos3, jnp.logical_and(slot(UP3) >= 0, flag(HAS3_ZERO))))
         def _():
-            cube[r, slot(UP3)] += product([left(a3)], [right(mid_above[r])])
-
-        back3 = jnp.logical_and(jnp.logical_not(pos3), flag(NPOS3))
-
-        @pl.when(jnp.logical_and(back3, jnp.logical_and(slot(ZERO) >= 0, flag(HAS3_STEP))))
-        def _():
-            b3 = below[r]
-            step = product([left(below_d[r]), left(b3)], [right(b3), right(d)])
-            cube[r, slot(ZERO)] += product([left(a3)], [right(step)])
+            cube[r, slot(UP3)] += product([left(x[r, 3])], [right(mid_above[r])])
 
 
 def call(kernel, out_shapes, *operands, smem=0, smem_out=False, flops=0):
@@ -289,15 +276,11 @@
 
     pair2 = jnp.stack([x[:, 0], x[:, 2]])
     pair3 = jnp.stack([x[:, 0], x[:, 3]])
-    above = to_row(pair3, -GY)
-    below = to_row(x[:, 3], GY)
+    relayed = along(pair3, "row", lambda i: i + 2 * GY * (2 * (i // GY % 2) - 1), row_count)
+    from_right = to_col(jnp.stack([x[0, 0], x[0, 1], x[1, 0]]), -1)
+    from_left = to_col(x[1, 0:2], 1)
     opposite = flip_row(pair2, 2)
     near = flip_row(pair2, 1)
-    from_left = to_col(x[1, 0:2], 1)
-    from_right = to_col(x[0, 0:2], -1)
-    across = flip_row(opposite, 1)
-    below_d = to_row(x[:, 0], GY)
-    right_next = to_col(x[1, 0:1], -1)
 
     place = jnp.stack([row, col]).astype(jnp.int32)
     meta = call(
@@ -310,48 +293,56 @@
         smem=4,
         smem_out=True,
     )
-    square, middle, middle0, middle1 = call(
-        square_kernel,
-        [block(2, SLOTS), block(2), block(1), block(1)],
+    own = meta[:, RELAY_OWN][None, :, None, None] != 0
+    third = flip_row(jnp.where(own, pair3, relayed), GY)
+    across = flip_row(opposite, 1)
+    middle, middle0, middle1 = call(
+        middle_kernel,
+        [block(2), block(1), block(1)],
         meta,
         x,
         from_left,
         from_right,
         near,
         across,
-        above,
-        below,
+        third,
         smem=1,
-        flops=60 * 2 * BS**3,
+        flops=24 * 2 * BS**3,
     )
     mid_above = to_row(middle, -GY)
     mid_left = to_col(middle1, 1)
     mid_right = to_col(middle0, -1)
     mid_across = flip_row(middle, 3)
     mid_near = flip_row(middle, 1)
+    square, part = call(
+        square_kernel,
+        [block(2, SLOTS), block(2, SLOTS)],
+        meta,
+        x,
+        middle,
+        from_left,
+        from_right,
+        near,
+        across,
+        opposite,
+        third,
+        smem=1,
+        flops=100 * 2 * BS**3,
+    )
     cube = call(
         cube_kernel,
         block(2, SLOTS),
         meta,
         x,
-        square,
-        from_left,
-        from_right,
-        right_next,
-        near,
-        across,
-        opposite,
-        above,
-        below,
-        below_d,
+        part,
+        middle,
         mid_left,
         mid_right,
-        middle,
         mid_near,
         mid_across,
         mid_above,
         smem=1,
-        flops=80 * 2 * BS**3,
+        flops=18 * 2 * BS**3,
     )
     return square, cube
 

time: 102 us -> 95.6 us (0.937)
  starting transfers between devices: 78.8 us -> 66.4 us
  waiting for transfers between devices: 9.17 us -> 15.6 us
    ppermute x14 -> x12, starting transfers between devices: 78.8 us -> 66.4 us  [along(): lax.ppermute(value, axis, [(i, target(i) % count) for i in range(count)])]
    ppermute x14 -> x12, waiting for transfers between devices: 9.17 us -> 15.6 us  [along(): lax.ppermute(value, axis, [(i, target(i) % count) for i in range(count)])]
    squeeze x3 -> x1, local copies, waits for them, and re-layouts: 1.11 us -> 0.01 us  [per_device(): from_left = to_col(x[1, 0:2], 1)]
    another operation x0 -> x2, local copies, waits for them, and re-layouts: none -> 1.08 us  [the longest x1 1.07 us: per_device(): pair3 = jnp.stack([x[:, 0], x[:, 3]])]
    pallas_call x3 -> x4, Pallas kernels: 9.25 us -> 9.98 us  [call(): pl.pallas_call(kernel, out_shape=out_shapes, in_specs=[pl.BlockSpec(memor...]
  transfers between devices with their start and end apart: 14 -> 12, of which waited for: 3 -> 3; matrix products, arithmetic and copies ran while one was open for 0% -> 0% of each run, Pallas kernels for 6% -> 7%
where the time goes in v2:
time: 95.6 us; the launch traced here: 95 us
  starting transfers between devices  66.4 us (69%)
  waiting for transfers between devices  15.6 us (16%)
  Pallas kernels  9.98 us (10%)
  local copies, waits for them, and re-layouts  1.72 us (2%)
    ppermute x12, starting transfers between devices, along(): lax.ppermute(value, axis, [(i, target(i) % count) for i in range(count)])  66.4 us
    ppermute x12, waiting for transfers between devices, along(): lax.ppermute(value, axis, [(i, target(i) % count) for i in range(count)])  15.6 us
    pallas_call x4, Pallas kernels, call(): pl.pallas_call(kernel, out_shape=out_shapes, in_specs=[pl.BlockSpec(memor...  9.98 us
  transfers between devices with their start and end apart: 12, of which 3 were waited for; matrix products, arithmetic and copies ran while one was open for 0% of the time, Pallas kernels for 7%

profile of v2, /device:TPU:1, one launch (start us, length us, event | category | flops | bytes accessed | tf_op | source)
XLA Modules:
  0.0 95.0 jit_solution(2812365163274319415)
XLA Ops:
  0.6 1.1 %slice_bitcast_fusion = (f32[1,2,128,128]{3,2,1,0:T(8,128)S(1)}, f32[1,2,128,128]{3,2,1,0:T(8,128)S(1)}, f32[1,2,128,128]{3,2,1,0:T(8,128)S(1)}) fusion(f32[2,4,128,128]{3,2,1,0:T(8,128)} %x.5), kind=kLoop, calls=%fused_computation.3 | loop fusion | bytes 786432 | tf_op jit(solution)/shard_map/stack;squeeze | solution.py:278
  1.7 0.0 copy-start.1
  1.7 0.0 copy-start.2
  1.8 5.2 %collective-permute-start.5 = (f32[2,2,128,128]{3,2,1,0:T(8,128)S(1)}, f32[2,2,128,128]{3,2,1,0:T(8,128)S(1)}, u32[]{:S(2)}, u32[]{:S(2)}) collective-permute-start(f32[2,2,128,128]{3,2,1,0:T(8,128)S(1)} %pad_maximum_fusion), channel_id=1, source_target_pairs={{0,576},{24,600},{48,624},{72,648},{96,288},{120,312},{144,336},{1... | collective-permute-start | bytes 786440 | tf_op jit(solution)/shard_map/ppermute | solution.py:264
  7.0 0.0 copy-start.3
  7.0 0.1 pad_add_fusion.place_ref
  7.1 0.6 copy-done.3
  7.7 3.0 %shard_map.59.meta = s32[2,24]{1,0:T(2,128)S(1)} custom-call(s32[2]{0:T(128)S(1)} %pad_add_fusion.place_ref, s32[4,1536]{1,0:T(4,128)S(1)} %bitcast.25, s32[6,1536]{1,0:T(8,128)S(1)} %bitcast.24, s32[1536]{0:T(1024)S(1)} %copy-done.3), custom_call_target="tpu_custom_call" | custom-call | bytes 2097152 | tf_op jit(solution)/shard_map/pallas_call | solution.py:249
  10.7 0.2 compare_reduce_fusion
  10.8 0.0 collective-permute-done.5
  10.8 0.0 copy-start
  10.9 0.1 broadcast_select_fusion
  11.0 5.2 %collective-permute-start.3 = (f32[2,2,128,128]{3,2,1,0:T(8,128)S(1)}, f32[2,2,128,128]{3,2,1,0:T(8,128)S(1)}, u32[]{:S(2)}, u32[]{:S(2)}) collective-permute-start(f32[2,2,128,128]{3,2,1,0:T(8,128)S(1)} %get-tuple-element.19), channel_id=1, source_target_pairs={{0,48},{24,72},{48,0},{72,24},{96,144},{120,168},{144,96},{168,120... | collective-permute-start | bytes 786440 | tf_op jit(solution)/shard_map/ppermute | solution.py:264
  16.2 16.3 %collective-permute-start.1 = (f32[3,128,128]{2,1,0:T(8,128)S(1)}, f32[3,128,128]{2,1,0:T(8,128)S(1)}, u32[]{:S(2)}, u32[]{:S(2)}) collective-permute-start(f32[3,128,128]{2,1,0:T(8,128)S(1)} %pad_maximum_fusion.2), channel_id=1, source_target_pairs={{0,23},{1,0},{2,1},{3,2},{4,3},{5,4},{6,5},{7,6},{8,7},{9,8},{10,9... | collective-permute-start | bytes 589832 | tf_op jit(solution)/shard_map/ppermute | solution.py:264
  32.5 4.0 %collective-permute-start.2 = (f32[2,2,128,128]{3,2,1,0:T(8,128)S(1)}, f32[2,2,128,128]{3,2,1,0:T(8,128)S(1)}, u32[]{:S(2)}, u32[]{:S(2)}) collective-permute-start(f32[2,2,128,128]{3,2,1,0:T(8,128)S(1)} %get-tuple-element.19), channel_id=1, source_target_pairs={{0,24},{24,0},{48,72},{72,48},{96,120},{120,96},{144,168},{168,144... | collective-permute-start | bytes 786440 | tf_op jit(solution)/shard_map/ppermute | solution.py:264
  36.5 4.9 %collective-permute-start.6 = (f32[2,2,128,128]{3,2,1,0:T(8,128)S(1)}, f32[2,2,128,128]{3,2,1,0:T(8,128)S(1)}, u32[]{:S(2)}, u32[]{:S(2)}) collective-permute-start(f32[2,2,128,128]{3,2,1,0:T(8,128)S(1)} %get-tuple-element.18), channel_id=1, source_target_pairs={{0,96},{24,120},{48,144},{72,168},{96,0},{120,24},{144,48},{168,72... | collective-permute-start | bytes 786440 | tf_op jit(solution)/shard_map/ppermute | solution.py:264
  41.5 0.0 collective-permute-done.3.opposite
  41.5 2.2 %collective-permute-start.4 = (f32[2,2,128,128]{3,2,1,0:T(8,128)S(1)}, f32[2,2,128,128]{3,2,1,0:T(8,128)S(1)}, u32[]{:S(2)}, u32[]{:S(2)}) collective-permute-start(f32[2,2,128,128]{3,2,1,0:T(8,128)S(1)} %collective-permute-done.3.opposite), channel_id=1, source_target_pairs={{0,24},{24,0},{48,72},{72,48},{96,120},{120,96},{144,168},{168,144... | collective-permute-start | bytes 786440 | tf_op jit(solution)/shard_map/ppermute | solution.py:264
  43.7 1.9 %collective-permute-start = (f32[2,128,128]{2,1,0:T(8,128)S(1)}, f32[2,128,128]{2,1,0:T(8,128)S(1)}, u32[]{:S(2)}, u32[]{:S(2)}) collective-permute-start(f32[2,128,128]{2,1,0:T(8,128)S(1)} %slice_bitcast_fusion.3), channel_id=1, source_target_pairs={{0,1},{1,2},{2,3},{3,4},{4,5},{5,6},{6,7},{7,8},{8,9},{9,10},{10,1... | collective-permute-start | bytes 393224 | tf_op jit(solution)/shard_map/ppermute | solution.py:264
  45.6 13.6 %collective-permute-done.from_left = f32[2,128,128]{2,1,0:T(8,128)S(1)} collective-permute-done((f32[2,128,128]{2,1,0:T(8,128)S(1)}, f32[2,128,128]{2,1,0:T(8,128)S(1)}, u32[]{:S(2)}, u32[]{:S(2)}) %collective-permute-start) | collective-permute-done | bytes 131104 | tf_op jit(solution)/shard_map/ppermute | solution.py:264
  59.2 0.0 collective-permute-done.1.from_right
  59.2 0.5 collective-permute-done.6.third
  59.8 0.9 shard_map.60
  60.7 9.0 %collective-permute-start.10 = (f32[2,128,128]{2,1,0:T(8,128)S(1)}, f32[2,128,128]{2,1,0:T(8,128)S(1)}, u32[]{:S(2)}, u32[]{:S(2)}) collective-permute-start(f32[2,128,128]{2,1,0:T(8,128)S(1)} %get-tuple-element.7.middle), channel_id=1, source_target_pairs={{0,72},{24,48},{48,24},{72,0},{96,168},{120,144},{144,120},{168,96... | collective-permute-start | bytes 393224 | tf_op jit(solution)/shard_map/ppermute | solution.py:264
  69.7 3.1 %collective-permute-start.11 = (f32[2,128,128]{2,1,0:T(8,128)S(1)}, f32[2,128,128]{2,1,0:T(8,128)S(1)}, u32[]{:S(2)}, u32[]{:S(2)}) collective-permute-start(f32[2,128,128]{2,1,0:T(8,128)S(1)} %get-tuple-element.7.middle), channel_id=1, source_target_pairs={{0,672},{24,696},{48,720},{72,744},{96,0},{120,24},{144,48},{168,7... | collective-permute-start | bytes 393224 | tf_op jit(solution)/shard_map/ppermute | solution.py:264
  72.7 3.3 %collective-permute-start.9 = (f32[2,128,128]{2,1,0:T(8,128)S(1)}, f32[2,128,128]{2,1,0:T(8,128)S(1)}, u32[]{:S(2)}, u32[]{:S(2)}) collective-permute-start(f32[2,128,128]{2,1,0:T(8,128)S(1)} %get-tuple-element.7.middle), channel_id=1, source_target_pairs={{0,24},{24,0},{48,72},{72,48},{96,120},{120,96},{144,168},{168,144... | collective-permute-start | bytes 393224 | tf_op jit(solution)/shard_map/ppermute | solution.py:264
  76.1 1.9 %collective-permute-start.7 = (f32[1,128,128]{2,1,0:T(8,128)S(1)}, f32[1,128,128]{2,1,0:T(8,128)S(1)}, u32[]{:S(2)}, u32[]{:S(2)}) collective-permute-start(f32[1,128,128]{2,1,0:T(8,128)S(1)} %get-tuple-element.10), channel_id=1, source_target_pairs={{0,1},{1,2},{2,3},{3,4},{4,5},{5,6},{6,7},{7,8},{8,9},{9,10},{10,1... | collective-permute-start | bytes 196616 | tf_op jit(solution)/shard_map/ppermute | solution.py:264
  78.0 9.4 %collective-permute-start.8 = (f32[1,128,128]{2,1,0:T(8,128)S(1)}, f32[1,128,128]{2,1,0:T(8,128)S(1)}, u32[]{:S(2)}, u32[]{:S(2)}) collective-permute-start(f32[1,128,128]{2,1,0:T(8,128)S(1)} %get-tuple-element.11), channel_id=1, source_target_pairs={{0,23},{1,0},{2,1},{3,2},{4,3},{5,4},{6,5},{7,6},{8,7},{9,8},{10,9... | collective-permute-start | bytes 196616 | tf_op jit(solution)/shard_map/ppermute | solution.py:264
  87.4 3.9 %shard_map.61 = (f32[2,6,128,128]{3,2,1,0:T(8,128)}, f32[2,6,128,128]{3,2,1,0:T(8,128)S(1)}) custom-call(s32[2,24]{1,0:T(2,128)S(1)} %shard_map.59.meta, f32[2,4,128,128]{3,2,1,0:T(8,128)S(1)} %copy-done, f32[2,128,128]{2,1,0:T(8,128)S(1)} %get-tuple-element.7.middle, f32[2,128,128]{2,1,0:T(8,128)S(1)} %collective-permute-done.from_left, ...), custom_call_target="tpu_custom_call" | custom-call | flops 419430400 | bytes 2097152 | tf_op jit(solution)/shard_map/pallas_call | solution.py:249
  91.3 0.0 collective-permute-done.7.mid_left
  91.3 1.5 %collective-permute-done.8.mid_right = f32[1,128,128]{2,1,0:T(8,128)S(1)} collective-permute-done((f32[1,128,128]{2,1,0:T(8,128)S(1)}, f32[1,128,128]{2,1,0:T(8,128)S(1)}, u32[]{:S(2)}, u32[]{:S(2)}) %collective-permute-start.8) | collective-permute-done | bytes 65568 | tf_op jit(solution)/shard_map/ppermute | solution.py:264
  92.8 2.2 %shard_map.62 = f32[2,6,128,128]{3,2,1,0:T(8,128)} custom-call(s32[2,24]{1,0:T(2,128)S(1)} %shard_map.59.meta, f32[2,4,128,128]{3,2,1,0:T(8,128)S(1)} %copy-done, f32[2,6,128,128]{3,2,1,0:T(8,128)S(1)} %get-tuple-element.9.part, f32[2,128,128]{2,1,0:T(8,128)S(1)} %get-tuple-element.7.middle, f32[1,128,128]{2,1,0:T(8,128)S(1)} %collective-permute-done.7.mid_left, ...), custom_call_target="tpu_custom_call" | custom-call | flops 75497472 | bytes 2097152 | tf_op jit(solution)/shard_map/pallas_call | solution.py:249
  (12 shorter events, 0.1 us)
Async XLA Ops:
  1.7 5.4 %copy-start.1 = (s32[1536,6]{0,1:T(8,128)S(1)}, s32[1536,6]{0,1:T(8,128)}, u32[]{:S(2)}) copy-start(s32[1536,6]{0,1:T(8,128)} %param.6) | copy-start | bytes 110596
  1.7 5.4 %copy-start.2 = (s32[1536,4]{0,1:T(4,128)S(1)}, s32[1536,4]{0,1:T(4,128)}, u32[]{:S(2)}) copy-start(s32[1536,4]{0,1:T(4,128)} %param.5) | copy-start | bytes 73732
  1.8 9.1 %collective-permute-start.5 = (f32[2,2,128,128]{3,2,1,0:T(8,128)S(1)}, f32[2,2,128,128]{3,2,1,0:T(8,128)S(1)}, u32[]{:S(2)}, u32[]{:S(2)}) collective-permute-start(f32[2,2,128,128]{3,2,1,0:T(8,128)S(1)} %pad_maximum_fusion), channel_id=1, source_target_pairs={{0,576},{24,600},{48,624},{72,648},{96,288},{120,312},{144,336},{1... | collective-permute-start | bytes 786440 | tf_op jit(solution)/shard_map/ppermute | solution.py:264
  7.0 0.7 copy-start.3
  10.8 5.3 %copy-start = (f32[2,4,128,128]{3,2,1,0:T(8,128)S(1)}, f32[2,4,128,128]{3,2,1,0:T(8,128)}, u32[]{:S(2)}) copy-start(f32[2,4,128,128]{3,2,1,0:T(8,128)} %x.5) | copy-start | bytes 1572868
  11.0 30.5 %collective-permute-start.3 = (f32[2,2,128,128]{3,2,1,0:T(8,128)S(1)}, f32[2,2,128,128]{3,2,1,0:T(8,128)S(1)}, u32[]{:S(2)}, u32[]{:S(2)}) collective-permute-start(f32[2,2,128,128]{3,2,1,0:T(8,128)S(1)} %get-tuple-element.19), channel_id=1, source_target_pairs={{0,48},{24,72},{48,0},{72,24},{96,144},{120,168},{144,96},{168,120... | collective-permute-start | bytes 786440 | tf_op jit(solution)/shard_map/ppermute | solution.py:264
  16.2 43.0 %collective-permute-start.1 = (f32[3,128,128]{2,1,0:T(8,128)S(1)}, f32[3,128,128]{2,1,0:T(8,128)S(1)}, u32[]{:S(2)}, u32[]{:S(2)}) collective-permute-start(f32[3,128,128]{2,1,0:T(8,128)S(1)} %pad_maximum_fusion.2), channel_id=1, source_target_pairs={{0,23},{1,0},{2,1},{3,2},{4,3},{5,4},{6,5},{7,6},{8,7},{9,8},{10,9... | collective-permute-start | bytes 589832 | tf_op jit(solution)/shard_map/ppermute | solution.py:264
  32.5 26.7 %collective-permute-start.2 = (f32[2,2,128,128]{3,2,1,0:T(8,128)S(1)}, f32[2,2,128,128]{3,2,1,0:T(8,128)S(1)}, u32[]{:S(2)}, u32[]{:S(2)}) collective-permute-start(f32[2,2,128,128]{3,2,1,0:T(8,128)S(1)} %get-tuple-element.19), channel_id=1, source_target_pairs={{0,24},{24,0},{48,72},{72,48},{96,120},{120,96},{144,168},{168,144... | collective-permute-start | bytes 786440 | tf_op jit(solution)/shard_map/ppermute | solution.py:264
  36.5 23.2 %collective-permute-start.6 = (f32[2,2,128,128]{3,2,1,0:T(8,128)S(1)}, f32[2,2,128,128]{3,2,1,0:T(8,128)S(1)}, u32[]{:S(2)}, u32[]{:S(2)}) collective-permute-start(f32[2,2,128,128]{3,2,1,0:T(8,128)S(1)} %get-tuple-element.18), channel_id=1, source_target_pairs={{0,96},{24,120},{48,144},{72,168},{96,0},{120,24},{144,48},{168,72... | collective-permute-start | bytes 786440 | tf_op jit(solution)/shard_map/ppermute | solution.py:264
  41.5 18.3 %collective-permute-start.4 = (f32[2,2,128,128]{3,2,1,0:T(8,128)S(1)}, f32[2,2,128,128]{3,2,1,0:T(8,128)S(1)}, u32[]{:S(2)}, u32[]{:S(2)}) collective-permute-start(f32[2,2,128,128]{3,2,1,0:T(8,128)S(1)} %collective-permute-done.3.opposite), channel_id=1, source_target_pairs={{0,24},{24,0},{48,72},{72,48},{96,120},{120,96},{144,168},{168,144... | collective-permute-start | bytes 786440 | tf_op jit(solution)/shard_map/ppermute | solution.py:264
  43.7 15.5 %collective-permute-start = (f32[2,128,128]{2,1,0:T(8,128)S(1)}, f32[2,128,128]{2,1,0:T(8,128)S(1)}, u32[]{:S(2)}, u32[]{:S(2)}) collective-permute-start(f32[2,128,128]{2,1,0:T(8,128)S(1)} %slice_bitcast_fusion.3), channel_id=1, source_target_pairs={{0,1},{1,2},{2,3},{3,4},{4,5},{5,6},{6,7},{7,8},{8,9},{9,10},{10,1... | collective-permute-start | bytes 393224 | tf_op jit(solution)/shard_map/ppermute | solution.py:264
  60.7 32.1 %collective-permute-start.10 = (f32[2,128,128]{2,1,0:T(8,128)S(1)}, f32[2,128,128]{2,1,0:T(8,128)S(1)}, u32[]{:S(2)}, u32[]{:S(2)}) collective-permute-start(f32[2,128,128]{2,1,0:T(8,128)S(1)} %get-tuple-element.7.middle), channel_id=1, source_target_pairs={{0,72},{24,48},{48,24},{72,0},{96,168},{120,144},{144,120},{168,96... | collective-permute-start | bytes 393224 | tf_op jit(solution)/shard_map/ppermute | solution.py:264
  69.7 23.1 %collective-permute-start.11 = (f32[2,128,128]{2,1,0:T(8,128)S(1)}, f32[2,128,128]{2,1,0:T(8,128)S(1)}, u32[]{:S(2)}, u32[]{:S(2)}) collective-permute-start(f32[2,128,128]{2,1,0:T(8,128)S(1)} %get-tuple-element.7.middle), channel_id=1, source_target_pairs={{0,672},{24,696},{48,720},{72,744},{96,0},{120,24},{144,48},{168,7... | collective-permute-start | bytes 393224 | tf_op jit(solution)/shard_map/ppermute | solution.py:264
  72.7 20.1 %collective-permute-start.9 = (f32[2,128,128]{2,1,0:T(8,128)S(1)}, f32[2,128,128]{2,1,0:T(8,128)S(1)}, u32[]{:S(2)}, u32[]{:S(2)}) collective-permute-start(f32[2,128,128]{2,1,0:T(8,128)S(1)} %get-tuple-element.7.middle), channel_id=1, source_target_pairs={{0,24},{24,0},{48,72},{72,48},{96,120},{120,96},{144,168},{168,144... | collective-permute-start | bytes 393224 | tf_op jit(solution)/shard_map/ppermute | solution.py:264
  76.1 15.2 %collective-permute-start.7 = (f32[1,128,128]{2,1,0:T(8,128)S(1)}, f32[1,128,128]{2,1,0:T(8,128)S(1)}, u32[]{:S(2)}, u32[]{:S(2)}) collective-permute-start(f32[1,128,128]{2,1,0:T(8,128)S(1)} %get-tuple-element.10), channel_id=1, source_target_pairs={{0,1},{1,2},{2,3},{3,4},{4,5},{5,6},{6,7},{7,8},{8,9},{9,10},{10,1... | collective-permute-start | bytes 196616 | tf_op jit(solution)/shard_map/ppermute | solution.py:264
  78.0 14.8 %collective-permute-start.8 = (f32[1,128,128]{2,1,0:T(8,128)S(1)}, f32[1,128,128]{2,1,0:T(8,128)S(1)}, u32[]{:S(2)}, u32[]{:S(2)}) collective-permute-start(f32[1,128,128]{2,1,0:T(8,128)S(1)} %get-tuple-element.11), channel_id=1, source_target_pairs={{0,23},{1,0},{2,1},{3,2},{4,3},{5,4},{6,5},{7,6},{8,7},{9,8},{10,9... | collective-permute-start | bytes 196616 | tf_op jit(solution)/shard_map/ppermute | solution.py:264

commit v3 on v1

v3 whole, which is shorter than its diff:
```python
import jax
import jax.numpy as jnp
from jax import lax
from jax.experimental import pallas as pl
from jax.experimental.pallas import tpu as pltpu
from jax.sharding import PartitionSpec as P

GX, GY, GZ = 48, 4, 8
BS = 128
SLOTS = 6
FIRST_FLOPS = 10**10
RING = 8

ZERO, UP1, DOWN1, TWO1, UP2, DOWN2, TWO2, UP3 = range(8)
OFFSETS = ((0, 0, 0), (1, 0, 0), (-1, 0, 0), (2, 0, 0), (0, 1, 0), (0, -1, 0), (0, 2, 0), (0, 0, 1))

POS1, POS2, POS3, NPOS1, NPOS2, NPOS3, FPOS2, NEAR2 = range(8)
SLOT_OF = 8
HAS1_ZERO, HAS1_STEP, HAS2_ZERO, HAS2_STEP, HAS2_TWO, HAS3_ZERO, HAS3_STEP = range(16, 23)
FIX_LEFT, FIX_RIGHT, OTHER = 23, 24, 25
META = 26


def wrap(value, size):
    value = jnp.where(value >= size, value - size, value)
    return jnp.where(value < 0, value + size, value)


def structure_kernel(place_ref, xcol_ref, mcol_ref, count_ref, out_ref):
    row, col = place_ref[0], place_ref[1]
    second, third = lax.rem(row, GY), lax.div(row, GY)

    def column(a, b, c):
        return wrap(a, GX) + GX * (wrap(b, GY) + GY * wrap(c, GZ))

    def holds(place, target):
        found = jnp.int32(0)
        count = count_ref[place]
        for m in range(SLOTS):
            hit = jnp.logical_and(count > m, mcol_ref[m, place] == target)
            found = found + hit.astype(jnp.int32)
        return found

    for r in range(2):
        first = 2 * col + r
        me = column(first, second, third)
        pos1 = xcol_ref[1, me] == column(first + 1, second, third)
        pos2 = xcol_ref[2, me] == column(first, second + 1, third)
        pos3 = xcol_ref[3, me] == column(first, second, third + 1)
        s1, s2, s3 = (jnp.where(p, 1, -1) for p in (pos1, pos2, pos3))
        f1, f2, f3 = wrap(first + s1, GX), wrap(second + s2, GY), wrap(third + s3, GZ)
        c1, c2, c3 = column(f1, second, third), column(first, f2, third), column(first, second, f3)
        far2 = column(first, f2 + s2, third)
        npos1 = xcol_ref[1, c1] == column(f1 + 1, second, third)
        npos2 = xcol_ref[2, c2] == column(first, f2 + 1, third)
        npos3 = xcol_ref[3, c3] == column(first, second, f3 + 1)
        fpos2 = xcol_ref[2, far2] == column(first, f2 + s2 + 1 - jnp.where(f2 + s2 >= GY, GY, 0), third)
        even = lax.rem(second, 2) == 0
        for place, flag in (
            (POS1, pos1),
            (POS2, pos2),
            (POS3, pos3),
            (NPOS1, npos1),
            (NPOS2, npos2),
            (NPOS3, npos3),
            (FPOS2, fpos2),
            (NEAR2, pos2 == even),
        ):
            out_ref[r, place] = flag.astype(jnp.int32)
        count = count_ref[me]
        for k, (a, b, c) in enumerate(OFFSETS):
            target = column(first + a, second + b, third + c)
            slot = jnp.int32(-1)
            for m in range(SLOTS):
                hit = jnp.logical_and(count > m, mcol_ref[m, me] == target)
                slot = jnp.where(hit, m, slot)
            out_ref[r, SLOT_OF + k] = slot
        n1, n2 = jnp.where(npos1, 1, -1), jnp.where(npos2, 1, -1)
        out_ref[r, HAS1_ZERO] = holds(c1, c1)
        out_ref[r, HAS1_STEP] = holds(c1, column(f1 + n1, second, third))
        out_ref[r, HAS2_ZERO] = holds(c2, c2)
        out_ref[r, HAS2_STEP] = holds(c2, column(first, f2 + n2, third))
        out_ref[r, HAS2_TWO] = holds(c2, column(first, f2 + 2, third))
        out_ref[r, HAS3_ZERO] = holds(c3, c3)
        out_ref[r, HAS3_STEP] = holds(c3, column(first, second, f3 + 1))
        out_ref[r, OTHER] = 1 - lax.rem(row, 2)
        out_ref[r, FIX_LEFT] = (lax.rem(col, RING) == 0).astype(jnp.int32)
        out_ref[r, FIX_RIGHT] = (lax.rem(col, RING) == RING - 1).astype(jnp.int32)


def halves(value):
    high = value.astype(jnp.bfloat16)
    low = (value - high.astype(jnp.float32)).astype(jnp.bfloat16)
    return high, low


def left(value):
    high, low = halves(value)
    return jnp.concatenate([high, low, high], axis=1)


def right(value):
    high, low = halves(value)
    return jnp.concatenate([high, high, low], axis=0)


def product(lefts, rights):
    a = lefts[0] if len(lefts) == 1 else jnp.concatenate(lefts, axis=1)
    b = rights[0] if len(rights) == 1 else jnp.concatenate(rights, axis=0)
    return jnp.dot(a, b, preferred_element_type=jnp.float32)


def row_view(meta, r):
    flag = lambda k: meta[r, k] != 0
    slot = lambda k: meta[r, SLOT_OF + k]
    return flag, slot


def from_side(flag, fix, ring, wraps, k):
    return jnp.where(flag(fix), wraps[k // 2][k % 2], ring[k])


def first_neighbour(r, flag, x, ring_left, ring_right, wraps):
    blocks = []
    for k in range(2):
        up = x[1, k] if r == 0 else from_side(flag, FIX_RIGHT, ring_right, wraps, k)
        down = from_side(flag, FIX_LEFT, ring_left, wraps, k) if r == 0 else x[0, k]
        blocks.append(jnp.where(flag(POS1), up, down))
    return blocks


def second_neighbour(meta, r, flag, near, across):
    other = meta[0, OTHER]
    return [jnp.where(flag(NEAR2), near[other, k, r], across[k, r]) for k in range(2)]


def base_kernel(
    meta, x, near, across, above, below, base, sides, third, to_left, to_right, to_wrap
):
    to_left[0:2] = x[0, 0:2]
    to_left[3] = x[1, 0]
    to_right[0:2] = x[1, 0:2]
    to_wrap[1] = x[1, 0]
    inside = jnp.logical_and(meta[0, POS1] != 0, meta[1, POS1] == 0)
    for r in range(2):
        flag, _ = row_view(meta, r)
        d, a1, a2, a3 = (x[r, s] for s in range(4))
        d2, b2 = second_neighbour(meta, r, flag, near, across)
        b3 = jnp.where(flag(POS3), above[r], below[r])
        third[r] = b3
        rights = [right(x[1 - r, 1]), right(b2), right(b3)]
        mutual = [inside] + [flag(POS1 + k) != flag(NPOS1 + k) for k in (1, 2)]
        none = jnp.zeros_like(rights[0])
        ld, l2 = left(d), left(a2)
        sides[0, r] = product([ld, l2], [right(a2), right(d2)])
        sides[1, r] = product([l2], [rights[1]])
        value = product(
            [ld, left(a1), l2, left(a3)],
            [right(d)] + [jnp.where(m, b, none) for m, b in zip(mutual, rights)],
        )
        base[r] = value
        (to_left if r == 0 else to_right)[2] = value
        if r == 0:
            to_wrap[0] = value
        else:

            @pl.when(flag(FIX_RIGHT))
            def _():
                to_wrap[0] = value


def early_kernel(meta, x, sides, square, cube):
    square[...] = jnp.zeros_like(square)
    cube[...] = jnp.zeros_like(cube)
    for r in range(2):
        flag, slot = row_view(meta, r)
        ld = left(x[r, 0])
        step2 = jnp.where(flag(POS2), slot(UP2), slot(DOWN2))
        twice2 = jnp.where(flag(POS2) == flag(NPOS2), slot(TWO2), -1)
        for k, where in enumerate((step2, twice2)):

            @pl.when(where >= 0)
            def _():
                square[r, where] = sides[k, r]
                cube[r, where] = product([ld], [right(sides[k, r])])


def copy_kernel(given, taken):
    taken[...] = given[...]


def meeting(flag, r):
    away = flag(POS1) if r == 1 else jnp.logical_not(flag(POS1))
    return away, jnp.logical_and(away, flag(POS1) != flag(NPOS1))


def side_block(flag, r, ring_left, ring_right, wraps, k):
    fix, ring = (FIX_LEFT, ring_left) if r == 0 else (FIX_RIGHT, ring_right)
    return from_side(flag, fix, ring, wraps, k)


def middle_kernel(meta, x, base, sides, ring_left, ring_right, wrap_a, middle, beside, upward):
    beside[1:3] = sides[...]
    for r in range(2):
        flag, _ = row_view(meta, r)
        _, met = meeting(flag, r)
        b1 = side_block(flag, r, ring_left, ring_right, (wrap_a,), 1)
        added = product([left(x[r, 1])], [right(b1)])
        whole = base[r] + jnp.where(met, added, jnp.zeros_like(added))
        middle[r] = whole
        beside[0, r] = whole
        upward[0, r] = whole
        upward[1, r] = x[r, 0]


def late_kernel(
    meta,
    x,
    early,
    early_part,
    middle,
    ring_left,
    ring_right,
    wrap_a,
    third,
    below_d,
    square,
    cube,
):
    wraps = (wrap_a,)
    square[...] = early[...]
    cube[...] = early_part[...]
    for r in range(2):
        flag, slot = row_view(meta, r)
        pos1, pos3, npos1 = flag(POS1), flag(POS3), flag(NPOS1)
        d, a1 = x[r, 0], x[r, 1]
        d1, b1 = first_neighbour(r, flag, x, ring_left, ring_right, wraps)
        ld, l1, r1 = left(d), left(a1), right(b1)

        def put(where, value):
            square[r, where] = value
            cube[r, where] += product([ld], [right(value)])

        step1 = jnp.where(pos1, slot(UP1), slot(DOWN1))

        @pl.when(slot(ZERO) >= 0)
        def _():
            put(slot(ZERO), middle[r])

        @pl.when(step1 >= 0)
        def _():
            put(step1, product([ld, l1], [right(a1), right(d1)]))

        @pl.when(jnp.logical_and(slot(TWO1) >= 0, jnp.logical_and(pos1, npos1)))
        def _():
            put(slot(TWO1), product([l1], [r1]))

        back3 = jnp.logical_and(jnp.logical_not(pos3), flag(NPOS3))

        @pl.when(jnp.logical_and(back3, jnp.logical_and(slot(ZERO) >= 0, flag(HAS3_STEP))))
        def _():
            b3 = third[r]
            step = product([left(below_d[r]), left(b3)], [right(b3), right(d)])
            cube[r, slot(ZERO)] += product([left(x[r, 3])], [right(step)])


def cube_kernel(
    meta,
    x,
    late,
    late_part,
    middle,
    ring_left,
    ring_right,
    wrap_a,
    wrap_b,
    mid_near,
    mid_across,
    mid_above,
    square,
    cube,
):
    wraps = (wrap_a, wrap_b)
    square[...] = late[...]
    cube[...] = late_part[...]
    for r in range(2):
        flag, slot = row_view(meta, r)
        pos1, npos1 = flag(POS1), flag(NPOS1)
        d, a1 = x[r, 0], x[r, 1]
        d1, b1 = first_neighbour(r, flag, x, ring_left, ring_right, wraps)
        l1, r1 = left(a1), right(b1)
        step1 = jnp.where(pos1, slot(UP1), slot(DOWN1))
        step2 = jnp.where(flag(POS2), slot(UP2), slot(DOWN2))
        mutual1 = pos1 != npos1
        other1 = jnp.where(mutual1, slot(ZERO), jnp.where(pos1, slot(TWO1), -1))

        @pl.when(jnp.logical_and(step1 >= 0, flag(HAS1_ZERO)))
        def _():
            away, met = meeting(flag, r)
            back = product([left(b1)], [right(a1)])
            outer = side_block(flag, r, ring_left, ring_right, wraps, 2)
            outer += jnp.where(met, back, jnp.zeros_like(back))
            cube[r, step1] += product([l1], [right(jnp.where(away, outer, middle[1 - r]))])

        @pl.when(jnp.logical_and(other1 >= 0, flag(HAS1_STEP)))
        def _():
            far = from_side(flag, FIX_RIGHT, ring_right, wraps, 3 * r)
            beyond = jnp.where(mutual1, d, far)
            step = product([left(d1), left(b1)], [r1, right(beyond)])
            cube[r, other1] += product([l1], [right(step)])

        pos2, npos2 = flag(POS2), flag(NPOS2)
        back2 = jnp.where(pos2, slot(DOWN2), slot(UP2))
        mutual2 = pos2 != npos2
        other2 = jnp.where(mutual2, slot(ZERO), slot(TWO2))
        onward2 = jnp.where(npos2 == flag(FPOS2), jnp.where(mutual2, -1, back2), -1)
        l2 = left(x[r, 2])
        for k, where, has in (
            (0, step2, HAS2_ZERO),
            (1, other2, HAS2_STEP),
            (2, onward2, HAS2_TWO),
        ):

            @pl.when(jnp.logical_and(where >= 0, flag(has)))
            def _():
                value = jnp.where(flag(NEAR2), mid_near[meta[0, OTHER], k, r], mid_across[k, r])
                cube[r, where] += product([l2], [right(value)])

        @pl.when(jnp.logical_and(slot(UP3) >= 0, flag(POS3)))
        def _():
            a3 = x[r, 3]
            ld, l3 = left(d), left(a3)
            value = product([ld, l3], [right(a3), right(mid_above[1, r])])
            square[r, slot(UP3)] = value
            centre = right(mid_above[0, r])
            centre = jnp.where(flag(HAS3_ZERO), centre, jnp.zeros_like(centre))
            cube[r, slot(UP3)] += product([ld, l3], [right(value), centre])


def call(kernel, out_shapes, *operands, smem=0, free=0, smem_out=False, flops=0):
    held = len(operands) - smem - free
    spaces = [pltpu.SMEM] * smem + [pltpu.VMEM] * held + [pl.ANY] * free
    out_space = pltpu.SMEM if smem_out else pltpu.VMEM
    return pl.pallas_call(
        kernel,
        out_shape=out_shapes,
        in_specs=[pl.BlockSpec(memory_space=s) for s in spaces],
        out_specs=jax.tree.map(lambda _: pl.BlockSpec(memory_space=out_space), out_shapes),
        compiler_params=pltpu.CompilerParams(vmem_limit_bytes=32 * 2**20),
        cost_estimate=pl.CostEstimate(flops=flops, bytes_accessed=2**21, transcendentals=0),
    )(*operands)


def per_device(x, x_cols, mask_cols, mask_count):
    row_count, col_count = lax.axis_size("row"), lax.axis_size("col")
    row, col = lax.axis_index("row"), lax.axis_index("col")

    def along(value, axis, target, count):
        return lax.ppermute(value, axis, [(i, target(i) % count) for i in range(count)])

    def anywhere(value, target):
        pairs = []
        for i in range(row_count * col_count):
            there = target(i // col_count, i % col_count)
            if there is not None:
                pairs.append((i, there[0] * col_count + there[1] % col_count))
        return lax.ppermute(value, ("row", "col"), pairs)

    def to_col(value, step):
        def target(i, j):
            return (i, j + step) if j // RING == (j + step) // RING else None

        return anywhere(value, target)

    def to_wrap(value):
        return anywhere(value, lambda i, j: {0: (i, j - 1), RING - 1: (i, j + 1)}.get(j % RING))

    def to_row(value, step):
        return along(value, "row", lambda i: i + step, row_count)

    def flip_row(value, bits):
        return along(value, "row", lambda i: i ^ bits, row_count)

    def both_cores(value):
        groups = [[i, i + 1] for i in range(0, row_count, 2)]
        return lax.all_gather(value, "row", axis_index_groups=groups)

    block = lambda *lead: jax.ShapeDtypeStruct(lead + (BS, BS), jnp.float32)

    place = jnp.stack([row, col]).astype(jnp.int32)
    pair2 = jnp.stack([x[:, 0], x[:, 2]])
    above = to_row(x[:, 3], -GY)
    below = to_row(x[:, 3], GY)
    below_d = to_row(x[:, 0], GY)
    across = flip_row(pair2, 3)
    edge = lax.dynamic_index_in_dim(x, (lax.rem(col, RING) == RING - 1).astype(jnp.int32), 0, False)
    wrap_a = call(copy_kernel, block(2), to_wrap(edge[0:2]), flops=FIRST_FLOPS)
    near = both_cores(pair2)

    meta = call(
        structure_kernel,
        jax.ShapeDtypeStruct((2, META), jnp.int32),
        *(place, x_cols.T, mask_cols.T, mask_count),
        smem=4,
        smem_out=True,
    )
    base, sides, third, left_message, right_message, wrap_message = call(
        base_kernel,
        [block(2), block(2, 2), block(2), block(4), block(3), block(2)],
        *(meta, x, near, across, above, below),
        smem=1,
        flops=24 * 2 * BS**3,
    )
    ring_right = to_col(left_message, -1)
    ring_left = to_col(right_message, 1)
    wrap_b = call(copy_kernel, block(2), to_wrap(wrap_message), flops=FIRST_FLOPS)
    early, early_part = call(
        early_kernel,
        [block(2, SLOTS), block(2, SLOTS)],
        *(meta, x, sides),
        smem=1,
        flops=12 * 2 * BS**3,
    )
    middle, beside, upward = call(
        middle_kernel,
        [block(2), block(3, 2), block(2, 2)],
        *(meta, x, base, sides, ring_left, ring_right, wrap_a),
        smem=1,
        flops=6 * 2 * BS**3,
    )
    mid_above = to_row(upward, -GY)
    mid_across = flip_row(beside, 3)
    mid_near = both_cores(beside)
    late, late_part = call(
        late_kernel,
        [block(2, SLOTS), block(2, SLOTS)],
        *(meta, x, early, early_part, middle, ring_left, ring_right, wrap_a, third, below_d),
        smem=1,
        flops=50 * 2 * BS**3,
    )
    return call(
        cube_kernel,
        [block(2, SLOTS), block(2, SLOTS)],
        *(meta, x, late, late_part, middle, ring_left, ring_right, wrap_a, wrap_b),
        *(mid_near, mid_across, mid_above),
        smem=1,
        flops=50 * 2 * BS**3,
    )


def solution(mesh):
    in_specs = (P(("row", "col"), None, None, None), P(), P(), P())
    out_specs = (P(("row", "col"), None, None, None), P(("row", "col"), None, None, None))
    return jax.shard_map(
        per_device, mesh=mesh, in_specs=in_specs, out_specs=out_specs, check_vma=False
    )
```

time: 102 us -> 82.6 us (0.81)
  starting transfers between devices: 78.8 us -> 58.6 us
  blocking collectives: 0 us -> 4.63 us
  waiting for transfers between devices: 9.17 us -> 6.36 us
  local copies, waits for them, and re-layouts: 2.26 us -> 1.17 us
  Pallas kernels: 9.25 us -> 10.3 us
    ppermute x14 -> x6, starting transfers between devices: 78.8 us -> 36.1 us  [along(): lax.ppermute(value, axis, [(i, target(i) % count) for i in range(count)])]
    ppermute x0 -> x4, starting transfers between devices: none -> 22.5 us  [anywhere(): return lax.ppermute(value, ('row', 'col'), pairs)]
    all_gather x0 -> x2, blocking collectives: none -> 4.63 us  [both_cores(): return lax.all_gather(value, 'row', axis_index_groups=groups)]
    ppermute x14 -> x6, waiting for transfers between devices: 9.17 us -> 5.66 us  [along(): lax.ppermute(value, axis, [(i, target(i) % count) for i in range(count)])]
    unnamed x10 -> x8, local copies, waits for them, and re-layouts: 1.15 us -> 0.02 us
    pallas_call x3 -> x8, Pallas kernels: 9.25 us -> 10.3 us  [call(): pl.pallas_call(kernel, out_shape=out_shapes, in_specs=[pl.BlockSpec(memor...]
  transfers between devices with their start and end apart: 14 -> 10, of which waited for: 3 -> 4; matrix products, arithmetic and copies ran while one was open for 0% -> 0% of each run, Pallas kernels for 6% -> 9%
where the time goes in v3:
time: 82.6 us; the launch traced here: 82.1 us
  starting transfers between devices  58.6 us (71%)
  Pallas kernels  10.3 us (12%)
  waiting for transfers between devices  6.36 us (8%)
  blocking collectives  4.63 us (6%)
  local copies, waits for them, and re-layouts  1.17 us (1%)
  between operations  0.88 us (1%)
    ppermute x6, starting transfers between devices, along(): lax.ppermute(value, axis, [(i, target(i) % count) for i in range(count)])  36.1 us
    ppermute x4, starting transfers between devices, anywhere(): return lax.ppermute(value, ('row', 'col'), pairs)  22.5 us
    pallas_call x8, Pallas kernels, call(): pl.pallas_call(kernel, out_shape=out_shapes, in_specs=[pl.BlockSpec(memor...  10.3 us
    ppermute x6, waiting for transfers between devices, along(): lax.ppermute(value, axis, [(i, target(i) % count) for i in range(count)])  5.66 us
    all_gather x2, blocking collectives, both_cores(): return lax.all_gather(value, 'row', axis_index_groups=groups)  4.63 us
  transfers between devices with their start and end apart: 10, of which 4 were waited for; matrix products, arithmetic and copies ran while one was open for 0% of the time, Pallas kernels for 9%

profile of v3, /device:TPU:1, one launch (start us, length us, event | category | flops | bytes accessed | tf_op | source)
XLA Modules:
  0.0 82.1 jit_solution(15364723247308328418)
XLA Ops:
  0.6 1.1 %slice_bitcast_fusion.3 = (f32[2,128,128]{2,1,0:T(8,128)S(1)}, f32[1,2,128,128]{3,2,1,0:T(8,128)S(1)}, f32[1,2,128,128]{3,2,1,0:T(8,128)S(1)}, f32[2,128,128]{2,1,0:T(8,128)S(1)}) fusion(f32[2,4,128,128]{3,2,1,0:T(8,128)} %x.9), kind=kLoop, calls=%fused_computation.5 | loop fusion | bytes 917504 | tf_op jit(solution)/shard_map/squeeze | solution.py:394
  1.8 8.8 %collective-permute-start.1 = (f32[2,128,128]{2,1,0:T(8,128)S(1)}, f32[2,128,128]{2,1,0:T(8,128)S(1)}, u32[]{:S(2)}, u32[]{:S(2)}) collective-permute-start(f32[2,128,128]{2,1,0:T(8,128)S(1)} %get-tuple-element.31), channel_id=1, source_target_pairs={{0,672},{24,696},{48,720},{72,744},{96,0},{120,24},{144,48},{168,7... | collective-permute-start | bytes 393224 | tf_op jit(solution)/shard_map/ppermute | solution.py:359
  10.6 1.9 %collective-permute-start.2 = (f32[2,128,128]{2,1,0:T(8,128)S(1)}, f32[2,128,128]{2,1,0:T(8,128)S(1)}, u32[]{:S(2)}, u32[]{:S(2)}) collective-permute-start(f32[2,128,128]{2,1,0:T(8,128)S(1)} %get-tuple-element.31), channel_id=1, source_target_pairs={{0,96},{24,120},{48,144},{72,168},{96,192},{120,216},{144,240},{16... | collective-permute-start | bytes 393224 | tf_op jit(solution)/shard_map/ppermute | solution.py:359
  12.6 4.8 %collective-permute-start = (f32[2,2,128,128]{3,2,1,0:T(8,128)S(1)}, f32[2,2,128,128]{3,2,1,0:T(8,128)S(1)}, u32[]{:S(2)}, u32[]{:S(2)}) collective-permute-start(f32[2,2,128,128]{3,2,1,0:T(8,128)S(1)} %pad_maximum_fusion), channel_id=1, source_target_pairs={{0,72},{24,48},{48,24},{72,0},{96,168},{120,144},{144,120},{168,96... | collective-permute-start | bytes 786440 | tf_op jit(solution)/shard_map/ppermute | solution.py:359
  17.4 0.0 copy-start.1
  17.5 0.0 copy-start.2
  17.5 14.5 %collective-permute-start.5 = (f32[2,128,128]{2,1,0:T(8,128)S(1)}, f32[2,128,128]{2,1,0:T(8,128)S(1)}, u32[]{:S(2)}, u32[]{:S(2)}) collective-permute-start(f32[2,128,128]{2,1,0:T(8,128)S(1)} %dynamic-slice_bitcast_fusion), channel_id=1, source_target_pairs={{0,23},{7,8},{8,7},{15,16},{16,15},{23,0},{24,47},{31,32},{32,31},... | collective-permute-start | bytes 393224 | tf_op jit(solution)/shard_map/ppermute | solution.py:367
  32.0 0.0 copy-start.3
  32.0 3.2 %collective-permute-start.6 = (f32[2,128,128]{2,1,0:T(8,128)S(1)}, f32[2,128,128]{2,1,0:T(8,128)S(1)}, u32[]{:S(2)}, u32[]{:S(2)}) collective-permute-start(f32[2,128,128]{2,1,0:T(8,128)S(1)} %get-tuple-element.28), channel_id=1, source_target_pairs={{0,96},{24,120},{48,144},{72,168},{96,192},{120,216},{144,240},{16... | collective-permute-start | bytes 393224 | tf_op jit(solution)/shard_map/ppermute | solution.py:359
  35.3 0.1 pad_add_fusion.place_ref
  35.3 2.9 %shard_map.59.meta = s32[2,26]{1,0:T(2,128)S(1)} custom-call(s32[2]{0:T(128)S(1)} %pad_add_fusion.place_ref, s32[4,1536]{1,0:T(4,128)S(1)} %bitcast.26, s32[6,1536]{1,0:T(8,128)S(1)} %bitcast.25, s32[1536]{0:T(1024)S(1)} %copy-done.3), custom_call_target="tpu_custom_call" | custom-call | bytes 2097152 | tf_op jit(solution)/shard_map/pallas_call | solution.py:344
  38.3 2.2 %all-gather = f32[4,2,128,128]{3,2,1,0:T(8,128)S(1)} all-gather(f32[2,2,128,128]{3,2,1,0:T(8,128)S(1)} %pad_maximum_fusion), channel_id=2, replica_groups={{0,24},{48,72},{96,120},{144,168},{192,216},{240,264},{288,312},{336,36..., dimensions={0}, use_global_device_ids=true | all-gather | bytes 786432 | tf_op jit(solution)/shard_map/all_gather | solution.py:386
  40.5 0.0 collective-permute-done.1.above
  40.5 0.0 collective-permute-done.2.below
  40.5 0.0 collective-permute-done.across
  40.5 1.1 %shard_map.60 = (f32[2,128,128]{2,1,0:T(8,128)S(1)}, f32[2,2,128,128]{3,2,1,0:T(8,128)S(1)}, f32[2,128,128]{2,1,0:T(8,128)S(1)}, f32[4,128,128]{2,1,0:T(8,128)S(...) custom-call(s32[2,26]{1,0:T(2,128)S(1)} %shard_map.59.meta, f32[2,4,128,128]{3,2,1,0:T(8,128)S(1)} %copy-done, ...), custom_call_target="tpu_custom_call" | custom-call | flops 100663296 | bytes 2097152 | tf_op jit(solution)/shard_map/pallas_call | solution.py:344
  41.6 1.3 %collective-permute-start.4 = (f32[4,128,128]{2,1,0:T(8,128)S(1)}, f32[4,128,128]{2,1,0:T(8,128)S(1)}, u32[]{:S(2)}, u32[]{:S(2)}) collective-permute-start(f32[4,128,128]{2,1,0:T(8,128)S(1)} %get-tuple-element.20), channel_id=1, source_target_pairs={{1,0},{2,1},{3,2},{4,3},{5,4},{6,5},{7,6},{9,8},{10,9},{11,10},{12... | collective-permute-start | bytes 786440 | tf_op jit(solution)/shard_map/ppermute | solution.py:367
  42.9 4.0 %collective-permute-start.3 = (f32[3,128,128]{2,1,0:T(8,128)S(1)}, f32[3,128,128]{2,1,0:T(8,128)S(1)}, u32[]{:S(2)}, u32[]{:S(2)}) collective-permute-start(f32[3,128,128]{2,1,0:T(8,128)S(1)} %get-tuple-element.19), channel_id=1, source_target_pairs={{0,1},{1,2},{2,3},{3,4},{4,5},{5,6},{6,7},{8,9},{9,10},{10,11},{11... | collective-permute-start | bytes 589832 | tf_op jit(solution)/shard_map/ppermute | solution.py:367
  46.9 2.8 %collective-permute-start.7 = (f32[2,128,128]{2,1,0:T(8,128)S(1)}, f32[2,128,128]{2,1,0:T(8,128)S(1)}, u32[]{:S(2)}, u32[]{:S(2)}) collective-permute-start(f32[2,128,128]{2,1,0:T(8,128)S(1)} %get-tuple-element.25), channel_id=1, source_target_pairs={{0,23},{7,8},{8,7},{15,16},{16,15},{23,0},{24,47},{31,32},{32,31},... | collective-permute-start | bytes 393224 | tf_op jit(solution)/shard_map/ppermute | solution.py:367
  49.7 0.8 %shard_map.61 = (f32[2,6,128,128]{3,2,1,0:T(8,128)S(1)}, f32[2,6,128,128]{3,2,1,0:T(8,128)S(1)}) custom-call(s32[2,26]{1,0:T(2,128)S(1)} %shard_map.59.meta, f32[2,4,128,128]{3,2,1,0:T(8,128)S(1)} %copy-done, f32[2,2,128,128]{3,2,1,0:T(8,128)S(1)} %get-tuple-element.15.sides), custom_call_target="tpu_custom_call" | custom-call | flops 50331648 | bytes 2097152 | tf_op jit(solution)/shard_map/pallas_call | solution.py:344
  50.5 0.2 collective-permute-done.3.ring_left
  50.7 0.5 collective-permute-done.4.ring_right
  51.2 0.8 shard_map.63
  52.0 3.1 %collective-permute-start.8 = (f32[3,2,128,128]{3,2,1,0:T(8,128)S(1)}, f32[3,2,128,128]{3,2,1,0:T(8,128)S(1)}, u32[]{:S(2)}, u32[]{:S(2)}) collective-permute-start(f32[3,2,128,128]{3,2,1,0:T(8,128)S(1)} %get-tuple-element.26), channel_id=1, source_target_pairs={{0,72},{24,48},{48,24},{72,0},{96,168},{120,144},{144,120},{168,96... | collective-permute-start | bytes 1179656 | tf_op jit(solution)/shard_map/ppermute | solution.py:359
  55.1 14.2 %collective-permute-start.9 = (f32[2,2,128,128]{3,2,1,0:T(8,128)S(1)}, f32[2,2,128,128]{3,2,1,0:T(8,128)S(1)}, u32[]{:S(2)}, u32[]{:S(2)}) collective-permute-start(f32[2,2,128,128]{3,2,1,0:T(8,128)S(1)} %get-tuple-element.27), channel_id=1, source_target_pairs={{0,672},{24,696},{48,720},{72,744},{96,0},{120,24},{144,48},{168,7... | collective-permute-start | bytes 786440 | tf_op jit(solution)/shard_map/ppermute | solution.py:359
  69.3 0.0 collective-permute-done.7.given
  69.3 0.0 collective-permute-done.6.below_d
  69.3 1.8 %shard_map.64 = (f32[2,6,128,128]{3,2,1,0:T(8,128)S(1)}, f32[2,6,128,128]{3,2,1,0:T(8,128)S(1)}) custom-call(s32[2,26]{1,0:T(2,128)S(1)} %shard_map.59.meta, f32[2,4,128,128]{3,2,1,0:T(8,128)S(1)} %copy-done, f32[2,6,128,128]{3,2,1,0:T(8,128)S(1)} %get-tuple-element.16.early, f32[2,6,128,128]{3,2,1,0:T(8,128)S(1)} %get-tuple-element.17.early_part, ...), custom_call_target="tpu_custom_call" | custom-call | flops 209715200 | bytes 2097152 | tf_op jit(solution)/shard_map/pallas_call | solution.py:344
  71.1 2.5 %all-gather.1 = f32[6,2,128,128]{3,2,1,0:T(8,128)S(1)} all-gather(f32[3,2,128,128]{3,2,1,0:T(8,128)S(1)} %get-tuple-element.26), channel_id=3, replica_groups={{0,24},{48,72},{96,120},{144,168},{192,216},{240,264},{288,312},{336,36..., dimensions={0}, use_global_device_ids=true | all-gather | bytes 1179648 | tf_op jit(solution)/shard_map/all_gather | solution.py:386
  73.6 2.0 %collective-permute-done.9.mid_above = f32[2,2,128,128]{3,2,1,0:T(8,128)S(1)} collective-permute-done((f32[2,2,128,128]{3,2,1,0:T(8,128)S(1)}, f32[2,2,128,128]{3,2,1,0:T(8,128)S(1)}, u32[]{:S(2)}, u32[]{:S(2)}) %collective-permute-start.9) | collective-permute-done | bytes 262176 | tf_op jit(solution)/shard_map/ppermute | solution.py:359
  75.5 3.7 %collective-permute-done.8.mid_across = f32[3,2,128,128]{3,2,1,0:T(8,128)S(1)} collective-permute-done((f32[3,2,128,128]{3,2,1,0:T(8,128)S(1)}, f32[3,2,128,128]{3,2,1,0:T(8,128)S(1)}, u32[]{:S(2)}, u32[]{:S(2)}) %collective-permute-start.8) | collective-permute-done | bytes 393248 | tf_op jit(solution)/shard_map/ppermute | solution.py:359
  79.2 2.9 %shard_map.66 = (f32[2,6,128,128]{3,2,1,0:T(8,128)}, f32[2,6,128,128]{3,2,1,0:T(8,128)}) custom-call(s32[2,26]{1,0:T(2,128)S(1)} %shard_map.59.meta, f32[2,4,128,128]{3,2,1,0:T(8,128)S(1)} %copy-done, f32[2,6,128,128]{3,2,1,0:T(8,128)S(1)} %get-tuple-element.23.late, f32[2,6,128,128]{3,2,1,0:T(8,128)S(1)} %get-tuple-element.24.late_part, ...), custom_call_target="tpu_custom_call" | custom-call | flops 209715200 | bytes 2097152 | tf_op jit(solution)/shard_map/pallas_call | solution.py:344
  (10 shorter events, 0.1 us)
Async XLA Ops:
  0.6 16.8 %copy-start = (f32[2,4,128,128]{3,2,1,0:T(8,128)S(1)}, f32[2,4,128,128]{3,2,1,0:T(8,128)}, u32[]{:S(2)}) copy-start(f32[2,4,128,128]{3,2,1,0:T(8,128)} %x.9) | copy-start | bytes 1572868
  1.8 38.7 %collective-permute-start.1 = (f32[2,128,128]{2,1,0:T(8,128)S(1)}, f32[2,128,128]{2,1,0:T(8,128)S(1)}, u32[]{:S(2)}, u32[]{:S(2)}) collective-permute-start(f32[2,128,128]{2,1,0:T(8,128)S(1)} %get-tuple-element.31), channel_id=1, source_target_pairs={{0,672},{24,696},{48,720},{72,744},{96,0},{120,24},{144,48},{168,7... | collective-permute-start | bytes 393224 | tf_op jit(solution)/shard_map/ppermute | solution.py:359
  10.6 29.9 %collective-permute-start.2 = (f32[2,128,128]{2,1,0:T(8,128)S(1)}, f32[2,128,128]{2,1,0:T(8,128)S(1)}, u32[]{:S(2)}, u32[]{:S(2)}) collective-permute-start(f32[2,128,128]{2,1,0:T(8,128)S(1)} %get-tuple-element.31), channel_id=1, source_target_pairs={{0,96},{24,120},{48,144},{72,168},{96,192},{120,216},{144,240},{16... | collective-permute-start | bytes 393224 | tf_op jit(solution)/shard_map/ppermute | solution.py:359
  12.6 27.9 %collective-permute-start = (f32[2,2,128,128]{3,2,1,0:T(8,128)S(1)}, f32[2,2,128,128]{3,2,1,0:T(8,128)S(1)}, u32[]{:S(2)}, u32[]{:S(2)}) collective-permute-start(f32[2,2,128,128]{3,2,1,0:T(8,128)S(1)} %pad_maximum_fusion), channel_id=1, source_target_pairs={{0,72},{24,48},{48,24},{72,0},{96,168},{120,144},{144,120},{168,96... | collective-permute-start | bytes 786440 | tf_op jit(solution)/shard_map/ppermute | solution.py:359
  17.4 17.9 %copy-start.1 = (s32[1536,6]{0,1:T(8,128)S(1)}, s32[1536,6]{0,1:T(8,128)}, u32[]{:S(2)}) copy-start(s32[1536,6]{0,1:T(8,128)} %param.6) | copy-start | bytes 110596
  17.5 17.9 %copy-start.2 = (s32[1536,4]{0,1:T(4,128)S(1)}, s32[1536,4]{0,1:T(4,128)}, u32[]{:S(2)}) copy-start(s32[1536,4]{0,1:T(4,128)} %param.5) | copy-start | bytes 73732
  17.5 32.2 %collective-permute-start.5 = (f32[2,128,128]{2,1,0:T(8,128)S(1)}, f32[2,128,128]{2,1,0:T(8,128)S(1)}, u32[]{:S(2)}, u32[]{:S(2)}) collective-permute-start(f32[2,128,128]{2,1,0:T(8,128)S(1)} %dynamic-slice_bitcast_fusion), channel_id=1, source_target_pairs={{0,23},{7,8},{8,7},{15,16},{16,15},{23,0},{24,47},{31,32},{32,31},... | collective-permute-start | bytes 393224 | tf_op jit(solution)/shard_map/ppermute | solution.py:367
  32.0 3.4 %copy-start.3 = (s32[1536]{0:T(1024)S(1)}, s32[1536]{0:T(1024)}, u32[]{:S(2)}) copy-start(s32[1536]{0:T(1024)} %count_ref.1) | copy-start | bytes 18436
  32.0 37.3 %collective-permute-start.6 = (f32[2,128,128]{2,1,0:T(8,128)S(1)}, f32[2,128,128]{2,1,0:T(8,128)S(1)}, u32[]{:S(2)}, u32[]{:S(2)}) collective-permute-start(f32[2,128,128]{2,1,0:T(8,128)S(1)} %get-tuple-element.28), channel_id=1, source_target_pairs={{0,96},{24,120},{48,144},{72,168},{96,192},{120,216},{144,240},{16... | collective-permute-start | bytes 393224 | tf_op jit(solution)/shard_map/ppermute | solution.py:359
  41.6 9.7 %collective-permute-start.4 = (f32[4,128,128]{2,1,0:T(8,128)S(1)}, f32[4,128,128]{2,1,0:T(8,128)S(1)}, u32[]{:S(2)}, u32[]{:S(2)}) collective-permute-start(f32[4,128,128]{2,1,0:T(8,128)S(1)} %get-tuple-element.20), channel_id=1, source_target_pairs={{1,0},{2,1},{3,2},{4,3},{5,4},{6,5},{7,6},{9,8},{10,9},{11,10},{12... | collective-permute-start | bytes 786440 | tf_op jit(solution)/shard_map/ppermute | solution.py:367
  42.9 7.8 %collective-permute-start.3 = (f32[3,128,128]{2,1,0:T(8,128)S(1)}, f32[3,128,128]{2,1,0:T(8,128)S(1)}, u32[]{:S(2)}, u32[]{:S(2)}) collective-permute-start(f32[3,128,128]{2,1,0:T(8,128)S(1)} %get-tuple-element.19), channel_id=1, source_target_pairs={{0,1},{1,2},{2,3},{3,4},{4,5},{5,6},{6,7},{8,9},{9,10},{10,11},{11... | collective-permute-start | bytes 589832 | tf_op jit(solution)/shard_map/ppermute | solution.py:367
  46.9 22.4 %collective-permute-start.7 = (f32[2,128,128]{2,1,0:T(8,128)S(1)}, f32[2,128,128]{2,1,0:T(8,128)S(1)}, u32[]{:S(2)}, u32[]{:S(2)}) collective-permute-start(f32[2,128,128]{2,1,0:T(8,128)S(1)} %get-tuple-element.25), channel_id=1, source_target_pairs={{0,23},{7,8},{8,7},{15,16},{16,15},{23,0},{24,47},{31,32},{32,31},... | collective-permute-start | bytes 393224 | tf_op jit(solution)/shard_map/ppermute | solution.py:367
  52.0 27.2 %collective-permute-start.8 = (f32[3,2,128,128]{3,2,1,0:T(8,128)S(1)}, f32[3,2,128,128]{3,2,1,0:T(8,128)S(1)}, u32[]{:S(2)}, u32[]{:S(2)}) collective-permute-start(f32[3,2,128,128]{3,2,1,0:T(8,128)S(1)} %get-tuple-element.26), channel_id=1, source_target_pairs={{0,72},{24,48},{48,24},{72,0},{96,168},{120,144},{144,120},{168,96... | collective-permute-start | bytes 1179656 | tf_op jit(solution)/shard_map/ppermute | solution.py:359
  55.1 20.4 %collective-permute-start.9 = (f32[2,2,128,128]{3,2,1,0:T(8,128)S(1)}, f32[2,2,128,128]{3,2,1,0:T(8,128)S(1)}, u32[]{:S(2)}, u32[]{:S(2)}) collective-permute-start(f32[2,2,128,128]{3,2,1,0:T(8,128)S(1)} %get-tuple-element.27), channel_id=1, source_target_pairs={{0,672},{24,696},{48,720},{72,744},{96,0},{120,24},{144,48},{168,7... | collective-permute-start | bytes 786440 | tf_op jit(solution)/shard_map/ppermute | solution.py:359

commit v4 on v3

--- a/solution.py
+++ b/solution.py
@@ -8,7 +8,7 @@
 GX, GY, GZ = 48, 4, 8
 BS = 128
 SLOTS = 6
-FIRST_FLOPS = 10**10
+FIRST_FLOPS = 24 * 10**8
 RING = 8
 
 ZERO, UP1, DOWN1, TWO1, UP2, DOWN2, TWO2, UP3 = range(8)
@@ -17,8 +17,8 @@
 POS1, POS2, POS3, NPOS1, NPOS2, NPOS3, FPOS2, NEAR2 = range(8)
 SLOT_OF = 8
 HAS1_ZERO, HAS1_STEP, HAS2_ZERO, HAS2_STEP, HAS2_TWO, HAS3_ZERO, HAS3_STEP = range(16, 23)
-FIX_LEFT, FIX_RIGHT, OTHER = 23, 24, 25
-META = 26
+FIX_LEFT, FIX_RIGHT, OTHER, RELAY_OWN = 23, 24, 25, 26
+META = 27
 
 
 def wrap(value, size):
@@ -84,6 +84,10 @@
         out_ref[r, HAS3_ZERO] = holds(c3, c3)
         out_ref[r, HAS3_STEP] = holds(c3, column(first, second, f3 + 1))
         out_ref[r, OTHER] = 1 - lax.rem(row, 2)
+        odd = lax.rem(third, 2)
+        partner = third + 1 - 2 * odd
+        wants_up = xcol_ref[3, column(first, second, partner)] == column(first, second, partner + 1)
+        out_ref[r, RELAY_OWN] = (wants_up == (odd == 1)).astype(jnp.int32)
         out_ref[r, FIX_LEFT] = (lax.rem(col, RING) == 0).astype(jnp.int32)
         out_ref[r, FIX_RIGHT] = (lax.rem(col, RING) == RING - 1).astype(jnp.int32)
 
@@ -117,7 +121,8 @@
 
 
 def from_side(flag, fix, ring, wraps, k):
-    return jnp.where(flag(fix), wraps[k // 2][k % 2], ring[k])
+    wrap, place = ((0, 0), (0, 1), (1, 0), (0, 2))[k]
+    return jnp.where(flag(fix), wraps[wrap][place], ring[k])
 
 
 def first_neighbour(r, flag, x, ring_left, ring_right, wraps):
@@ -131,31 +136,36 @@
 
 def second_neighbour(meta, r, flag, near, across):
     other = meta[0, OTHER]
-    return [jnp.where(flag(NEAR2), near[other, k, r], across[k, r]) for k in range(2)]
+    return [jnp.where(flag(NEAR2), near[other, k, r], across[other, k, r]) for k in range(2)]
+
+
+def edge_kernel(place, x, arrived, edge):
+    del arrived
+    last = lax.rem(place[1], RING) == RING - 1
+    for k in range(2):
+        edge[k] = jnp.where(last, x[1, k], x[0, k])
+    edge[2] = x[1, 0]
 
 
 def base_kernel(
-    meta, x, near, across, above, below, base, sides, third, to_left, to_right, to_wrap
+    meta, x, near, across, above, below, relayed, base, third, to_left, to_right, to_wrap, handed
 ):
     to_left[0:2] = x[0, 0:2]
     to_left[3] = x[1, 0]
     to_right[0:2] = x[1, 0:2]
-    to_wrap[1] = x[1, 0]
     inside = jnp.logical_and(meta[0, POS1] != 0, meta[1, POS1] == 0)
     for r in range(2):
         flag, _ = row_view(meta, r)
         d, a1, a2, a3 = (x[r, s] for s in range(4))
-        d2, b2 = second_neighbour(meta, r, flag, near, across)
+        _, b2 = second_neighbour(meta, r, flag, near, across)
         b3 = jnp.where(flag(POS3), above[r], below[r])
+        handed[r] = jnp.where(flag(RELAY_OWN), d, relayed[r])
         third[r] = b3
         rights = [right(x[1 - r, 1]), right(b2), right(b3)]
         mutual = [inside] + [flag(POS1 + k) != flag(NPOS1 + k) for k in (1, 2)]
         none = jnp.zeros_like(rights[0])
-        ld, l2 = left(d), left(a2)
-        sides[0, r] = product([ld, l2], [right(a2), right(d2)])
-        sides[1, r] = product([l2], [rights[1]])
         value = product(
-            [ld, left(a1), l2, left(a3)],
+            [left(d), left(a1), left(a2), left(a3)],
             [right(d)] + [jnp.where(m, b, none) for m, b in zip(mutual, rights)],
         )
         base[r] = value
@@ -169,20 +179,49 @@
                 to_wrap[0] = value
 
 
-def early_kernel(meta, x, sides, square, cube):
+def early_kernel(
+    meta, x, near, across, opposite, to_wrap, handed, square, cube, wrap_message, third_message
+):
+    wrap_message[...] = to_wrap[...]
+    third_message[...] = handed[...]
     square[...] = jnp.zeros_like(square)
     cube[...] = jnp.zeros_like(cube)
     for r in range(2):
         flag, slot = row_view(meta, r)
-        ld = left(x[r, 0])
-        step2 = jnp.where(flag(POS2), slot(UP2), slot(DOWN2))
-        twice2 = jnp.where(flag(POS2) == flag(NPOS2), slot(TWO2), -1)
-        for k, where in enumerate((step2, twice2)):
-
-            @pl.when(where >= 0)
-            def _():
-                square[r, where] = sides[k, r]
-                cube[r, where] = product([ld], [right(sides[k, r])])
+        pos2, npos2 = flag(POS2), flag(NPOS2)
+        d, a2 = x[r, 0], x[r, 2]
+        d2, b2 = second_neighbour(meta, r, flag, near, across)
+        ld, l2, r2 = left(d), left(a2), right(b2)
+
+        def put(where, value):
+            square[r, where] = value
+            cube[r, where] += product([ld], [right(value)])
+
+        step2 = jnp.where(pos2, slot(UP2), slot(DOWN2))
+        back2 = jnp.where(pos2, slot(DOWN2), slot(UP2))
+        mutual2 = pos2 != npos2
+        other2 = jnp.where(mutual2, slot(ZERO), slot(TWO2))
+
+        @pl.when(step2 >= 0)
+        def _():
+            put(step2, product([ld, l2], [right(a2), right(d2)]))
+
+        @pl.when(jnp.logical_and(slot(TWO2) >= 0, jnp.logical_not(mutual2)))
+        def _():
+            put(slot(TWO2), product([l2], [r2]))
+
+        @pl.when(jnp.logical_and(other2 >= 0, flag(HAS2_STEP)))
+        def _():
+            beyond = jnp.where(mutual2, d, opposite[0, r])
+            step = product([left(d2), left(b2)], [r2, right(beyond)])
+            cube[r, other2] += product([l2], [right(step)])
+
+        onward2 = jnp.logical_and(jnp.logical_not(mutual2), npos2 == flag(FPOS2))
+
+        @pl.when(jnp.logical_and(onward2, jnp.logical_and(back2 >= 0, flag(HAS2_TWO))))
+        def _():
+            two = product([left(b2)], [right(opposite[1, r])])
+            cube[r, back2] += product([l2], [right(two)])
 
 
 def copy_kernel(given, taken):
@@ -199,18 +238,13 @@
     return from_side(flag, fix, ring, wraps, k)
 
 
-def middle_kernel(meta, x, base, sides, ring_left, ring_right, wrap_a, middle, beside, upward):
-    beside[1:3] = sides[...]
+def middle_kernel(meta, x, base, ring_left, ring_right, wrap_a, middle):
     for r in range(2):
         flag, _ = row_view(meta, r)
         _, met = meeting(flag, r)
         b1 = side_block(flag, r, ring_left, ring_right, (wrap_a,), 1)
         added = product([left(x[r, 1])], [right(b1)])
-        whole = base[r] + jnp.where(met, added, jnp.zeros_like(added))
-        middle[r] = whole
-        beside[0, r] = whole
-        upward[0, r] = whole
-        upward[1, r] = x[r, 0]
+        middle[r] = base[r] + jnp.where(met, added, jnp.zeros_like(added))
 
 
 def late_kernel(
@@ -222,12 +256,13 @@
     ring_left,
     ring_right,
     wrap_a,
+    wrap_b,
     third,
-    below_d,
+    third_d,
     square,
     cube,
 ):
-    wraps = (wrap_a,)
+    wraps = (wrap_a, wrap_b)
     square[...] = early[...]
     cube[...] = early_part[...]
     for r in range(2):
@@ -255,42 +290,6 @@
         def _():
             put(slot(TWO1), product([l1], [r1]))
 
-        back3 = jnp.logical_and(jnp.logical_not(pos3), flag(NPOS3))
-
-        @pl.when(jnp.logical_and(back3, jnp.logical_and(slot(ZERO) >= 0, flag(HAS3_STEP))))
-        def _():
-            b3 = third[r]
-            step = product([left(below_d[r]), left(b3)], [right(b3), right(d)])
-            cube[r, slot(ZERO)] += product([left(x[r, 3])], [right(step)])
-
-
-def cube_kernel(
-    meta,
-    x,
-    late,
-    late_part,
-    middle,
-    ring_left,
-    ring_right,
-    wrap_a,
-    wrap_b,
-    mid_near,
-    mid_across,
-    mid_above,
-    square,
-    cube,
-):
-    wraps = (wrap_a, wrap_b)
-    square[...] = late[...]
-    cube[...] = late_part[...]
-    for r in range(2):
-        flag, slot = row_view(meta, r)
-        pos1, npos1 = flag(POS1), flag(NPOS1)
-        d, a1 = x[r, 0], x[r, 1]
-        d1, b1 = first_neighbour(r, flag, x, ring_left, ring_right, wraps)
-        l1, r1 = left(a1), right(b1)
-        step1 = jnp.where(pos1, slot(UP1), slot(DOWN1))
-        step2 = jnp.where(flag(POS2), slot(UP2), slot(DOWN2))
         mutual1 = pos1 != npos1
         other1 = jnp.where(mutual1, slot(ZERO), jnp.where(pos1, slot(TWO1), -1))
 
@@ -309,32 +308,36 @@
             step = product([left(d1), left(b1)], [r1, right(beyond)])
             cube[r, other1] += product([l1], [right(step)])
 
-        pos2, npos2 = flag(POS2), flag(NPOS2)
-        back2 = jnp.where(pos2, slot(DOWN2), slot(UP2))
-        mutual2 = pos2 != npos2
-        other2 = jnp.where(mutual2, slot(ZERO), slot(TWO2))
-        onward2 = jnp.where(npos2 == flag(FPOS2), jnp.where(mutual2, -1, back2), -1)
-        l2 = left(x[r, 2])
-        for k, where, has in (
-            (0, step2, HAS2_ZERO),
-            (1, other2, HAS2_STEP),
-            (2, onward2, HAS2_TWO),
-        ):
-
-            @pl.when(jnp.logical_and(where >= 0, flag(has)))
-            def _():
-                value = jnp.where(flag(NEAR2), mid_near[meta[0, OTHER], k, r], mid_across[k, r])
-                cube[r, where] += product([l2], [right(value)])
-
-        @pl.when(jnp.logical_and(slot(UP3) >= 0, flag(POS3)))
+        back3 = jnp.logical_and(jnp.logical_not(pos3), flag(NPOS3))
+
+        @pl.when(jnp.logical_and(back3, jnp.logical_and(slot(ZERO) >= 0, flag(HAS3_STEP))))
+        def _():
+            b3 = third[r]
+            step = product([left(third_d[r]), left(b3)], [right(b3), right(d)])
+            cube[r, slot(ZERO)] += product([left(x[r, 3])], [right(step)])
+
+        @pl.when(jnp.logical_and(slot(UP3) >= 0, pos3))
         def _():
             a3 = x[r, 3]
-            ld, l3 = left(d), left(a3)
-            value = product([ld, l3], [right(a3), right(mid_above[1, r])])
-            square[r, slot(UP3)] = value
-            centre = right(mid_above[0, r])
-            centre = jnp.where(flag(HAS3_ZERO), centre, jnp.zeros_like(centre))
-            cube[r, slot(UP3)] += product([ld, l3], [right(value), centre])
+            put(slot(UP3), product([ld, left(a3)], [right(a3), right(third_d[r])]))
+
+
+def cube_kernel(meta, x, part, mid_near, mid_across, mid_above, cube):
+    cube[...] = part[...]
+    for r in range(2):
+        flag, slot = row_view(meta, r)
+        step2 = jnp.where(flag(POS2), slot(UP2), slot(DOWN2))
+
+        @pl.when(jnp.logical_and(step2 >= 0, flag(HAS2_ZERO)))
+        def _():
+            value = jnp.where(flag(NEAR2), mid_near[meta[0, OTHER], r], mid_across[r])
+            cube[r, step2] += product([left(x[r, 2])], [right(value)])
+
+        ahead = jnp.logical_and(flag(POS3), flag(HAS3_ZERO))
+
+        @pl.when(jnp.logical_and(ahead, slot(UP3) >= 0))
+        def _():
+            cube[r, slot(UP3)] += product([left(x[r, 3])], [right(mid_above[r])])
 
 
 def call(kernel, out_shapes, *operands, smem=0, free=0, smem_out=False, flops=0):
@@ -389,13 +392,14 @@
 
     place = jnp.stack([row, col]).astype(jnp.int32)
     pair2 = jnp.stack([x[:, 0], x[:, 2]])
+    opposite = flip_row(pair2, 2)
     above = to_row(x[:, 3], -GY)
     below = to_row(x[:, 3], GY)
-    below_d = to_row(x[:, 0], GY)
-    across = flip_row(pair2, 3)
-    edge = lax.dynamic_index_in_dim(x, (lax.rem(col, RING) == RING - 1).astype(jnp.int32), 0, False)
-    wrap_a = call(copy_kernel, block(2), to_wrap(edge[0:2]), flops=FIRST_FLOPS)
+    edge = call(edge_kernel, block(3), place, x, opposite, smem=1, free=1)
+    wrap_a = call(copy_kernel, block(3), to_wrap(edge), flops=FIRST_FLOPS)
+    relayed = along(x[:, 0], "row", lambda i: i + 2 * GY * (2 * (i // GY % 2) - 1), row_count)
     near = both_cores(pair2)
+    across = both_cores(opposite)
 
     meta = call(
         structure_kernel,
@@ -404,48 +408,50 @@
         smem=4,
         smem_out=True,
     )
-    base, sides, third, left_message, right_message, wrap_message = call(
+    base, third, left_message, right_message, wrap_message, handed = call(
         base_kernel,
-        [block(2), block(2, 2), block(2), block(4), block(3), block(2)],
-        *(meta, x, near, across, above, below),
+        [block(2), block(2), block(4), block(3), block(1), block(2)],
+        *(meta, x, near, across, above, below, relayed),
         smem=1,
         flops=24 * 2 * BS**3,
     )
     ring_right = to_col(left_message, -1)
     ring_left = to_col(right_message, 1)
-    wrap_b = call(copy_kernel, block(2), to_wrap(wrap_message), flops=FIRST_FLOPS)
-    early, early_part = call(
+    early, early_part, wrap_message, handed = call(
         early_kernel,
+        [block(2, SLOTS), block(2, SLOTS), block(1), block(2)],
+        *(meta, x, near, across, opposite, wrap_message, handed),
+        smem=1,
+        flops=60 * 2 * BS**3,
+    )
+    wrap_b = to_wrap(wrap_message)
+    third_d = flip_row(handed, GY)
+    middle = call(
+        middle_kernel,
+        block(2),
+        *(meta, x, base, ring_left, ring_right, wrap_a),
+        smem=1,
+        flops=6 * 2 * BS**3,
+    )
+    mid_above = to_row(middle, -GY)
+    mid_across = flip_row(middle, 3)
+    mid_near = both_cores(middle)
+    square, part = call(
+        late_kernel,
         [block(2, SLOTS), block(2, SLOTS)],
-        *(meta, x, sides),
+        *(meta, x, early, early_part, middle, ring_left, ring_right),
+        *(wrap_a, wrap_b, third, third_d),
+        smem=1,
+        flops=60 * 2 * BS**3,
+    )
+    cube = call(
+        cube_kernel,
+        block(2, SLOTS),
+        *(meta, x, part, mid_near, mid_across, mid_above),
         smem=1,
         flops=12 * 2 * BS**3,
     )
-    middle, beside, upward = call(
-        middle_kernel,
-        [block(2), block(3, 2), block(2, 2)],
-        *(meta, x, base, sides, ring_left, ring_right, wrap_a),
-        smem=1,
-        flops=6 * 2 * BS**3,
-    )
-    mid_above = to_row(upward, -GY)
-    mid_across = flip_row(beside, 3)
-    mid_near = both_cores(beside)
-    late, late_part = call(
-        late_kernel,
-        [block(2, SLOTS), block(2, SLOTS)],
-        *(meta, x, early, early_part, middle, ring_left, ring_right, wrap_a, third, below_d),
-        smem=1,
-        flops=50 * 2 * BS**3,
-    )
-    return call(
-        cube_kernel,
-        [block(2, SLOTS), block(2, SLOTS)],
-        *(meta, x, late, late_part, middle, ring_left, ring_right, wrap_a, wrap_b),
-        *(mid_near, mid_across, mid_above),
-        smem=1,
-        flops=50 * 2 * BS**3,
-    )
+    return square, cube
 
 
 def solution(mesh):

time: 82.6 us -> 79.1 us (0.958)
  the two profiles are of different devices: /device:TPU:1 before, /device:TPU:71 now
where the time goes in v4:
time: 79.1 us; the launch traced here: 78.6 us
  starting transfers between devices  45.3 us (57%)
  blocking collectives  17.5 us (22%)
  Pallas kernels  12.6 us (16%)
  local copies, waits for them, and re-layouts  1.15 us (1%)
  waiting for transfers between devices  1.11 us (1%)
  between operations  0.86 us (1%)
    ppermute x4, starting transfers between devices, anywhere(): return lax.ppermute(value, ('row', 'col'), pairs)  23.2 us
    ppermute x7, starting transfers between devices, along(): lax.ppermute(value, axis, [(i, target(i) % count) for i in range(count)])  22 us
    all_gather x3, blocking collectives, both_cores(): return lax.all_gather(value, 'row', axis_index_groups=groups)  17.5 us
    pallas_call x8, Pallas kernels, call(): pl.pallas_call(kernel, out_shape=out_shapes, in_specs=[pl.BlockSpec(memor...  12.6 us
  transfers between devices with their start and end apart: 11, of which 1 were waited for; matrix products, arithmetic and copies ran while one was open for 0% of the time, Pallas kernels for 14%

profile of v4, /device:TPU:71, one launch (start us, length us, event | category | flops | bytes accessed | tf_op | source)
XLA Modules:
  0.0 78.6 jit_solution(2935216119088285624)
XLA Ops:
  0.6 1.1 %slice_bitcast_fusion.3 = (f32[2,128,128]{2,1,0:T(8,128)S(1)}, f32[1,2,128,128]{3,2,1,0:T(8,128)S(1)}, f32[1,2,128,128]{3,2,1,0:T(8,128)S(1)}, f32[2,128,128]{2,1,0:T(8,128)S(1)}) fusion(f32[2,4,128,128]{3,2,1,0:T(8,128)} %x.11), kind=kLoop, calls=%fused_computation.4 | loop fusion | bytes 917504 | tf_op jit(solution)/shard_map/squeeze | solution.py:400
  1.8 1.9 %collective-permute-start = (f32[2,2,128,128]{3,2,1,0:T(8,128)S(1)}, f32[2,2,128,128]{3,2,1,0:T(8,128)S(1)}, u32[]{:S(2)}, u32[]{:S(2)}) collective-permute-start(f32[2,2,128,128]{3,2,1,0:T(8,128)S(1)} %pad_maximum_fusion), channel_id=1, source_target_pairs={{0,48},{24,72},{48,0},{72,24},{96,144},{120,168},{144,96},{168,120... | collective-permute-start | bytes 786440 | tf_op jit(solution)/shard_map/ppermute | solution.py:362
  3.7 5.8 %collective-permute-start.2 = (f32[2,128,128]{2,1,0:T(8,128)S(1)}, f32[2,128,128]{2,1,0:T(8,128)S(1)}, u32[]{:S(2)}, u32[]{:S(2)}) collective-permute-start(f32[2,128,128]{2,1,0:T(8,128)S(1)} %get-tuple-element.29), channel_id=1, source_target_pairs={{0,96},{24,120},{48,144},{72,168},{96,192},{120,216},{144,240},{16... | collective-permute-start | bytes 393224 | tf_op jit(solution)/shard_map/ppermute | solution.py:362
  9.5 2.2 %collective-permute-start.1 = (f32[2,128,128]{2,1,0:T(8,128)S(1)}, f32[2,128,128]{2,1,0:T(8,128)S(1)}, u32[]{:S(2)}, u32[]{:S(2)}) collective-permute-start(f32[2,128,128]{2,1,0:T(8,128)S(1)} %get-tuple-element.29), channel_id=1, source_target_pairs={{0,672},{24,696},{48,720},{72,744},{96,0},{120,24},{144,48},{168,7... | collective-permute-start | bytes 393224 | tf_op jit(solution)/shard_map/ppermute | solution.py:362
  11.7 2.2 %collective-permute-start.3 = (f32[2,128,128]{2,1,0:T(8,128)S(1)}, f32[2,128,128]{2,1,0:T(8,128)S(1)}, u32[]{:S(2)}, u32[]{:S(2)}) collective-permute-start(f32[2,128,128]{2,1,0:T(8,128)S(1)} %get-tuple-element.26), channel_id=1, source_target_pairs={{0,576},{24,600},{48,624},{72,648},{96,288},{120,312},{144,336},{1... | collective-permute-start | bytes 393224 | tf_op jit(solution)/shard_map/ppermute | solution.py:362
  13.9 0.1 pad_add_fusion.place_ref.place
  14.0 0.0 collective-permute-done.opposite.arrived
  14.0 0.6 shard_map.62
  14.6 0.0 copy-start.1
  14.6 0.0 copy-start.2
  14.6 16.0 %collective-permute-start.6 = (f32[3,128,128]{2,1,0:T(8,128)S(1)}, f32[3,128,128]{2,1,0:T(8,128)S(1)}, u32[]{:S(2)}, u32[]{:S(2)}) collective-permute-start(f32[3,128,128]{2,1,0:T(8,128)S(1)} %shard_map.62), channel_id=1, source_target_pairs={{0,23},{7,8},{8,7},{15,16},{16,15},{23,0},{24,47},{31,32},{32,31},... | collective-permute-start | bytes 589832 | tf_op jit(solution)/shard_map/ppermute | solution.py:370
  30.7 0.0 copy-start.3
  30.7 3.9 %all-gather = f32[4,2,128,128]{3,2,1,0:T(8,128)S(1)} all-gather(f32[2,2,128,128]{3,2,1,0:T(8,128)S(1)} %pad_maximum_fusion), channel_id=2, replica_groups={{0,24},{48,72},{96,120},{144,168},{192,216},{240,264},{288,312},{336,36..., dimensions={0}, use_global_device_ids=true | all-gather | bytes 786432 | tf_op jit(solution)/shard_map/all_gather | solution.py:389
  34.6 3.0 %shard_map.59.meta = s32[2,27]{1,0:T(2,128)S(1)} custom-call(s32[2]{0:T(128)S(1)} %pad_add_fusion.place_ref.place, s32[4,1536]{1,0:T(4,128)S(1)} %bitcast.28, s32[6,1536]{1,0:T(8,128)S(1)} %bitcast.27, s32[1536]{0:T(1024)S(1)} %copy-done.3), custom_call_target="tpu_custom_call" | custom-call | bytes 2097152 | tf_op jit(solution)/shard_map/pallas_call | solution.py:347
  37.5 2.2 %all-gather.1 = f32[4,2,128,128]{3,2,1,0:T(8,128)S(1)} all-gather(f32[2,2,128,128]{3,2,1,0:T(8,128)S(1)} %collective-permute-done.opposite.arrived), channel_id=3, replica_groups={{0,24},{48,72},{96,120},{144,168},{192,216},{240,264},{288,312},{336,36..., dimensions={0}, use_global_device_ids=true | all-gather | bytes 786432 | tf_op jit(solution)/shard_map/all_gather | solution.py:389
  39.7 0.0 collective-permute-done.3.relayed
  39.7 0.0 collective-permute-done.2.below
  39.7 0.0 collective-permute-done.1.above
  39.7 0.9 %shard_map.60 = (f32[2,128,128]{2,1,0:T(8,128)S(1)}, f32[2,128,128]{2,1,0:T(8,128)S(1)}, f32[4,128,128]{2,1,0:T(8,128)S(1)}, f32[3,128,128]{2,1,0:T(8,128)S(1)},...) custom-call(s32[2,27]{1,0:T(2,128)S(1)} %shard_map.59.meta, f32[2,4,128,128]{3,2,1,0:T(8,128)S(1)} %copy-done, ...), custom_call_target="tpu_custom_call" | custom-call | flops 100663296 | bytes 2097152 | tf_op jit(solution)/shard_map/pallas_call | solution.py:347
  40.7 1.3 %collective-permute-start.5 = (f32[4,128,128]{2,1,0:T(8,128)S(1)}, f32[4,128,128]{2,1,0:T(8,128)S(1)}, u32[]{:S(2)}, u32[]{:S(2)}) collective-permute-start(f32[4,128,128]{2,1,0:T(8,128)S(1)} %get-tuple-element.20), channel_id=1, source_target_pairs={{1,0},{2,1},{3,2},{4,3},{5,4},{6,5},{7,6},{9,8},{10,9},{11,10},{12... | collective-permute-start | bytes 786440 | tf_op jit(solution)/shard_map/ppermute | solution.py:370
  42.0 4.0 %collective-permute-start.4 = (f32[3,128,128]{2,1,0:T(8,128)S(1)}, f32[3,128,128]{2,1,0:T(8,128)S(1)}, u32[]{:S(2)}, u32[]{:S(2)}) collective-permute-start(f32[3,128,128]{2,1,0:T(8,128)S(1)} %get-tuple-element.19), channel_id=1, source_target_pairs={{0,1},{1,2},{2,3},{3,4},{4,5},{5,6},{6,7},{8,9},{9,10},{10,11},{11... | collective-permute-start | bytes 589832 | tf_op jit(solution)/shard_map/ppermute | solution.py:370
  46.0 2.2 %shard_map.61 = (f32[2,6,128,128]{3,2,1,0:T(8,128)S(1)}, f32[2,6,128,128]{3,2,1,0:T(8,128)S(1)}, f32[1,128,128]{2,1,0:T(8,128)S(1)}, f32[2,128,128]{2,1,0:T(8,128)S(1)}) custom-call(s32[2,27]{1,0:T(2,128)S(1)} %shard_map.59.meta, f32[2,4,128,128]{3,2,1,0:T(8,128)S(1)} %copy-done, f32[2,2,2,128,128]{4,3,2,1,0:T(8,128)S(1)} %bitcast.23, ...), custom_call_target="tpu_custom_call" | custom-call | flops 251658240 | bytes 2097152 | tf_op jit(solution)/shard_map/pallas_call | solution.py:347
  48.2 1.9 %collective-permute-start.7 = (f32[1,128,128]{2,1,0:T(8,128)S(1)}, f32[1,128,128]{2,1,0:T(8,128)S(1)}, u32[]{:S(2)}, u32[]{:S(2)}) collective-permute-start(f32[1,128,128]{2,1,0:T(8,128)S(1)} %get-tuple-element.21), channel_id=1, source_target_pairs={{0,23},{7,8},{8,7},{15,16},{16,15},{23,0},{24,47},{31,32},{32,31},... | collective-permute-start | bytes 196616 | tf_op jit(solution)/shard_map/ppermute | solution.py:370
  50.1 3.6 %collective-permute-start.8 = (f32[2,128,128]{2,1,0:T(8,128)S(1)}, f32[2,128,128]{2,1,0:T(8,128)S(1)}, u32[]{:S(2)}, u32[]{:S(2)}) collective-permute-start(f32[2,128,128]{2,1,0:T(8,128)S(1)} %get-tuple-element.23), channel_id=1, source_target_pairs={{0,96},{24,120},{48,144},{72,168},{96,0},{120,24},{144,48},{168,72... | collective-permute-start | bytes 393224 | tf_op jit(solution)/shard_map/ppermute | solution.py:362
  53.7 0.0 collective-permute-done.6.given
  53.7 0.8 shard_map.64.middle
  54.5 2.2 %collective-permute-start.10 = (f32[2,128,128]{2,1,0:T(8,128)S(1)}, f32[2,128,128]{2,1,0:T(8,128)S(1)}, u32[]{:S(2)}, u32[]{:S(2)}) collective-permute-start(f32[2,128,128]{2,1,0:T(8,128)S(1)} %shard_map.64.middle), channel_id=1, source_target_pairs={{0,672},{24,696},{48,720},{72,744},{96,0},{120,24},{144,48},{168,7... | collective-permute-start | bytes 393224 | tf_op jit(solution)/shard_map/ppermute | solution.py:362
  56.7 4.2 %collective-permute-start.9 = (f32[2,128,128]{2,1,0:T(8,128)S(1)}, f32[2,128,128]{2,1,0:T(8,128)S(1)}, u32[]{:S(2)}, u32[]{:S(2)}) collective-permute-start(f32[2,128,128]{2,1,0:T(8,128)S(1)} %shard_map.64.middle), channel_id=1, source_target_pairs={{0,72},{24,48},{48,24},{72,0},{96,168},{120,144},{144,120},{168,96... | collective-permute-start | bytes 393224 | tf_op jit(solution)/shard_map/ppermute | solution.py:362
  60.9 1.1 %collective-permute-done.8.third_d = f32[2,128,128]{2,1,0:T(8,128)S(1)} collective-permute-done((f32[2,128,128]{2,1,0:T(8,128)S(1)}, f32[2,128,128]{2,1,0:T(8,128)S(1)}, u32[]{:S(2)}, u32[]{:S(2)}) %collective-permute-start.8) | collective-permute-done | bytes 131104 | tf_op jit(solution)/shard_map/ppermute | solution.py:362
  62.0 3.3 %shard_map.65 = (f32[2,6,128,128]{3,2,1,0:T(8,128)}, f32[2,6,128,128]{3,2,1,0:T(8,128)S(1)}) custom-call(s32[2,27]{1,0:T(2,128)S(1)} %shard_map.59.meta, f32[2,4,128,128]{3,2,1,0:T(8,128)S(1)} %copy-done, f32[2,6,128,128]{3,2,1,0:T(8,128)S(1)} %get-tuple-element.16.early, f32[2,6,128,128]{3,2,1,0:T(8,128)S(1)} %get-tuple-element.17.early_part, ...), custom_call_target="tpu_custom_call" | custom-call | flops 251658240 | bytes 2097152 | tf_op jit(solution)/shard_map/pallas_call | solution.py:347
  65.3 11.4 %all-gather.2 = f32[4,128,128]{2,1,0:T(8,128)S(1)} all-gather(f32[2,128,128]{2,1,0:T(8,128)S(1)} %shard_map.64.middle), channel_id=4, replica_groups={{0,24},{48,72},{96,120},{144,168},{192,216},{240,264},{288,312},{336,36..., dimensions={0}, use_global_device_ids=true | all-gather | bytes 393216 | tf_op jit(solution)/shard_map/all_gather | solution.py:389
  76.7 1.9 %shard_map.66 = f32[2,6,128,128]{3,2,1,0:T(8,128)} custom-call(s32[2,27]{1,0:T(2,128)S(1)} %shard_map.59.meta, f32[2,4,128,128]{3,2,1,0:T(8,128)S(1)} %copy-done, f32[2,6,128,128]{3,2,1,0:T(8,128)S(1)} %get-tuple-element.25.part, f32[2,2,128,128]{3,2,1,0:T(8,128)S(1)} %bitcast.26, f32[2,128,128]{2,1,0:T(8,128)S(1)} %collective-permute-done.9.mid_across, ...), custom_call_target="tpu_custom_call" | custom-call | flops 50331648 | bytes 2097152 | tf_op jit(solution)/shard_map/pallas_call | solution.py:347
  (12 shorter events, 0.1 us)
Async XLA Ops:
  0.6 13.4 %copy-start = (f32[2,4,128,128]{3,2,1,0:T(8,128)S(1)}, f32[2,4,128,128]{3,2,1,0:T(8,128)}, u32[]{:S(2)}) copy-start(f32[2,4,128,128]{3,2,1,0:T(8,128)} %x.11) | copy-start | bytes 1572868
  1.8 12.2 %collective-permute-start = (f32[2,2,128,128]{3,2,1,0:T(8,128)S(1)}, f32[2,2,128,128]{3,2,1,0:T(8,128)S(1)}, u32[]{:S(2)}, u32[]{:S(2)}) collective-permute-start(f32[2,2,128,128]{3,2,1,0:T(8,128)S(1)} %pad_maximum_fusion), channel_id=1, source_target_pairs={{0,48},{24,72},{48,0},{72,24},{96,144},{120,168},{144,96},{168,120... | collective-permute-start | bytes 786440 | tf_op jit(solution)/shard_map/ppermute | solution.py:362
  3.7 36.0 %collective-permute-start.2 = (f32[2,128,128]{2,1,0:T(8,128)S(1)}, f32[2,128,128]{2,1,0:T(8,128)S(1)}, u32[]{:S(2)}, u32[]{:S(2)}) collective-permute-start(f32[2,128,128]{2,1,0:T(8,128)S(1)} %get-tuple-element.29), channel_id=1, source_target_pairs={{0,96},{24,120},{48,144},{72,168},{96,192},{120,216},{144,240},{16... | collective-permute-start | bytes 393224 | tf_op jit(solution)/shard_map/ppermute | solution.py:362
  9.5 30.2 %collective-permute-start.1 = (f32[2,128,128]{2,1,0:T(8,128)S(1)}, f32[2,128,128]{2,1,0:T(8,128)S(1)}, u32[]{:S(2)}, u32[]{:S(2)}) collective-permute-start(f32[2,128,128]{2,1,0:T(8,128)S(1)} %get-tuple-element.29), channel_id=1, source_target_pairs={{0,672},{24,696},{48,720},{72,744},{96,0},{120,24},{144,48},{168,7... | collective-permute-start | bytes 393224 | tf_op jit(solution)/shard_map/ppermute | solution.py:362
  11.7 28.0 %collective-permute-start.3 = (f32[2,128,128]{2,1,0:T(8,128)S(1)}, f32[2,128,128]{2,1,0:T(8,128)S(1)}, u32[]{:S(2)}, u32[]{:S(2)}) collective-permute-start(f32[2,128,128]{2,1,0:T(8,128)S(1)} %get-tuple-element.26), channel_id=1, source_target_pairs={{0,576},{24,600},{48,624},{72,648},{96,288},{120,312},{144,336},{1... | collective-permute-start | bytes 393224 | tf_op jit(solution)/shard_map/ppermute | solution.py:362
  14.6 20.0 %copy-start.1 = (s32[1536,6]{0,1:T(8,128)S(1)}, s32[1536,6]{0,1:T(8,128)}, u32[]{:S(2)}) copy-start(s32[1536,6]{0,1:T(8,128)} %param.6) | copy-start | bytes 110596
  14.6 19.9 %copy-start.2 = (s32[1536,4]{0,1:T(4,128)S(1)}, s32[1536,4]{0,1:T(4,128)}, u32[]{:S(2)}) copy-start(s32[1536,4]{0,1:T(4,128)} %param.5) | copy-start | bytes 73732
  14.6 39.1 %collective-permute-start.6 = (f32[3,128,128]{2,1,0:T(8,128)S(1)}, f32[3,128,128]{2,1,0:T(8,128)S(1)}, u32[]{:S(2)}, u32[]{:S(2)}) collective-permute-start(f32[3,128,128]{2,1,0:T(8,128)S(1)} %shard_map.62), channel_id=1, source_target_pairs={{0,23},{7,8},{8,7},{15,16},{16,15},{23,0},{24,47},{31,32},{32,31},... | collective-permute-start | bytes 589832 | tf_op jit(solution)/shard_map/ppermute | solution.py:370
  30.7 3.9 %copy-start.3 = (s32[1536]{0:T(1024)S(1)}, s32[1536]{0:T(1024)}, u32[]{:S(2)}) copy-start(s32[1536]{0:T(1024)} %count_ref.1) | copy-start | bytes 18436
  40.7 13.1 %collective-permute-start.5 = (f32[4,128,128]{2,1,0:T(8,128)S(1)}, f32[4,128,128]{2,1,0:T(8,128)S(1)}, u32[]{:S(2)}, u32[]{:S(2)}) collective-permute-start(f32[4,128,128]{2,1,0:T(8,128)S(1)} %get-tuple-element.20), channel_id=1, source_target_pairs={{1,0},{2,1},{3,2},{4,3},{5,4},{6,5},{7,6},{9,8},{10,9},{11,10},{12... | collective-permute-start | bytes 786440 | tf_op jit(solution)/shard_map/ppermute | solution.py:370
  42.0 11.8 %collective-permute-start.4 = (f32[3,128,128]{2,1,0:T(8,128)S(1)}, f32[3,128,128]{2,1,0:T(8,128)S(1)}, u32[]{:S(2)}, u32[]{:S(2)}) collective-permute-start(f32[3,128,128]{2,1,0:T(8,128)S(1)} %get-tuple-element.19), channel_id=1, source_target_pairs={{0,1},{1,2},{2,3},{3,4},{4,5},{5,6},{6,7},{8,9},{9,10},{10,11},{11... | collective-permute-start | bytes 589832 | tf_op jit(solution)/shard_map/ppermute | solution.py:370
  48.2 12.7 %collective-permute-start.7 = (f32[1,128,128]{2,1,0:T(8,128)S(1)}, f32[1,128,128]{2,1,0:T(8,128)S(1)}, u32[]{:S(2)}, u32[]{:S(2)}) collective-permute-start(f32[1,128,128]{2,1,0:T(8,128)S(1)} %get-tuple-element.21), channel_id=1, source_target_pairs={{0,23},{7,8},{8,7},{15,16},{16,15},{23,0},{24,47},{31,32},{32,31},... | collective-permute-start | bytes 196616 | tf_op jit(solution)/shard_map/ppermute | solution.py:370
  50.1 11.9 %collective-permute-start.8 = (f32[2,128,128]{2,1,0:T(8,128)S(1)}, f32[2,128,128]{2,1,0:T(8,128)S(1)}, u32[]{:S(2)}, u32[]{:S(2)}) collective-permute-start(f32[2,128,128]{2,1,0:T(8,128)S(1)} %get-tuple-element.23), channel_id=1, source_target_pairs={{0,96},{24,120},{48,144},{72,168},{96,0},{120,24},{144,48},{168,72... | collective-permute-start | bytes 393224 | tf_op jit(solution)/shard_map/ppermute | solution.py:362
  54.5 22.2 %collective-permute-start.10 = (f32[2,128,128]{2,1,0:T(8,128)S(1)}, f32[2,128,128]{2,1,0:T(8,128)S(1)}, u32[]{:S(2)}, u32[]{:S(2)}) collective-permute-start(f32[2,128,128]{2,1,0:T(8,128)S(1)} %shard_map.64.middle), channel_id=1, source_target_pairs={{0,672},{24,696},{48,720},{72,744},{96,0},{120,24},{144,48},{168,7... | collective-permute-start | bytes 393224 | tf_op jit(solution)/shard_map/ppermute | solution.py:362
  56.7 20.0 %collective-permute-start.9 = (f32[2,128,128]{2,1,0:T(8,128)S(1)}, f32[2,128,128]{2,1,0:T(8,128)S(1)}, u32[]{:S(2)}, u32[]{:S(2)}) collective-permute-start(f32[2,128,128]{2,1,0:T(8,128)S(1)} %shard_map.64.middle), channel_id=1, source_target_pairs={{0,72},{24,48},{48,24},{72,0},{96,168},{120,144},{144,120},{168,96... | collective-permute-start | bytes 393224 | tf_op jit(solution)/shard_map/ppermute | solution.py:362

commit v5 on v4

--- a/solution.py
+++ b/solution.py
@@ -99,19 +99,19 @@
 
 
 def left(value):
-    high, low = halves(value)
-    return jnp.concatenate([high, low, high], axis=1)
+    return jnp.concatenate(halves(value), axis=0)
 
 
 def right(value):
-    high, low = halves(value)
-    return jnp.concatenate([high, high, low], axis=0)
+    return jnp.concatenate(halves(value), axis=1)
 
 
 def product(lefts, rights):
     a = lefts[0] if len(lefts) == 1 else jnp.concatenate(lefts, axis=1)
     b = rights[0] if len(rights) == 1 else jnp.concatenate(rights, axis=0)
-    return jnp.dot(a, b, preferred_element_type=jnp.float32)
+    all_four = jnp.dot(a, b, preferred_element_type=jnp.float32)
+    small = all_four[:BS, BS:] + all_four[BS:, :BS]
+    return all_four[:BS, :BS] + (small + all_four[BS:, BS:])
 
 
 def row_view(meta, r):
@@ -186,42 +186,55 @@
     third_message[...] = handed[...]
     square[...] = jnp.zeros_like(square)
     cube[...] = jnp.zeros_like(cube)
-    for r in range(2):
+    results = []
+    for r in range(2):
+        flag, _ = row_view(meta, r)
+        mutual2 = flag(POS2) != flag(NPOS2)
+        d, a2 = x[r, 0], x[r, 2]
+        d2, b2 = second_neighbour(meta, r, flag, near, across)
+        ld, l2, lb, r2 = left(d), left(a2), left(b2), right(b2)
+        once = product([ld, l2], [right(a2), right(d2)])
+        twice = product([l2], [r2])
+        beyond = jnp.where(mutual2, d, opposite[0, r])
+        step = right(product([left(d2), lb], [r2, right(beyond)]))
+        two = product([lb], [right(opposite[1, r])])
+        ahead = jnp.where(flag(HAS2_STEP), step, jnp.zeros_like(step))
+        results.append(
+            (
+                once,
+                twice,
+                product([ld], [right(once)]),
+                product([ld, l2], [right(twice), ahead]),
+                product([l2], [step]),
+                product([l2], [right(two)]),
+            )
+        )
+    for r, (once, twice, cube_once, cube_twice, cube_zero, cube_back) in enumerate(results):
         flag, slot = row_view(meta, r)
         pos2, npos2 = flag(POS2), flag(NPOS2)
-        d, a2 = x[r, 0], x[r, 2]
-        d2, b2 = second_neighbour(meta, r, flag, near, across)
-        ld, l2, r2 = left(d), left(a2), right(b2)
-
-        def put(where, value):
-            square[r, where] = value
-            cube[r, where] += product([ld], [right(value)])
-
+        mutual2 = pos2 != npos2
         step2 = jnp.where(pos2, slot(UP2), slot(DOWN2))
         back2 = jnp.where(pos2, slot(DOWN2), slot(UP2))
-        mutual2 = pos2 != npos2
-        other2 = jnp.where(mutual2, slot(ZERO), slot(TWO2))
 
         @pl.when(step2 >= 0)
         def _():
-            put(step2, product([ld, l2], [right(a2), right(d2)]))
+            square[r, step2] = once
+            cube[r, step2] = cube_once
 
         @pl.when(jnp.logical_and(slot(TWO2) >= 0, jnp.logical_not(mutual2)))
         def _():
-            put(slot(TWO2), product([l2], [r2]))
-
-        @pl.when(jnp.logical_and(other2 >= 0, flag(HAS2_STEP)))
-        def _():
-            beyond = jnp.where(mutual2, d, opposite[0, r])
-            step = product([left(d2), left(b2)], [r2, right(beyond)])
-            cube[r, other2] += product([l2], [right(step)])
+            square[r, slot(TWO2)] = twice
+            cube[r, slot(TWO2)] = cube_twice
+
+        @pl.when(jnp.logical_and(slot(ZERO) >= 0, jnp.logical_and(mutual2, flag(HAS2_STEP))))
+        def _():
+            cube[r, slot(ZERO)] = cube_zero
 
         onward2 = jnp.logical_and(jnp.logical_not(mutual2), npos2 == flag(FPOS2))
 
         @pl.when(jnp.logical_and(onward2, jnp.logical_and(back2 >= 0, flag(HAS2_TWO))))
         def _():
-            two = product([left(b2)], [right(opposite[1, r])])
-            cube[r, back2] += product([l2], [right(two)])
+            cube[r, back2] = cube_back
 
 
 def copy_kernel(given, taken):
@@ -265,79 +278,95 @@
     wraps = (wrap_a, wrap_b)
     square[...] = early[...]
     cube[...] = early_part[...]
-    for r in range(2):
+    results = []
+    for r in range(2):
+        flag, _ = row_view(meta, r)
+        pos1, pos3 = flag(POS1), flag(POS3)
+        mutual1 = pos1 != flag(NPOS1)
+        d, a1, a3 = x[r, 0], x[r, 1], x[r, 3]
+        d1, b1 = first_neighbour(r, flag, x, ring_left, ring_right, wraps)
+        d3, b3 = third_d[r], third[r]
+        ld, l1, l3, lb, r1 = left(d), left(a1), left(a3), left(b1), right(b1)
+        ra1, rd = right(a1), right(d)
+        once = product([ld, l1], [ra1, right(d1)])
+        twice = product([l1], [r1])
+        up = product([ld, l3], [right(a3), right(d3)])
+        far = from_side(flag, FIX_RIGHT, ring_right, wraps, 3 * r)
+        step = right(product([left(d1), lb], [r1, right(jnp.where(mutual1, d, far))]))
+        step3 = right(product([left(d3), left(b3)], [right(b3), rd]))
+        away, met = meeting(flag, r)
+        back = product([lb], [ra1])
+        outer = side_block(flag, r, ring_left, ring_right, wraps, 2)
+        outer += jnp.where(met, back, jnp.zeros_like(back))
+        beside = right(jnp.where(away, outer, middle[1 - r]))
+        none = jnp.zeros_like(step)
+        beside = jnp.where(flag(HAS1_ZERO), beside, none)
+        step = jnp.where(flag(HAS1_STEP), step, none)
+        back3 = jnp.logical_and(jnp.logical_not(pos3), flag(NPOS3))
+        step3 = jnp.where(jnp.logical_and(back3, flag(HAS3_STEP)), step3, none)
+        zero = [right(middle[r]), jnp.where(mutual1, step, none), step3]
+        results.append(
+            (
+                once,
+                twice,
+                up,
+                product([ld, l1], [right(once), beside]),
+                product([ld, l1], [right(twice), step]),
+                product([ld], [right(up)]),
+                product([ld, l1, l3], zero),
+            )
+        )
+    for r, (once, twice, up, cube_once, cube_twice, cube_up, cube_zero) in enumerate(results):
         flag, slot = row_view(meta, r)
-        pos1, pos3, npos1 = flag(POS1), flag(POS3), flag(NPOS1)
-        d, a1 = x[r, 0], x[r, 1]
-        d1, b1 = first_neighbour(r, flag, x, ring_left, ring_right, wraps)
-        ld, l1, r1 = left(d), left(a1), right(b1)
-
-        def put(where, value):
-            square[r, where] = value
-            cube[r, where] += product([ld], [right(value)])
-
+        pos1 = flag(POS1)
         step1 = jnp.where(pos1, slot(UP1), slot(DOWN1))
 
         @pl.when(slot(ZERO) >= 0)
         def _():
-            put(slot(ZERO), middle[r])
+            square[r, slot(ZERO)] = middle[r]
+            cube[r, slot(ZERO)] += cube_zero
 
         @pl.when(step1 >= 0)
         def _():
-            put(step1, product([ld, l1], [right(a1), right(d1)]))
-
-        @pl.when(jnp.logical_and(slot(TWO1) >= 0, jnp.logical_and(pos1, npos1)))
-        def _():
-            put(slot(TWO1), product([l1], [r1]))
-
-        mutual1 = pos1 != npos1
-        other1 = jnp.where(mutual1, slot(ZERO), jnp.where(pos1, slot(TWO1), -1))
-
-        @pl.when(jnp.logical_and(step1 >= 0, flag(HAS1_ZERO)))
-        def _():
-            away, met = meeting(flag, r)
-            back = product([left(b1)], [right(a1)])
-            outer = side_block(flag, r, ring_left, ring_right, wraps, 2)
-            outer += jnp.where(met, back, jnp.zeros_like(back))
-            cube[r, step1] += product([l1], [right(jnp.where(away, outer, middle[1 - r]))])
-
-        @pl.when(jnp.logical_and(other1 >= 0, flag(HAS1_STEP)))
-        def _():
-            far = from_side(flag, FIX_RIGHT, ring_right, wraps, 3 * r)
-            beyond = jnp.where(mutual1, d, far)
-            step = product([left(d1), left(b1)], [r1, right(beyond)])
-            cube[r, other1] += product([l1], [right(step)])
-
-        back3 = jnp.logical_and(jnp.logical_not(pos3), flag(NPOS3))
-
-        @pl.when(jnp.logical_and(back3, jnp.logical_and(slot(ZERO) >= 0, flag(HAS3_STEP))))
-        def _():
-            b3 = third[r]
-            step = product([left(third_d[r]), left(b3)], [right(b3), right(d)])
-            cube[r, slot(ZERO)] += product([left(x[r, 3])], [right(step)])
-
-        @pl.when(jnp.logical_and(slot(UP3) >= 0, pos3))
-        def _():
-            a3 = x[r, 3]
-            put(slot(UP3), product([ld, left(a3)], [right(a3), right(third_d[r])]))
+            square[r, step1] = once
+            cube[r, step1] = cube_once
+
+        @pl.when(jnp.logical_and(slot(TWO1) >= 0, jnp.logical_and(pos1, flag(NPOS1))))
+        def _():
+            square[r, slot(TWO1)] = twice
+            cube[r, slot(TWO1)] = cube_twice
+
+        @pl.when(jnp.logical_and(slot(UP3) >= 0, flag(POS3)))
+        def _():
+            square[r, slot(UP3)] = up
+            cube[r, slot(UP3)] = cube_up
 
 
 def cube_kernel(meta, x, part, mid_near, mid_across, mid_above, cube):
     cube[...] = part[...]
-    for r in range(2):
+    added = []
+    for r in range(2):
+        flag, _ = row_view(meta, r)
+        value = jnp.where(flag(NEAR2), mid_near[meta[0, OTHER], r], mid_across[r])
+        added.append(
+            (
+                product([left(x[r, 2])], [right(value)]),
+                product([left(x[r, 3])], [right(mid_above[r])]),
+            )
+        )
+    for r, (beside, above) in enumerate(added):
         flag, slot = row_view(meta, r)
         step2 = jnp.where(flag(POS2), slot(UP2), slot(DOWN2))
 
         @pl.when(jnp.logical_and(step2 >= 0, flag(HAS2_ZERO)))
         def _():
-            value = jnp.where(flag(NEAR2), mid_near[meta[0, OTHER], r], mid_across[r])
-            cube[r, step2] += product([left(x[r, 2])], [right(value)])
+            cube[r, step2] += beside
 
         ahead = jnp.logical_and(flag(POS3), flag(HAS3_ZERO))
 
         @pl.when(jnp.logical_and(ahead, slot(UP3) >= 0))
         def _():
-            cube[r, slot(UP3)] += product([left(x[r, 3])], [right(mid_above[r])])
+            cube[r, slot(UP3)] += above
 
 
 def call(kernel, out_shapes, *operands, smem=0, free=0, smem_out=False, flops=0):

time: 79.1 us -> 75.6 us (0.956)
  the two profiles are of different devices: /device:TPU:71 before, /device:TPU:1 now
where the time goes in v5:
time: 75.6 us; the launch traced here: 74.4 us
  starting transfers between devices  49.9 us (66%)
  Pallas kernels  11.5 us (15%)
  blocking collectives  8.47 us (11%)
  waiting for transfers between devices  2.32 us (3%)
  local copies, waits for them, and re-layouts  1.15 us (2%)
  between operations  0.86 us (1%)
    ppermute x7, starting transfers between devices, along(): lax.ppermute(value, axis, [(i, target(i) % count) for i in range(count)])  27.2 us
    ppermute x4, starting transfers between devices, anywhere(): return lax.ppermute(value, ('row', 'col'), pairs)  22.7 us
    pallas_call x8, Pallas kernels, call(): pl.pallas_call(kernel, out_shape=out_shapes, in_specs=[pl.BlockSpec(memor...  11.5 us
    all_gather x3, blocking collectives, both_cores(): return lax.all_gather(value, 'row', axis_index_groups=groups)  8.47 us
    ppermute x7, waiting for transfers between devices, along(): lax.ppermute(value, axis, [(i, target(i) % count) for i in range(count)])  2.31 us
  transfers between devices with their start and end apart: 11, of which 1 were waited for; matrix products, arithmetic and copies ran while one was open for 0% of the time, Pallas kernels for 13%

profile of v5, /device:TPU:1, one launch (start us, length us, event | category | flops | bytes accessed | tf_op | source)
XLA Modules:
  0.0 74.4 jit_solution(207397313781808916)
XLA Ops:
  0.6 1.1 %slice_bitcast_fusion.3 = (f32[2,128,128]{2,1,0:T(8,128)S(1)}, f32[1,2,128,128]{3,2,1,0:T(8,128)S(1)}, f32[1,2,128,128]{3,2,1,0:T(8,128)S(1)}, f32[2,128,128]{2,1,0:T(8,128)S(1)}) fusion(f32[2,4,128,128]{3,2,1,0:T(8,128)} %x.11), kind=kLoop, calls=%fused_computation.4 | loop fusion | bytes 917504 | tf_op jit(solution)/shard_map/squeeze | solution.py:429
  1.8 4.8 %collective-permute-start = (f32[2,2,128,128]{3,2,1,0:T(8,128)S(1)}, f32[2,2,128,128]{3,2,1,0:T(8,128)S(1)}, u32[]{:S(2)}, u32[]{:S(2)}) collective-permute-start(f32[2,2,128,128]{3,2,1,0:T(8,128)S(1)} %pad_maximum_fusion), channel_id=1, source_target_pairs={{0,48},{24,72},{48,0},{72,24},{96,144},{120,168},{144,96},{168,120... | collective-permute-start | bytes 786440 | tf_op jit(solution)/shard_map/ppermute | solution.py:391
  6.6 5.8 %collective-permute-start.2 = (f32[2,128,128]{2,1,0:T(8,128)S(1)}, f32[2,128,128]{2,1,0:T(8,128)S(1)}, u32[]{:S(2)}, u32[]{:S(2)}) collective-permute-start(f32[2,128,128]{2,1,0:T(8,128)S(1)} %get-tuple-element.29), channel_id=1, source_target_pairs={{0,96},{24,120},{48,144},{72,168},{96,192},{120,216},{144,240},{16... | collective-permute-start | bytes 393224 | tf_op jit(solution)/shard_map/ppermute | solution.py:391
  12.5 4.1 %collective-permute-start.1 = (f32[2,128,128]{2,1,0:T(8,128)S(1)}, f32[2,128,128]{2,1,0:T(8,128)S(1)}, u32[]{:S(2)}, u32[]{:S(2)}) collective-permute-start(f32[2,128,128]{2,1,0:T(8,128)S(1)} %get-tuple-element.29), channel_id=1, source_target_pairs={{0,672},{24,696},{48,720},{72,744},{96,0},{120,24},{144,48},{168,7... | collective-permute-start | bytes 393224 | tf_op jit(solution)/shard_map/ppermute | solution.py:391
  16.6 2.5 %collective-permute-start.3 = (f32[2,128,128]{2,1,0:T(8,128)S(1)}, f32[2,128,128]{2,1,0:T(8,128)S(1)}, u32[]{:S(2)}, u32[]{:S(2)}) collective-permute-start(f32[2,128,128]{2,1,0:T(8,128)S(1)} %get-tuple-element.26), channel_id=1, source_target_pairs={{0,576},{24,600},{48,624},{72,648},{96,288},{120,312},{144,336},{1... | collective-permute-start | bytes 393224 | tf_op jit(solution)/shard_map/ppermute | solution.py:391
  19.1 0.1 pad_add_fusion.place_ref.place
  19.1 0.6 shard_map.62
  19.7 0.0 copy-start.1
  19.7 0.0 copy-start.2
  19.7 15.5 %collective-permute-start.6 = (f32[3,128,128]{2,1,0:T(8,128)S(1)}, f32[3,128,128]{2,1,0:T(8,128)S(1)}, u32[]{:S(2)}, u32[]{:S(2)}) collective-permute-start(f32[3,128,128]{2,1,0:T(8,128)S(1)} %shard_map.62), channel_id=1, source_target_pairs={{0,23},{7,8},{8,7},{15,16},{16,15},{23,0},{24,47},{31,32},{32,31},... | collective-permute-start | bytes 589832 | tf_op jit(solution)/shard_map/ppermute | solution.py:399
  35.2 0.0 copy-start.3
  35.2 3.9 %all-gather = f32[4,2,128,128]{3,2,1,0:T(8,128)S(1)} all-gather(f32[2,2,128,128]{3,2,1,0:T(8,128)S(1)} %pad_maximum_fusion), channel_id=2, replica_groups={{0,24},{48,72},{96,120},{144,168},{192,216},{240,264},{288,312},{336,36..., dimensions={0}, use_global_device_ids=true | all-gather | bytes 786432 | tf_op jit(solution)/shard_map/all_gather | solution.py:418
  39.1 3.0 %shard_map.59.meta = s32[2,27]{1,0:T(2,128)S(1)} custom-call(s32[2]{0:T(128)S(1)} %pad_add_fusion.place_ref.place, s32[4,1536]{1,0:T(4,128)S(1)} %bitcast.28, s32[6,1536]{1,0:T(8,128)S(1)} %bitcast.27, s32[1536]{0:T(1024)S(1)} %copy-done.3), custom_call_target="tpu_custom_call" | custom-call | bytes 2097152 | tf_op jit(solution)/shard_map/pallas_call | solution.py:376
  42.1 2.2 %all-gather.1 = f32[4,2,128,128]{3,2,1,0:T(8,128)S(1)} all-gather(f32[2,2,128,128]{3,2,1,0:T(8,128)S(1)} %collective-permute-done.opposite.arrived), channel_id=3, replica_groups={{0,24},{48,72},{96,120},{144,168},{192,216},{240,264},{288,312},{336,36..., dimensions={0}, use_global_device_ids=true | all-gather | bytes 786432 | tf_op jit(solution)/shard_map/all_gather | solution.py:418
  44.3 0.0 collective-permute-done.3.relayed
  44.3 0.0 collective-permute-done.2.below
  44.3 0.0 collective-permute-done.1.above
  44.3 0.9 %shard_map.60 = (f32[2,128,128]{2,1,0:T(8,128)S(1)}, f32[2,128,128]{2,1,0:T(8,128)S(1)}, f32[4,128,128]{2,1,0:T(8,128)S(1)}, f32[3,128,128]{2,1,0:T(8,128)S(1)},...) custom-call(s32[2,27]{1,0:T(2,128)S(1)} %shard_map.59.meta, f32[2,4,128,128]{3,2,1,0:T(8,128)S(1)} %copy-done, ...), custom_call_target="tpu_custom_call" | custom-call | flops 100663296 | bytes 2097152 | tf_op jit(solution)/shard_map/pallas_call | solution.py:376
  45.2 1.3 %collective-permute-start.5 = (f32[4,128,128]{2,1,0:T(8,128)S(1)}, f32[4,128,128]{2,1,0:T(8,128)S(1)}, u32[]{:S(2)}, u32[]{:S(2)}) collective-permute-start(f32[4,128,128]{2,1,0:T(8,128)S(1)} %get-tuple-element.20), channel_id=1, source_target_pairs={{1,0},{2,1},{3,2},{4,3},{5,4},{6,5},{7,6},{9,8},{10,9},{11,10},{12... | collective-permute-start | bytes 786440 | tf_op jit(solution)/shard_map/ppermute | solution.py:399
  46.5 4.0 %collective-permute-start.4 = (f32[3,128,128]{2,1,0:T(8,128)S(1)}, f32[3,128,128]{2,1,0:T(8,128)S(1)}, u32[]{:S(2)}, u32[]{:S(2)}) collective-permute-start(f32[3,128,128]{2,1,0:T(8,128)S(1)} %get-tuple-element.19), channel_id=1, source_target_pairs={{0,1},{1,2},{2,3},{3,4},{4,5},{5,6},{6,7},{8,9},{9,10},{10,11},{11... | collective-permute-start | bytes 589832 | tf_op jit(solution)/shard_map/ppermute | solution.py:399
  50.5 1.6 %shard_map.61 = (f32[2,6,128,128]{3,2,1,0:T(8,128)S(1)}, f32[2,6,128,128]{3,2,1,0:T(8,128)S(1)}, f32[1,128,128]{2,1,0:T(8,128)S(1)}, f32[2,128,128]{2,1,0:T(8,128)S(1)}) custom-call(s32[2,27]{1,0:T(2,128)S(1)} %shard_map.59.meta, f32[2,4,128,128]{3,2,1,0:T(8,128)S(1)} %copy-done, f32[2,2,2,128,128]{4,3,2,1,0:T(8,128)S(1)} %bitcast.23, ...), custom_call_target="tpu_custom_call" | custom-call | flops 251658240 | bytes 2097152 | tf_op jit(solution)/shard_map/pallas_call | solution.py:376
  52.2 1.9 %collective-permute-start.7 = (f32[1,128,128]{2,1,0:T(8,128)S(1)}, f32[1,128,128]{2,1,0:T(8,128)S(1)}, u32[]{:S(2)}, u32[]{:S(2)}) collective-permute-start(f32[1,128,128]{2,1,0:T(8,128)S(1)} %get-tuple-element.21), channel_id=1, source_target_pairs={{0,23},{7,8},{8,7},{15,16},{16,15},{23,0},{24,47},{31,32},{32,31},... | collective-permute-start | bytes 196616 | tf_op jit(solution)/shard_map/ppermute | solution.py:399
  54.1 1.9 %collective-permute-start.8 = (f32[2,128,128]{2,1,0:T(8,128)S(1)}, f32[2,128,128]{2,1,0:T(8,128)S(1)}, u32[]{:S(2)}, u32[]{:S(2)}) collective-permute-start(f32[2,128,128]{2,1,0:T(8,128)S(1)} %get-tuple-element.23), channel_id=1, source_target_pairs={{0,96},{24,120},{48,144},{72,168},{96,0},{120,24},{144,48},{168,72... | collective-permute-start | bytes 393224 | tf_op jit(solution)/shard_map/ppermute | solution.py:391
  56.0 0.0 collective-permute-done.6.given
  56.0 0.0 collective-permute-done.4.ring_left
  56.1 0.8 %shard_map.64.middle = f32[2,128,128]{2,1,0:T(8,128)S(1)} custom-call(s32[2,27]{1,0:T(2,128)S(1)} %shard_map.59.meta, f32[2,4,128,128]{3,2,1,0:T(8,128)S(1)} %copy-done, f32[2,128,128]{2,1,0:T(8,128)S(1)} %get-tuple-element.18.base, f32[3,128,128]{2,1,0:T(8,128)S(1)} %collective-permute-done.4.ring_left, ...), custom_call_target="tpu_custom_call" | custom-call | flops 25165824 | bytes 2097152 | tf_op jit(solution)/shard_map/pallas_call | solution.py:376
  56.9 4.5 %collective-permute-start.10 = (f32[2,128,128]{2,1,0:T(8,128)S(1)}, f32[2,128,128]{2,1,0:T(8,128)S(1)}, u32[]{:S(2)}, u32[]{:S(2)}) collective-permute-start(f32[2,128,128]{2,1,0:T(8,128)S(1)} %shard_map.64.middle), channel_id=1, source_target_pairs={{0,672},{24,696},{48,720},{72,744},{96,0},{120,24},{144,48},{168,7... | collective-permute-start | bytes 393224 | tf_op jit(solution)/shard_map/ppermute | solution.py:391
  61.4 3.6 %collective-permute-start.9 = (f32[2,128,128]{2,1,0:T(8,128)S(1)}, f32[2,128,128]{2,1,0:T(8,128)S(1)}, u32[]{:S(2)}, u32[]{:S(2)}) collective-permute-start(f32[2,128,128]{2,1,0:T(8,128)S(1)} %shard_map.64.middle), channel_id=1, source_target_pairs={{0,72},{24,48},{48,24},{72,0},{96,168},{120,144},{144,120},{168,96... | collective-permute-start | bytes 393224 | tf_op jit(solution)/shard_map/ppermute | solution.py:391
  65.0 2.3 %collective-permute-done.8.third_d = f32[2,128,128]{2,1,0:T(8,128)S(1)} collective-permute-done((f32[2,128,128]{2,1,0:T(8,128)S(1)}, f32[2,128,128]{2,1,0:T(8,128)S(1)}, u32[]{:S(2)}, u32[]{:S(2)}) %collective-permute-start.8) | collective-permute-done | bytes 131104 | tf_op jit(solution)/shard_map/ppermute | solution.py:391
  67.3 2.9 %shard_map.65 = (f32[2,6,128,128]{3,2,1,0:T(8,128)}, f32[2,6,128,128]{3,2,1,0:T(8,128)S(1)}) custom-call(s32[2,27]{1,0:T(2,128)S(1)} %shard_map.59.meta, f32[2,4,128,128]{3,2,1,0:T(8,128)S(1)} %copy-done, f32[2,6,128,128]{3,2,1,0:T(8,128)S(1)} %get-tuple-element.16.early, f32[2,6,128,128]{3,2,1,0:T(8,128)S(1)} %get-tuple-element.17.early_part, ...), custom_call_target="tpu_custom_call" | custom-call | flops 251658240 | bytes 2097152 | tf_op jit(solution)/shard_map/pallas_call | solution.py:376
  70.1 2.4 %all-gather.2 = f32[4,128,128]{2,1,0:T(8,128)S(1)} all-gather(f32[2,128,128]{2,1,0:T(8,128)S(1)} %shard_map.64.middle), channel_id=4, replica_groups={{0,24},{48,72},{96,120},{144,168},{192,216},{240,264},{288,312},{336,36..., dimensions={0}, use_global_device_ids=true | all-gather | bytes 393216 | tf_op jit(solution)/shard_map/all_gather | solution.py:418
  72.5 1.8 %shard_map.66 = f32[2,6,128,128]{3,2,1,0:T(8,128)} custom-call(s32[2,27]{1,0:T(2,128)S(1)} %shard_map.59.meta, f32[2,4,128,128]{3,2,1,0:T(8,128)S(1)} %copy-done, f32[2,6,128,128]{3,2,1,0:T(8,128)S(1)} %get-tuple-element.25.part, f32[2,2,128,128]{3,2,1,0:T(8,128)S(1)} %bitcast.26, f32[2,128,128]{2,1,0:T(8,128)S(1)} %collective-permute-done.9.mid_across, ...), custom_call_target="tpu_custom_call" | custom-call | flops 50331648 | bytes 2097152 | tf_op jit(solution)/shard_map/pallas_call | solution.py:376
  (12 shorter events, 0.1 us)
Async XLA Ops:
  0.6 18.5 %copy-start = (f32[2,4,128,128]{3,2,1,0:T(8,128)S(1)}, f32[2,4,128,128]{3,2,1,0:T(8,128)}, u32[]{:S(2)}) copy-start(f32[2,4,128,128]{3,2,1,0:T(8,128)} %x.11) | copy-start | bytes 1572868
  1.8 17.3 %collective-permute-start = (f32[2,2,128,128]{3,2,1,0:T(8,128)S(1)}, f32[2,2,128,128]{3,2,1,0:T(8,128)S(1)}, u32[]{:S(2)}, u32[]{:S(2)}) collective-permute-start(f32[2,2,128,128]{3,2,1,0:T(8,128)S(1)} %pad_maximum_fusion), channel_id=1, source_target_pairs={{0,48},{24,72},{48,0},{72,24},{96,144},{120,168},{144,96},{168,120... | collective-permute-start | bytes 786440 | tf_op jit(solution)/shard_map/ppermute | solution.py:391
  6.6 37.7 %collective-permute-start.2 = (f32[2,128,128]{2,1,0:T(8,128)S(1)}, f32[2,128,128]{2,1,0:T(8,128)S(1)}, u32[]{:S(2)}, u32[]{:S(2)}) collective-permute-start(f32[2,128,128]{2,1,0:T(8,128)S(1)} %get-tuple-element.29), channel_id=1, source_target_pairs={{0,96},{24,120},{48,144},{72,168},{96,192},{120,216},{144,240},{16... | collective-permute-start | bytes 393224 | tf_op jit(solution)/shard_map/ppermute | solution.py:391
  12.5 31.9 %collective-permute-start.1 = (f32[2,128,128]{2,1,0:T(8,128)S(1)}, f32[2,128,128]{2,1,0:T(8,128)S(1)}, u32[]{:S(2)}, u32[]{:S(2)}) collective-permute-start(f32[2,128,128]{2,1,0:T(8,128)S(1)} %get-tuple-element.29), channel_id=1, source_target_pairs={{0,672},{24,696},{48,720},{72,744},{96,0},{120,24},{144,48},{168,7... | collective-permute-start | bytes 393224 | tf_op jit(solution)/shard_map/ppermute | solution.py:391
  16.6 27.7 %collective-permute-start.3 = (f32[2,128,128]{2,1,0:T(8,128)S(1)}, f32[2,128,128]{2,1,0:T(8,128)S(1)}, u32[]{:S(2)}, u32[]{:S(2)}) collective-permute-start(f32[2,128,128]{2,1,0:T(8,128)S(1)} %get-tuple-element.26), channel_id=1, source_target_pairs={{0,576},{24,600},{48,624},{72,648},{96,288},{120,312},{144,336},{1... | collective-permute-start | bytes 393224 | tf_op jit(solution)/shard_map/ppermute | solution.py:391
  19.7 19.4 %copy-start.1 = (s32[1536,6]{0,1:T(8,128)S(1)}, s32[1536,6]{0,1:T(8,128)}, u32[]{:S(2)}) copy-start(s32[1536,6]{0,1:T(8,128)} %param.6) | copy-start | bytes 110596
  19.7 19.4 %copy-start.2 = (s32[1536,4]{0,1:T(4,128)S(1)}, s32[1536,4]{0,1:T(4,128)}, u32[]{:S(2)}) copy-start(s32[1536,4]{0,1:T(4,128)} %param.5) | copy-start | bytes 73732
  19.7 36.3 %collective-permute-start.6 = (f32[3,128,128]{2,1,0:T(8,128)S(1)}, f32[3,128,128]{2,1,0:T(8,128)S(1)}, u32[]{:S(2)}, u32[]{:S(2)}) collective-permute-start(f32[3,128,128]{2,1,0:T(8,128)S(1)} %shard_map.62), channel_id=1, source_target_pairs={{0,23},{7,8},{8,7},{15,16},{16,15},{23,0},{24,47},{31,32},{32,31},... | collective-permute-start | bytes 589832 | tf_op jit(solution)/shard_map/ppermute | solution.py:399
  35.2 3.9 %copy-start.3 = (s32[1536]{0:T(1024)S(1)}, s32[1536]{0:T(1024)}, u32[]{:S(2)}) copy-start(s32[1536]{0:T(1024)} %count_ref.1) | copy-start | bytes 18436
  45.2 10.8 %collective-permute-start.5 = (f32[4,128,128]{2,1,0:T(8,128)S(1)}, f32[4,128,128]{2,1,0:T(8,128)S(1)}, u32[]{:S(2)}, u32[]{:S(2)}) collective-permute-start(f32[4,128,128]{2,1,0:T(8,128)S(1)} %get-tuple-element.20), channel_id=1, source_target_pairs={{1,0},{2,1},{3,2},{4,3},{5,4},{6,5},{7,6},{9,8},{10,9},{11,10},{12... | collective-permute-start | bytes 786440 | tf_op jit(solution)/shard_map/ppermute | solution.py:399
  46.5 9.5 %collective-permute-start.4 = (f32[3,128,128]{2,1,0:T(8,128)S(1)}, f32[3,128,128]{2,1,0:T(8,128)S(1)}, u32[]{:S(2)}, u32[]{:S(2)}) collective-permute-start(f32[3,128,128]{2,1,0:T(8,128)S(1)} %get-tuple-element.19), channel_id=1, source_target_pairs={{0,1},{1,2},{2,3},{3,4},{4,5},{5,6},{6,7},{8,9},{9,10},{10,11},{11... | collective-permute-start | bytes 589832 | tf_op jit(solution)/shard_map/ppermute | solution.py:399
  52.2 12.8 %collective-permute-start.7 = (f32[1,128,128]{2,1,0:T(8,128)S(1)}, f32[1,128,128]{2,1,0:T(8,128)S(1)}, u32[]{:S(2)}, u32[]{:S(2)}) collective-permute-start(f32[1,128,128]{2,1,0:T(8,128)S(1)} %get-tuple-element.21), channel_id=1, source_target_pairs={{0,23},{7,8},{8,7},{15,16},{16,15},{23,0},{24,47},{31,32},{32,31},... | collective-permute-start | bytes 196616 | tf_op jit(solution)/shard_map/ppermute | solution.py:399
  54.1 13.2 %collective-permute-start.8 = (f32[2,128,128]{2,1,0:T(8,128)S(1)}, f32[2,128,128]{2,1,0:T(8,128)S(1)}, u32[]{:S(2)}, u32[]{:S(2)}) collective-permute-start(f32[2,128,128]{2,1,0:T(8,128)S(1)} %get-tuple-element.23), channel_id=1, source_target_pairs={{0,96},{24,120},{48,144},{72,168},{96,0},{120,24},{144,48},{168,72... | collective-permute-start | bytes 393224 | tf_op jit(solution)/shard_map/ppermute | solution.py:391
  56.9 15.7 %collective-permute-start.10 = (f32[2,128,128]{2,1,0:T(8,128)S(1)}, f32[2,128,128]{2,1,0:T(8,128)S(1)}, u32[]{:S(2)}, u32[]{:S(2)}) collective-permute-start(f32[2,128,128]{2,1,0:T(8,128)S(1)} %shard_map.64.middle), channel_id=1, source_target_pairs={{0,672},{24,696},{48,720},{72,744},{96,0},{120,24},{144,48},{168,7... | collective-permute-start | bytes 393224 | tf_op jit(solution)/shard_map/ppermute | solution.py:391
  61.4 11.2 %collective-permute-start.9 = (f32[2,128,128]{2,1,0:T(8,128)S(1)}, f32[2,128,128]{2,1,0:T(8,128)S(1)}, u32[]{:S(2)}, u32[]{:S(2)}) collective-permute-start(f32[2,128,128]{2,1,0:T(8,128)S(1)} %shard_map.64.middle), channel_id=1, source_target_pairs={{0,72},{24,48},{48,24},{72,0},{96,168},{120,144},{144,120},{168,96... | collective-permute-start | bytes 393224 | tf_op jit(solution)/shard_map/ppermute | solution.py:391

commit v6 on v5

--- a/solution.py
+++ b/solution.py
@@ -179,10 +179,7 @@
                 to_wrap[0] = value
 
 
-def early_kernel(
-    meta, x, near, across, opposite, to_wrap, handed, square, cube, wrap_message, third_message
-):
-    wrap_message[...] = to_wrap[...]
+def early_kernel(meta, x, near, across, opposite, handed, square, cube, third_message):
     third_message[...] = handed[...]
     square[...] = jnp.zeros_like(square)
     cube[...] = jnp.zeros_like(cube)
@@ -446,14 +443,14 @@
     )
     ring_right = to_col(left_message, -1)
     ring_left = to_col(right_message, 1)
-    early, early_part, wrap_message, handed = call(
+    wrap_b = to_wrap(wrap_message)
+    early, early_part, handed = call(
         early_kernel,
-        [block(2, SLOTS), block(2, SLOTS), block(1), block(2)],
-        *(meta, x, near, across, opposite, wrap_message, handed),
+        [block(2, SLOTS), block(2, SLOTS), block(2)],
+        *(meta, x, near, across, opposite, handed),
         smem=1,
         flops=60 * 2 * BS**3,
     )
-    wrap_b = to_wrap(wrap_message)
     third_d = flip_row(handed, GY)
     middle = call(
         middle_kernel,

time: 75.6 us -> 73.3 us (0.970)
  waiting for transfers between devices: 2.32 us -> 0.03 us
  blocking collectives: 8.47 us -> 9.25 us
    ppermute x7, waiting for transfers between devices: 2.31 us -> 0.02 us  [along(): lax.ppermute(value, axis, [(i, target(i) % count) for i in range(count)])]
    ppermute x4, starting transfers between devices: 22.7 us -> 21.5 us  [anywhere(): return lax.ppermute(value, ('row', 'col'), pairs)]
    ppermute x7, starting transfers between devices: 27.2 us -> 28.4 us  [along(): lax.ppermute(value, axis, [(i, target(i) % count) for i in range(count)])]
    all_gather x3, blocking collectives: 8.47 us -> 9.25 us  [both_cores(): return lax.all_gather(value, 'row', axis_index_groups=groups)]
  transfers between devices with their start and end apart: 11 -> 11, of which waited for: 1 -> 0; matrix products, arithmetic and copies ran while one was open for 0% -> 0% of each run, Pallas kernels for 13% -> 13%
where the time goes in v6:
time: 73.3 us; the launch traced here: 72.8 us
  starting transfers between devices  49.8 us (68%)
  Pallas kernels  11.5 us (16%)
  blocking collectives  9.25 us (13%)
  local copies, waits for them, and re-layouts  1.15 us (2%)
  between operations  0.87 us (1%)
    ppermute x7, starting transfers between devices, along(): lax.ppermute(value, axis, [(i, target(i) % count) for i in range(count)])  28.4 us
    ppermute x4, starting transfers between devices, anywhere(): return lax.ppermute(value, ('row', 'col'), pairs)  21.5 us
    pallas_call x8, Pallas kernels, call(): pl.pallas_call(kernel, out_shape=out_shapes, in_specs=[pl.BlockSpec(memor...  11.5 us
    all_gather x3, blocking collectives, both_cores(): return lax.all_gather(value, 'row', axis_index_groups=groups)  9.25 us
  transfers between devices with their start and end apart: 11, of which 0 were waited for; matrix products, arithmetic and copies ran while one was open for 0% of the time, Pallas kernels for 13%

profile of v6, /device:TPU:1, one launch (start us, length us, event | category | flops | bytes accessed | tf_op | source)
XLA Modules:
  0.0 72.8 jit_solution(5285097996953858294)
XLA Ops:
  0.6 1.1 %slice_bitcast_fusion.3 = (f32[2,128,128]{2,1,0:T(8,128)S(1)}, f32[1,2,128,128]{3,2,1,0:T(8,128)S(1)}, f32[1,2,128,128]{3,2,1,0:T(8,128)S(1)}, f32[2,128,128]{2,1,0:T(8,128)S(1)}) fusion(f32[2,4,128,128]{3,2,1,0:T(8,128)} %x.11), kind=kLoop, calls=%fused_computation.4 | loop fusion | bytes 917504 | tf_op jit(solution)/shard_map/squeeze | solution.py:426
  1.8 4.8 %collective-permute-start = (f32[2,2,128,128]{3,2,1,0:T(8,128)S(1)}, f32[2,2,128,128]{3,2,1,0:T(8,128)S(1)}, u32[]{:S(2)}, u32[]{:S(2)}) collective-permute-start(f32[2,2,128,128]{3,2,1,0:T(8,128)S(1)} %pad_maximum_fusion), channel_id=1, source_target_pairs={{0,48},{24,72},{48,0},{72,24},{96,144},{120,168},{144,96},{168,120... | collective-permute-start | bytes 786440 | tf_op jit(solution)/shard_map/ppermute | solution.py:388
  6.6 5.8 %collective-permute-start.2 = (f32[2,128,128]{2,1,0:T(8,128)S(1)}, f32[2,128,128]{2,1,0:T(8,128)S(1)}, u32[]{:S(2)}, u32[]{:S(2)}) collective-permute-start(f32[2,128,128]{2,1,0:T(8,128)S(1)} %get-tuple-element.27), channel_id=1, source_target_pairs={{0,96},{24,120},{48,144},{72,168},{96,192},{120,216},{144,240},{16... | collective-permute-start | bytes 393224 | tf_op jit(solution)/shard_map/ppermute | solution.py:388
  12.5 4.1 %collective-permute-start.1 = (f32[2,128,128]{2,1,0:T(8,128)S(1)}, f32[2,128,128]{2,1,0:T(8,128)S(1)}, u32[]{:S(2)}, u32[]{:S(2)}) collective-permute-start(f32[2,128,128]{2,1,0:T(8,128)S(1)} %get-tuple-element.27), channel_id=1, source_target_pairs={{0,672},{24,696},{48,720},{72,744},{96,0},{120,24},{144,48},{168,7... | collective-permute-start | bytes 393224 | tf_op jit(solution)/shard_map/ppermute | solution.py:388
  16.6 2.5 %collective-permute-start.3 = (f32[2,128,128]{2,1,0:T(8,128)S(1)}, f32[2,128,128]{2,1,0:T(8,128)S(1)}, u32[]{:S(2)}, u32[]{:S(2)}) collective-permute-start(f32[2,128,128]{2,1,0:T(8,128)S(1)} %get-tuple-element.24), channel_id=1, source_target_pairs={{0,576},{24,600},{48,624},{72,648},{96,288},{120,312},{144,336},{1... | collective-permute-start | bytes 393224 | tf_op jit(solution)/shard_map/ppermute | solution.py:388
  19.1 0.1 pad_add_fusion.place_ref.place
  19.1 0.0 collective-permute-done.opposite.arrived
  19.1 0.6 shard_map.62
  19.7 0.0 copy-start.1
  19.7 0.0 copy-start.2
  19.7 15.5 %collective-permute-start.6 = (f32[3,128,128]{2,1,0:T(8,128)S(1)}, f32[3,128,128]{2,1,0:T(8,128)S(1)}, u32[]{:S(2)}, u32[]{:S(2)}) collective-permute-start(f32[3,128,128]{2,1,0:T(8,128)S(1)} %shard_map.62), channel_id=1, source_target_pairs={{0,23},{7,8},{8,7},{15,16},{16,15},{23,0},{24,47},{31,32},{32,31},... | collective-permute-start | bytes 589832 | tf_op jit(solution)/shard_map/ppermute | solution.py:396
  35.2 0.0 copy-start.3
  35.2 3.9 %all-gather = f32[4,2,128,128]{3,2,1,0:T(8,128)S(1)} all-gather(f32[2,2,128,128]{3,2,1,0:T(8,128)S(1)} %pad_maximum_fusion), channel_id=2, replica_groups={{0,24},{48,72},{96,120},{144,168},{192,216},{240,264},{288,312},{336,36..., dimensions={0}, use_global_device_ids=true | all-gather | bytes 786432 | tf_op jit(solution)/shard_map/all_gather | solution.py:415
  39.1 3.0 %shard_map.59.meta = s32[2,27]{1,0:T(2,128)S(1)} custom-call(s32[2]{0:T(128)S(1)} %pad_add_fusion.place_ref.place, s32[4,1536]{1,0:T(4,128)S(1)} %bitcast.28, s32[6,1536]{1,0:T(8,128)S(1)} %bitcast.27, s32[1536]{0:T(1024)S(1)} %copy-done.3), custom_call_target="tpu_custom_call" | custom-call | bytes 2097152 | tf_op jit(solution)/shard_map/pallas_call | solution.py:373
  42.1 2.2 %all-gather.1 = f32[4,2,128,128]{3,2,1,0:T(8,128)S(1)} all-gather(f32[2,2,128,128]{3,2,1,0:T(8,128)S(1)} %collective-permute-done.opposite.arrived), channel_id=3, replica_groups={{0,24},{48,72},{96,120},{144,168},{192,216},{240,264},{288,312},{336,36..., dimensions={0}, use_global_device_ids=true | all-gather | bytes 786432 | tf_op jit(solution)/shard_map/all_gather | solution.py:415
  44.3 0.0 collective-permute-done.3.relayed
  44.3 0.0 collective-permute-done.2.below
  44.3 0.0 collective-permute-done.1.above
  44.3 0.9 %shard_map.60 = (f32[2,128,128]{2,1,0:T(8,128)S(1)}, f32[2,128,128]{2,1,0:T(8,128)S(1)}, f32[4,128,128]{2,1,0:T(8,128)S(1)}, f32[3,128,128]{2,1,0:T(8,128)S(1)},...) custom-call(s32[2,27]{1,0:T(2,128)S(1)} %shard_map.59.meta, f32[2,4,128,128]{3,2,1,0:T(8,128)S(1)} %copy-done, ...), custom_call_target="tpu_custom_call" | custom-call | flops 100663296 | bytes 2097152 | tf_op jit(solution)/shard_map/pallas_call | solution.py:373
  45.2 1.3 %collective-permute-start.5 = (f32[4,128,128]{2,1,0:T(8,128)S(1)}, f32[4,128,128]{2,1,0:T(8,128)S(1)}, u32[]{:S(2)}, u32[]{:S(2)}) collective-permute-start(f32[4,128,128]{2,1,0:T(8,128)S(1)} %get-tuple-element.18), channel_id=1, source_target_pairs={{1,0},{2,1},{3,2},{4,3},{5,4},{6,5},{7,6},{9,8},{10,9},{11,10},{12... | collective-permute-start | bytes 786440 | tf_op jit(solution)/shard_map/ppermute | solution.py:396
  46.5 2.1 %collective-permute-start.7 = (f32[1,128,128]{2,1,0:T(8,128)S(1)}, f32[1,128,128]{2,1,0:T(8,128)S(1)}, u32[]{:S(2)}, u32[]{:S(2)}) collective-permute-start(f32[1,128,128]{2,1,0:T(8,128)S(1)} %get-tuple-element.19), channel_id=1, source_target_pairs={{0,23},{7,8},{8,7},{15,16},{16,15},{23,0},{24,47},{31,32},{32,31},... | collective-permute-start | bytes 196616 | tf_op jit(solution)/shard_map/ppermute | solution.py:396
  48.6 2.6 %collective-permute-start.4 = (f32[3,128,128]{2,1,0:T(8,128)S(1)}, f32[3,128,128]{2,1,0:T(8,128)S(1)}, u32[]{:S(2)}, u32[]{:S(2)}) collective-permute-start(f32[3,128,128]{2,1,0:T(8,128)S(1)} %get-tuple-element.17), channel_id=1, source_target_pairs={{0,1},{1,2},{2,3},{3,4},{4,5},{5,6},{6,7},{8,9},{9,10},{10,11},{11... | collective-permute-start | bytes 589832 | tf_op jit(solution)/shard_map/ppermute | solution.py:396
  51.2 1.6 %shard_map.61 = (f32[2,6,128,128]{3,2,1,0:T(8,128)S(1)}, f32[2,6,128,128]{3,2,1,0:T(8,128)S(1)}, f32[2,128,128]{2,1,0:T(8,128)S(1)}) custom-call(s32[2,27]{1,0:T(2,128)S(1)} %shard_map.59.meta, f32[2,4,128,128]{3,2,1,0:T(8,128)S(1)} %copy-done, f32[2,2,2,128,128]{4,3,2,1,0:T(8,128)S(1)} %bitcast.23, f32[2,2,2,128,128]{4,3,2,1,0:T(8,128)S(1)} %bitcast.25, ...), custom_call_target="tpu_custom_call" | custom-call | flops 251658240 | bytes 2097152 | tf_op jit(solution)/shard_map/pallas_call | solution.py:373
  52.8 1.9 %collective-permute-start.8 = (f32[2,128,128]{2,1,0:T(8,128)S(1)}, f32[2,128,128]{2,1,0:T(8,128)S(1)}, u32[]{:S(2)}, u32[]{:S(2)}) collective-permute-start(f32[2,128,128]{2,1,0:T(8,128)S(1)} %get-tuple-element.21), channel_id=1, source_target_pairs={{0,96},{24,120},{48,144},{72,168},{96,0},{120,24},{144,48},{168,72... | collective-permute-start | bytes 393224 | tf_op jit(solution)/shard_map/ppermute | solution.py:388
  54.8 0.0 collective-permute-done.6.given
  54.8 0.0 collective-permute-done.5.ring_right
  54.8 0.8 %shard_map.64.middle = f32[2,128,128]{2,1,0:T(8,128)S(1)} custom-call(s32[2,27]{1,0:T(2,128)S(1)} %shard_map.59.meta, f32[2,4,128,128]{3,2,1,0:T(8,128)S(1)} %copy-done, f32[2,128,128]{2,1,0:T(8,128)S(1)} %get-tuple-element.16.base, f32[3,128,128]{2,1,0:T(8,128)S(1)} %collective-permute-done.4.ring_left, ...), custom_call_target="tpu_custom_call" | custom-call | flops 25165824 | bytes 2097152 | tf_op jit(solution)/shard_map/pallas_call | solution.py:373
  55.6 4.5 %collective-permute-start.10 = (f32[2,128,128]{2,1,0:T(8,128)S(1)}, f32[2,128,128]{2,1,0:T(8,128)S(1)}, u32[]{:S(2)}, u32[]{:S(2)}) collective-permute-start(f32[2,128,128]{2,1,0:T(8,128)S(1)} %shard_map.64.middle), channel_id=1, source_target_pairs={{0,672},{24,696},{48,720},{72,744},{96,0},{120,24},{144,48},{168,7... | collective-permute-start | bytes 393224 | tf_op jit(solution)/shard_map/ppermute | solution.py:388
  60.1 4.7 %collective-permute-start.9 = (f32[2,128,128]{2,1,0:T(8,128)S(1)}, f32[2,128,128]{2,1,0:T(8,128)S(1)}, u32[]{:S(2)}, u32[]{:S(2)}) collective-permute-start(f32[2,128,128]{2,1,0:T(8,128)S(1)} %shard_map.64.middle), channel_id=1, source_target_pairs={{0,72},{24,48},{48,24},{72,0},{96,168},{120,144},{144,120},{168,96... | collective-permute-start | bytes 393224 | tf_op jit(solution)/shard_map/ppermute | solution.py:388
  64.9 2.9 %shard_map.65 = (f32[2,6,128,128]{3,2,1,0:T(8,128)}, f32[2,6,128,128]{3,2,1,0:T(8,128)S(1)}) custom-call(s32[2,27]{1,0:T(2,128)S(1)} %shard_map.59.meta, f32[2,4,128,128]{3,2,1,0:T(8,128)S(1)} %copy-done, f32[2,6,128,128]{3,2,1,0:T(8,128)S(1)} %get-tuple-element.14.early, f32[2,6,128,128]{3,2,1,0:T(8,128)S(1)} %get-tuple-element.15.early_part, ...), custom_call_target="tpu_custom_call" | custom-call | flops 251658240 | bytes 2097152 | tf_op jit(solution)/shard_map/pallas_call | solution.py:373
  67.8 3.2 %all-gather.2 = f32[4,128,128]{2,1,0:T(8,128)S(1)} all-gather(f32[2,128,128]{2,1,0:T(8,128)S(1)} %shard_map.64.middle), channel_id=4, replica_groups={{0,24},{48,72},{96,120},{144,168},{192,216},{240,264},{288,312},{336,36..., dimensions={0}, use_global_device_ids=true | all-gather | bytes 393216 | tf_op jit(solution)/shard_map/all_gather | solution.py:415
  70.9 1.8 %shard_map.66 = f32[2,6,128,128]{3,2,1,0:T(8,128)} custom-call(s32[2,27]{1,0:T(2,128)S(1)} %shard_map.59.meta, f32[2,4,128,128]{3,2,1,0:T(8,128)S(1)} %copy-done, f32[2,6,128,128]{3,2,1,0:T(8,128)S(1)} %get-tuple-element.23.part, f32[2,2,128,128]{3,2,1,0:T(8,128)S(1)} %bitcast.26, f32[2,128,128]{2,1,0:T(8,128)S(1)} %collective-permute-done.9.mid_across, ...), custom_call_target="tpu_custom_call" | custom-call | flops 50331648 | bytes 2097152 | tf_op jit(solution)/shard_map/pallas_call | solution.py:373
  (12 shorter events, 0.1 us)
Async XLA Ops:
  0.6 18.5 %copy-start = (f32[2,4,128,128]{3,2,1,0:T(8,128)S(1)}, f32[2,4,128,128]{3,2,1,0:T(8,128)}, u32[]{:S(2)}) copy-start(f32[2,4,128,128]{3,2,1,0:T(8,128)} %x.11) | copy-start | bytes 1572868
  1.8 17.3 %collective-permute-start = (f32[2,2,128,128]{3,2,1,0:T(8,128)S(1)}, f32[2,2,128,128]{3,2,1,0:T(8,128)S(1)}, u32[]{:S(2)}, u32[]{:S(2)}) collective-permute-start(f32[2,2,128,128]{3,2,1,0:T(8,128)S(1)} %pad_maximum_fusion), channel_id=1, source_target_pairs={{0,48},{24,72},{48,0},{72,24},{96,144},{120,168},{144,96},{168,120... | collective-permute-start | bytes 786440 | tf_op jit(solution)/shard_map/ppermute | solution.py:388
  6.6 37.7 %collective-permute-start.2 = (f32[2,128,128]{2,1,0:T(8,128)S(1)}, f32[2,128,128]{2,1,0:T(8,128)S(1)}, u32[]{:S(2)}, u32[]{:S(2)}) collective-permute-start(f32[2,128,128]{2,1,0:T(8,128)S(1)} %get-tuple-element.27), channel_id=1, source_target_pairs={{0,96},{24,120},{48,144},{72,168},{96,192},{120,216},{144,240},{16... | collective-permute-start | bytes 393224 | tf_op jit(solution)/shard_map/ppermute | solution.py:388
  12.5 31.9 %collective-permute-start.1 = (f32[2,128,128]{2,1,0:T(8,128)S(1)}, f32[2,128,128]{2,1,0:T(8,128)S(1)}, u32[]{:S(2)}, u32[]{:S(2)}) collective-permute-start(f32[2,128,128]{2,1,0:T(8,128)S(1)} %get-tuple-element.27), channel_id=1, source_target_pairs={{0,672},{24,696},{48,720},{72,744},{96,0},{120,24},{144,48},{168,7... | collective-permute-start | bytes 393224 | tf_op jit(solution)/shard_map/ppermute | solution.py:388
  16.6 27.7 %collective-permute-start.3 = (f32[2,128,128]{2,1,0:T(8,128)S(1)}, f32[2,128,128]{2,1,0:T(8,128)S(1)}, u32[]{:S(2)}, u32[]{:S(2)}) collective-permute-start(f32[2,128,128]{2,1,0:T(8,128)S(1)} %get-tuple-element.24), channel_id=1, source_target_pairs={{0,576},{24,600},{48,624},{72,648},{96,288},{120,312},{144,336},{1... | collective-permute-start | bytes 393224 | tf_op jit(solution)/shard_map/ppermute | solution.py:388
  19.7 19.4 %copy-start.1 = (s32[1536,6]{0,1:T(8,128)S(1)}, s32[1536,6]{0,1:T(8,128)}, u32[]{:S(2)}) copy-start(s32[1536,6]{0,1:T(8,128)} %param.6) | copy-start | bytes 110596
  19.7 19.4 %copy-start.2 = (s32[1536,4]{0,1:T(4,128)S(1)}, s32[1536,4]{0,1:T(4,128)}, u32[]{:S(2)}) copy-start(s32[1536,4]{0,1:T(4,128)} %param.5) | copy-start | bytes 73732
  19.7 35.0 %collective-permute-start.6 = (f32[3,128,128]{2,1,0:T(8,128)S(1)}, f32[3,128,128]{2,1,0:T(8,128)S(1)}, u32[]{:S(2)}, u32[]{:S(2)}) collective-permute-start(f32[3,128,128]{2,1,0:T(8,128)S(1)} %shard_map.62), channel_id=1, source_target_pairs={{0,23},{7,8},{8,7},{15,16},{16,15},{23,0},{24,47},{31,32},{32,31},... | collective-permute-start | bytes 589832 | tf_op jit(solution)/shard_map/ppermute | solution.py:396
  35.2 3.9 %copy-start.3 = (s32[1536]{0:T(1024)S(1)}, s32[1536]{0:T(1024)}, u32[]{:S(2)}) copy-start(s32[1536]{0:T(1024)} %count_ref.1) | copy-start | bytes 18436
  45.2 9.6 %collective-permute-start.5 = (f32[4,128,128]{2,1,0:T(8,128)S(1)}, f32[4,128,128]{2,1,0:T(8,128)S(1)}, u32[]{:S(2)}, u32[]{:S(2)}) collective-permute-start(f32[4,128,128]{2,1,0:T(8,128)S(1)} %get-tuple-element.18), channel_id=1, source_target_pairs={{1,0},{2,1},{3,2},{4,3},{5,4},{6,5},{7,6},{9,8},{10,9},{11,10},{12... | collective-permute-start | bytes 786440 | tf_op jit(solution)/shard_map/ppermute | solution.py:396
  46.5 18.4 %collective-permute-start.7 = (f32[1,128,128]{2,1,0:T(8,128)S(1)}, f32[1,128,128]{2,1,0:T(8,128)S(1)}, u32[]{:S(2)}, u32[]{:S(2)}) collective-permute-start(f32[1,128,128]{2,1,0:T(8,128)S(1)} %get-tuple-element.19), channel_id=1, source_target_pairs={{0,23},{7,8},{8,7},{15,16},{16,15},{23,0},{24,47},{31,32},{32,31},... | collective-permute-start | bytes 196616 | tf_op jit(solution)/shard_map/ppermute | solution.py:396
  48.6 6.2 %collective-permute-start.4 = (f32[3,128,128]{2,1,0:T(8,128)S(1)}, f32[3,128,128]{2,1,0:T(8,128)S(1)}, u32[]{:S(2)}, u32[]{:S(2)}) collective-permute-start(f32[3,128,128]{2,1,0:T(8,128)S(1)} %get-tuple-element.17), channel_id=1, source_target_pairs={{0,1},{1,2},{2,3},{3,4},{4,5},{5,6},{6,7},{8,9},{9,10},{10,11},{11... | collective-permute-start | bytes 589832 | tf_op jit(solution)/shard_map/ppermute | solution.py:396
  52.8 12.1 %collective-permute-start.8 = (f32[2,128,128]{2,1,0:T(8,128)S(1)}, f32[2,128,128]{2,1,0:T(8,128)S(1)}, u32[]{:S(2)}, u32[]{:S(2)}) collective-permute-start(f32[2,128,128]{2,1,0:T(8,128)S(1)} %get-tuple-element.21), channel_id=1, source_target_pairs={{0,96},{24,120},{48,144},{72,168},{96,0},{120,24},{144,48},{168,72... | collective-permute-start | bytes 393224 | tf_op jit(solution)/shard_map/ppermute | solution.py:388
  55.6 15.3 %collective-permute-start.10 = (f32[2,128,128]{2,1,0:T(8,128)S(1)}, f32[2,128,128]{2,1,0:T(8,128)S(1)}, u32[]{:S(2)}, u32[]{:S(2)}) collective-permute-start(f32[2,128,128]{2,1,0:T(8,128)S(1)} %shard_map.64.middle), channel_id=1, source_target_pairs={{0,672},{24,696},{48,720},{72,744},{96,0},{120,24},{144,48},{168,7... | collective-permute-start | bytes 393224 | tf_op jit(solution)/shard_map/ppermute | solution.py:388
  60.1 10.8 %collective-permute-start.9 = (f32[2,128,128]{2,1,0:T(8,128)S(1)}, f32[2,128,128]{2,1,0:T(8,128)S(1)}, u32[]{:S(2)}, u32[]{:S(2)}) collective-permute-start(f32[2,128,128]{2,1,0:T(8,128)S(1)} %shard_map.64.middle), channel_id=1, source_target_pairs={{0,72},{24,48},{48,24},{72,0},{96,168},{120,144},{144,120},{168,96... | collective-permute-start | bytes 393224 | tf_op jit(solution)/shard_map/ppermute | solution.py:388

commit v7 on v6

--- a/solution.py
+++ b/solution.py
@@ -274,7 +274,7 @@
 ):
     wraps = (wrap_a, wrap_b)
     square[...] = early[...]
-    cube[...] = early_part[...]
+    del early_part
     results = []
     for r in range(2):
         flag, _ = row_view(meta, r)
@@ -366,13 +366,14 @@
             cube[r, slot(UP3)] += above
 
 
-def call(kernel, out_shapes, *operands, smem=0, free=0, smem_out=False, flops=0):
+def call(kernel, out_shapes, *operands, smem=0, free=0, smem_out=False, flops=0, aliases=()):
     held = len(operands) - smem - free
     spaces = [pltpu.SMEM] * smem + [pltpu.VMEM] * held + [pl.ANY] * free
     out_space = pltpu.SMEM if smem_out else pltpu.VMEM
     return pl.pallas_call(
         kernel,
         out_shape=out_shapes,
+        input_output_aliases=dict(aliases),
         in_specs=[pl.BlockSpec(memory_space=s) for s in spaces],
         out_specs=jax.tree.map(lambda _: pl.BlockSpec(memory_space=out_space), out_shapes),
         compiler_params=pltpu.CompilerParams(vmem_limit_bytes=32 * 2**20),
@@ -468,6 +469,7 @@
         *(meta, x, early, early_part, middle, ring_left, ring_right),
         *(wrap_a, wrap_b, third, third_d),
         smem=1,
+        aliases=((3, 1),),
         flops=60 * 2 * BS**3,
     )
     cube = call(

time: 73.3 us -> 73.3 us (level)
  no operation moved by 1% of the time
where the time goes in v7:
time: 73.3 us; the launch traced here: 72.8 us
  starting transfers between devices  49.9 us (68%)
  Pallas kernels  11.5 us (16%)
  blocking collectives  9.24 us (13%)
  local copies, waits for them, and re-layouts  1.15 us (2%)
  between operations  0.87 us (1%)
    ppermute x7, starting transfers between devices, along(): lax.ppermute(value, axis, [(i, target(i) % count) for i in range(count)])  28.4 us
    ppermute x4, starting transfers between devices, anywhere(): return lax.ppermute(value, ('row', 'col'), pairs)  21.5 us
    pallas_call x8, Pallas kernels, call(): pl.pallas_call(kernel, out_shape=out_shapes, input_output_aliases=dict(al...  11.5 us
    all_gather x3, blocking collectives, both_cores(): return lax.all_gather(value, 'row', axis_index_groups=groups)  9.24 us
  transfers between devices with their start and end apart: 11, of which 0 were waited for; matrix products, arithmetic and copies ran while one was open for 0% of the time, Pallas kernels for 13%

profile of v7, /device:TPU:1, one launch (start us, length us, event | category | flops | bytes accessed | tf_op | source)
XLA Modules:
  0.0 72.8 jit_solution(5414865582168318899)
XLA Ops:
  0.6 1.1 %slice_bitcast_fusion.3 = (f32[2,128,128]{2,1,0:T(8,128)S(1)}, f32[1,2,128,128]{3,2,1,0:T(8,128)S(1)}, f32[1,2,128,128]{3,2,1,0:T(8,128)S(1)}, f32[2,128,128]{2,1,0:T(8,128)S(1)}) fusion(f32[2,4,128,128]{3,2,1,0:T(8,128)} %x.11), kind=kLoop, calls=%fused_computation.4 | loop fusion | bytes 917504 | tf_op jit(solution)/shard_map/squeeze | solution.py:427
  1.8 4.8 %collective-permute-start = (f32[2,2,128,128]{3,2,1,0:T(8,128)S(1)}, f32[2,2,128,128]{3,2,1,0:T(8,128)S(1)}, u32[]{:S(2)}, u32[]{:S(2)}) collective-permute-start(f32[2,2,128,128]{3,2,1,0:T(8,128)S(1)} %pad_maximum_fusion), channel_id=1, source_target_pairs={{0,48},{24,72},{48,0},{72,24},{96,144},{120,168},{144,96},{168,120... | collective-permute-start | bytes 786440 | tf_op jit(solution)/shard_map/ppermute | solution.py:389
  6.6 5.8 %collective-permute-start.2 = (f32[2,128,128]{2,1,0:T(8,128)S(1)}, f32[2,128,128]{2,1,0:T(8,128)S(1)}, u32[]{:S(2)}, u32[]{:S(2)}) collective-permute-start(f32[2,128,128]{2,1,0:T(8,128)S(1)} %get-tuple-element.27), channel_id=1, source_target_pairs={{0,96},{24,120},{48,144},{72,168},{96,192},{120,216},{144,240},{16... | collective-permute-start | bytes 393224 | tf_op jit(solution)/shard_map/ppermute | solution.py:389
  12.5 4.1 %collective-permute-start.1 = (f32[2,128,128]{2,1,0:T(8,128)S(1)}, f32[2,128,128]{2,1,0:T(8,128)S(1)}, u32[]{:S(2)}, u32[]{:S(2)}) collective-permute-start(f32[2,128,128]{2,1,0:T(8,128)S(1)} %get-tuple-element.27), channel_id=1, source_target_pairs={{0,672},{24,696},{48,720},{72,744},{96,0},{120,24},{144,48},{168,7... | collective-permute-start | bytes 393224 | tf_op jit(solution)/shard_map/ppermute | solution.py:389
  16.6 2.5 %collective-permute-start.3 = (f32[2,128,128]{2,1,0:T(8,128)S(1)}, f32[2,128,128]{2,1,0:T(8,128)S(1)}, u32[]{:S(2)}, u32[]{:S(2)}) collective-permute-start(f32[2,128,128]{2,1,0:T(8,128)S(1)} %get-tuple-element.24), channel_id=1, source_target_pairs={{0,576},{24,600},{48,624},{72,648},{96,288},{120,312},{144,336},{1... | collective-permute-start | bytes 393224 | tf_op jit(solution)/shard_map/ppermute | solution.py:389
  19.1 0.1 pad_add_fusion.place_ref.place
  19.1 0.0 collective-permute-done.opposite.arrived
  19.1 0.6 shard_map.62
  19.7 0.0 copy-start.1
  19.7 0.0 copy-start.2
  19.7 15.5 %collective-permute-start.6 = (f32[3,128,128]{2,1,0:T(8,128)S(1)}, f32[3,128,128]{2,1,0:T(8,128)S(1)}, u32[]{:S(2)}, u32[]{:S(2)}) collective-permute-start(f32[3,128,128]{2,1,0:T(8,128)S(1)} %shard_map.62), channel_id=1, source_target_pairs={{0,23},{7,8},{8,7},{15,16},{16,15},{23,0},{24,47},{31,32},{32,31},... | collective-permute-start | bytes 589832 | tf_op jit(solution)/shard_map/ppermute | solution.py:397
  35.2 0.0 copy-start.3
  35.2 3.9 %all-gather = f32[4,2,128,128]{3,2,1,0:T(8,128)S(1)} all-gather(f32[2,2,128,128]{3,2,1,0:T(8,128)S(1)} %pad_maximum_fusion), channel_id=2, replica_groups={{0,24},{48,72},{96,120},{144,168},{192,216},{240,264},{288,312},{336,36..., dimensions={0}, use_global_device_ids=true | all-gather | bytes 786432 | tf_op jit(solution)/shard_map/all_gather | solution.py:416
  39.1 3.0 %shard_map.59.meta = s32[2,27]{1,0:T(2,128)S(1)} custom-call(s32[2]{0:T(128)S(1)} %pad_add_fusion.place_ref.place, s32[4,1536]{1,0:T(4,128)S(1)} %bitcast.28, s32[6,1536]{1,0:T(8,128)S(1)} %bitcast.27, s32[1536]{0:T(1024)S(1)} %copy-done.3), custom_call_target="tpu_custom_call" | custom-call | bytes 2097152 | tf_op jit(solution)/shard_map/pallas_call | solution.py:373
  42.1 2.2 %all-gather.1 = f32[4,2,128,128]{3,2,1,0:T(8,128)S(1)} all-gather(f32[2,2,128,128]{3,2,1,0:T(8,128)S(1)} %collective-permute-done.opposite.arrived), channel_id=3, replica_groups={{0,24},{48,72},{96,120},{144,168},{192,216},{240,264},{288,312},{336,36..., dimensions={0}, use_global_device_ids=true | all-gather | bytes 786432 | tf_op jit(solution)/shard_map/all_gather | solution.py:416
  44.3 0.0 collective-permute-done.3.relayed
  44.3 0.0 collective-permute-done.2.below
  44.3 0.0 collective-permute-done.1.above
  44.3 0.9 %shard_map.60 = (f32[2,128,128]{2,1,0:T(8,128)S(1)}, f32[2,128,128]{2,1,0:T(8,128)S(1)}, f32[4,128,128]{2,1,0:T(8,128)S(1)}, f32[3,128,128]{2,1,0:T(8,128)S(1)},...) custom-call(s32[2,27]{1,0:T(2,128)S(1)} %shard_map.59.meta, f32[2,4,128,128]{3,2,1,0:T(8,128)S(1)} %copy-done, ...), custom_call_target="tpu_custom_call" | custom-call | flops 100663296 | bytes 2097152 | tf_op jit(solution)/shard_map/pallas_call | solution.py:373
  45.2 1.3 %collective-permute-start.5 = (f32[4,128,128]{2,1,0:T(8,128)S(1)}, f32[4,128,128]{2,1,0:T(8,128)S(1)}, u32[]{:S(2)}, u32[]{:S(2)}) collective-permute-start(f32[4,128,128]{2,1,0:T(8,128)S(1)} %get-tuple-element.18), channel_id=1, source_target_pairs={{1,0},{2,1},{3,2},{4,3},{5,4},{6,5},{7,6},{9,8},{10,9},{11,10},{12... | collective-permute-start | bytes 786440 | tf_op jit(solution)/shard_map/ppermute | solution.py:397
  46.5 2.1 %collective-permute-start.7 = (f32[1,128,128]{2,1,0:T(8,128)S(1)}, f32[1,128,128]{2,1,0:T(8,128)S(1)}, u32[]{:S(2)}, u32[]{:S(2)}) collective-permute-start(f32[1,128,128]{2,1,0:T(8,128)S(1)} %get-tuple-element.19), channel_id=1, source_target_pairs={{0,23},{7,8},{8,7},{15,16},{16,15},{23,0},{24,47},{31,32},{32,31},... | collective-permute-start | bytes 196616 | tf_op jit(solution)/shard_map/ppermute | solution.py:397
  48.6 2.6 %collective-permute-start.4 = (f32[3,128,128]{2,1,0:T(8,128)S(1)}, f32[3,128,128]{2,1,0:T(8,128)S(1)}, u32[]{:S(2)}, u32[]{:S(2)}) collective-permute-start(f32[3,128,128]{2,1,0:T(8,128)S(1)} %get-tuple-element.17), channel_id=1, source_target_pairs={{0,1},{1,2},{2,3},{3,4},{4,5},{5,6},{6,7},{8,9},{9,10},{10,11},{11... | collective-permute-start | bytes 589832 | tf_op jit(solution)/shard_map/ppermute | solution.py:397
  51.2 1.6 %shard_map.61 = (f32[2,6,128,128]{3,2,1,0:T(8,128)S(1)}, f32[2,6,128,128]{3,2,1,0:T(8,128)S(1)}, f32[2,128,128]{2,1,0:T(8,128)S(1)}) custom-call(s32[2,27]{1,0:T(2,128)S(1)} %shard_map.59.meta, f32[2,4,128,128]{3,2,1,0:T(8,128)S(1)} %copy-done, f32[2,2,2,128,128]{4,3,2,1,0:T(8,128)S(1)} %bitcast.23, f32[2,2,2,128,128]{4,3,2,1,0:T(8,128)S(1)} %bitcast.25, ...), custom_call_target="tpu_custom_call" | custom-call | flops 251658240 | bytes 2097152 | tf_op jit(solution)/shard_map/pallas_call | solution.py:373
  52.8 1.9 %collective-permute-start.8 = (f32[2,128,128]{2,1,0:T(8,128)S(1)}, f32[2,128,128]{2,1,0:T(8,128)S(1)}, u32[]{:S(2)}, u32[]{:S(2)}) collective-permute-start(f32[2,128,128]{2,1,0:T(8,128)S(1)} %get-tuple-element.21), channel_id=1, source_target_pairs={{0,96},{24,120},{48,144},{72,168},{96,0},{120,24},{144,48},{168,72... | collective-permute-start | bytes 393224 | tf_op jit(solution)/shard_map/ppermute | solution.py:389
  54.8 0.0 collective-permute-done.5.ring_right
  54.8 0.8 %shard_map.64.middle = f32[2,128,128]{2,1,0:T(8,128)S(1)} custom-call(s32[2,27]{1,0:T(2,128)S(1)} %shard_map.59.meta, f32[2,4,128,128]{3,2,1,0:T(8,128)S(1)} %copy-done, f32[2,128,128]{2,1,0:T(8,128)S(1)} %get-tuple-element.16.base, f32[3,128,128]{2,1,0:T(8,128)S(1)} %collective-permute-done.4.ring_left, ...), custom_call_target="tpu_custom_call" | custom-call | flops 25165824 | bytes 2097152 | tf_op jit(solution)/shard_map/pallas_call | solution.py:373
  55.6 4.5 %collective-permute-start.10 = (f32[2,128,128]{2,1,0:T(8,128)S(1)}, f32[2,128,128]{2,1,0:T(8,128)S(1)}, u32[]{:S(2)}, u32[]{:S(2)}) collective-permute-start(f32[2,128,128]{2,1,0:T(8,128)S(1)} %shard_map.64.middle), channel_id=1, source_target_pairs={{0,672},{24,696},{48,720},{72,744},{96,0},{120,24},{144,48},{168,7... | collective-permute-start | bytes 393224 | tf_op jit(solution)/shard_map/ppermute | solution.py:389
  60.1 4.8 %collective-permute-start.9 = (f32[2,128,128]{2,1,0:T(8,128)S(1)}, f32[2,128,128]{2,1,0:T(8,128)S(1)}, u32[]{:S(2)}, u32[]{:S(2)}) collective-permute-start(f32[2,128,128]{2,1,0:T(8,128)S(1)} %shard_map.64.middle), channel_id=1, source_target_pairs={{0,72},{24,48},{48,24},{72,0},{96,168},{120,144},{144,120},{168,96... | collective-permute-start | bytes 393224 | tf_op jit(solution)/shard_map/ppermute | solution.py:389
  64.9 2.8 %shard_map.65 = (f32[2,6,128,128]{3,2,1,0:T(8,128)}, f32[2,6,128,128]{3,2,1,0:T(8,128)S(1)}) custom-call(s32[2,27]{1,0:T(2,128)S(1)} %shard_map.59.meta, f32[2,4,128,128]{3,2,1,0:T(8,128)S(1)} %copy-done, f32[2,6,128,128]{3,2,1,0:T(8,128)S(1)} %get-tuple-element.14.early, ...), custom_call_target="tpu_custom_call", output_to_operand_aliasing={{1}: (3, {})} | custom-call | flops 251658240 | bytes 2097152 | tf_op jit(solution)/shard_map/pallas_call | solution.py:373
  67.7 3.2 %all-gather.2 = f32[4,128,128]{2,1,0:T(8,128)S(1)} all-gather(f32[2,128,128]{2,1,0:T(8,128)S(1)} %shard_map.64.middle), channel_id=4, replica_groups={{0,24},{48,72},{96,120},{144,168},{192,216},{240,264},{288,312},{336,36..., dimensions={0}, use_global_device_ids=true | all-gather | bytes 393216 | tf_op jit(solution)/shard_map/all_gather | solution.py:416
  70.9 0.0 collective-permute-done.9.mid_across
  70.9 1.8 %shard_map.66 = f32[2,6,128,128]{3,2,1,0:T(8,128)} custom-call(s32[2,27]{1,0:T(2,128)S(1)} %shard_map.59.meta, f32[2,4,128,128]{3,2,1,0:T(8,128)S(1)} %copy-done, f32[2,6,128,128]{3,2,1,0:T(8,128)S(1)} %get-tuple-element.23.part, f32[2,2,128,128]{3,2,1,0:T(8,128)S(1)} %bitcast.26, f32[2,128,128]{2,1,0:T(8,128)S(1)} %collective-permute-done.9.mid_across, ...), custom_call_target="tpu_custom_call" | custom-call | flops 50331648 | bytes 2097152 | tf_op jit(solution)/shard_map/pallas_call | solution.py:373
  (12 shorter events, 0.1 us)
Async XLA Ops:
  0.6 18.5 %copy-start = (f32[2,4,128,128]{3,2,1,0:T(8,128)S(1)}, f32[2,4,128,128]{3,2,1,0:T(8,128)}, u32[]{:S(2)}) copy-start(f32[2,4,128,128]{3,2,1,0:T(8,128)} %x.11) | copy-start | bytes 1572868
  1.8 17.3 %collective-permute-start = (f32[2,2,128,128]{3,2,1,0:T(8,128)S(1)}, f32[2,2,128,128]{3,2,1,0:T(8,128)S(1)}, u32[]{:S(2)}, u32[]{:S(2)}) collective-permute-start(f32[2,2,128,128]{3,2,1,0:T(8,128)S(1)} %pad_maximum_fusion), channel_id=1, source_target_pairs={{0,48},{24,72},{48,0},{72,24},{96,144},{120,168},{144,96},{168,120... | collective-permute-start | bytes 786440 | tf_op jit(solution)/shard_map/ppermute | solution.py:389
  6.6 37.7 %collective-permute-start.2 = (f32[2,128,128]{2,1,0:T(8,128)S(1)}, f32[2,128,128]{2,1,0:T(8,128)S(1)}, u32[]{:S(2)}, u32[]{:S(2)}) collective-permute-start(f32[2,128,128]{2,1,0:T(8,128)S(1)} %get-tuple-element.27), channel_id=1, source_target_pairs={{0,96},{24,120},{48,144},{72,168},{96,192},{120,216},{144,240},{16... | collective-permute-start | bytes 393224 | tf_op jit(solution)/shard_map/ppermute | solution.py:389
  12.5 31.9 %collective-permute-start.1 = (f32[2,128,128]{2,1,0:T(8,128)S(1)}, f32[2,128,128]{2,1,0:T(8,128)S(1)}, u32[]{:S(2)}, u32[]{:S(2)}) collective-permute-start(f32[2,128,128]{2,1,0:T(8,128)S(1)} %get-tuple-element.27), channel_id=1, source_target_pairs={{0,672},{24,696},{48,720},{72,744},{96,0},{120,24},{144,48},{168,7... | collective-permute-start | bytes 393224 | tf_op jit(solution)/shard_map/ppermute | solution.py:389
  16.6 27.7 %collective-permute-start.3 = (f32[2,128,128]{2,1,0:T(8,128)S(1)}, f32[2,128,128]{2,1,0:T(8,128)S(1)}, u32[]{:S(2)}, u32[]{:S(2)}) collective-permute-start(f32[2,128,128]{2,1,0:T(8,128)S(1)} %get-tuple-element.24), channel_id=1, source_target_pairs={{0,576},{24,600},{48,624},{72,648},{96,288},{120,312},{144,336},{1... | collective-permute-start | bytes 393224 | tf_op jit(solution)/shard_map/ppermute | solution.py:389
  19.7 19.4 %copy-start.1 = (s32[1536,6]{0,1:T(8,128)S(1)}, s32[1536,6]{0,1:T(8,128)}, u32[]{:S(2)}) copy-start(s32[1536,6]{0,1:T(8,128)} %param.6) | copy-start | bytes 110596
  19.7 19.4 %copy-start.2 = (s32[1536,4]{0,1:T(4,128)S(1)}, s32[1536,4]{0,1:T(4,128)}, u32[]{:S(2)}) copy-start(s32[1536,4]{0,1:T(4,128)} %param.5) | copy-start | bytes 73732
  19.7 35.0 %collective-permute-start.6 = (f32[3,128,128]{2,1,0:T(8,128)S(1)}, f32[3,128,128]{2,1,0:T(8,128)S(1)}, u32[]{:S(2)}, u32[]{:S(2)}) collective-permute-start(f32[3,128,128]{2,1,0:T(8,128)S(1)} %shard_map.62), channel_id=1, source_target_pairs={{0,23},{7,8},{8,7},{15,16},{16,15},{23,0},{24,47},{31,32},{32,31},... | collective-permute-start | bytes 589832 | tf_op jit(solution)/shard_map/ppermute | solution.py:397
  35.2 3.9 %copy-start.3 = (s32[1536]{0:T(1024)S(1)}, s32[1536]{0:T(1024)}, u32[]{:S(2)}) copy-start(s32[1536]{0:T(1024)} %count_ref.1) | copy-start | bytes 18436
  45.2 9.6 %collective-permute-start.5 = (f32[4,128,128]{2,1,0:T(8,128)S(1)}, f32[4,128,128]{2,1,0:T(8,128)S(1)}, u32[]{:S(2)}, u32[]{:S(2)}) collective-permute-start(f32[4,128,128]{2,1,0:T(8,128)S(1)} %get-tuple-element.18), channel_id=1, source_target_pairs={{1,0},{2,1},{3,2},{4,3},{5,4},{6,5},{7,6},{9,8},{10,9},{11,10},{12... | collective-permute-start | bytes 786440 | tf_op jit(solution)/shard_map/ppermute | solution.py:397
  46.5 18.4 %collective-permute-start.7 = (f32[1,128,128]{2,1,0:T(8,128)S(1)}, f32[1,128,128]{2,1,0:T(8,128)S(1)}, u32[]{:S(2)}, u32[]{:S(2)}) collective-permute-start(f32[1,128,128]{2,1,0:T(8,128)S(1)} %get-tuple-element.19), channel_id=1, source_target_pairs={{0,23},{7,8},{8,7},{15,16},{16,15},{23,0},{24,47},{31,32},{32,31},... | collective-permute-start | bytes 196616 | tf_op jit(solution)/shard_map/ppermute | solution.py:397
  48.6 6.2 %collective-permute-start.4 = (f32[3,128,128]{2,1,0:T(8,128)S(1)}, f32[3,128,128]{2,1,0:T(8,128)S(1)}, u32[]{:S(2)}, u32[]{:S(2)}) collective-permute-start(f32[3,128,128]{2,1,0:T(8,128)S(1)} %get-tuple-element.17), channel_id=1, source_target_pairs={{0,1},{1,2},{2,3},{3,4},{4,5},{5,6},{6,7},{8,9},{9,10},{10,11},{11... | collective-permute-start | bytes 589832 | tf_op jit(solution)/shard_map/ppermute | solution.py:397
  52.8 12.1 %collective-permute-start.8 = (f32[2,128,128]{2,1,0:T(8,128)S(1)}, f32[2,128,128]{2,1,0:T(8,128)S(1)}, u32[]{:S(2)}, u32[]{:S(2)}) collective-permute-start(f32[2,128,128]{2,1,0:T(8,128)S(1)} %get-tuple-element.21), channel_id=1, source_target_pairs={{0,96},{24,120},{48,144},{72,168},{96,0},{120,24},{144,48},{168,72... | collective-permute-start | bytes 393224 | tf_op jit(solution)/shard_map/ppermute | solution.py:389
  55.6 15.3 %collective-permute-start.10 = (f32[2,128,128]{2,1,0:T(8,128)S(1)}, f32[2,128,128]{2,1,0:T(8,128)S(1)}, u32[]{:S(2)}, u32[]{:S(2)}) collective-permute-start(f32[2,128,128]{2,1,0:T(8,128)S(1)} %shard_map.64.middle), channel_id=1, source_target_pairs={{0,672},{24,696},{48,720},{72,744},{96,0},{120,24},{144,48},{168,7... | collective-permute-start | bytes 393224 | tf_op jit(solution)/shard_map/ppermute | solution.py:389
  60.1 10.8 %collective-permute-start.9 = (f32[2,128,128]{2,1,0:T(8,128)S(1)}, f32[2,128,128]{2,1,0:T(8,128)S(1)}, u32[]{:S(2)}, u32[]{:S(2)}) collective-permute-start(f32[2,128,128]{2,1,0:T(8,128)S(1)} %shard_map.64.middle), channel_id=1, source_target_pairs={{0,72},{24,48},{48,24},{72,0},{96,168},{120,144},{144,120},{168,96... | collective-permute-start | bytes 393224 | tf_op jit(solution)/shard_map/ppermute | solution.py:389
